TPU v7x, 512 devices: a whole 4x8x8 slice. The times are simulated.
512 devices in a mesh: ctx: 64 (over y, x, core), tp: 8 (over z).
Axes of the slice: x: 4, y: 8, z: 8, core: 2. Of those that a mesh axis runs over, the one named last changes fastest.
Arguments:
- queries: bfloat16 [4096, 4096], P('ctx', 'tp'), may hold values from -256 to 256
- key_vectors: bfloat16 [4096, 1024], P('ctx', 'tp'), may hold values from -6 to 6
- value_vectors: bfloat16 [4096, 1024], P('ctx', 'tp'), may hold values from -6 to 6
- out_weight: bfloat16 [4096, 4096], P('tp'), may hold values from -0.09375 to 0.09375
- router_logit: float32 [4096], P('ctx'), may hold values from -8 to 8
- chosen_index: int32 [4096], P('ctx'), may hold values from 0 to 511, as said below
- chosen_count: int32 [64], P('ctx'), may hold values from 1 to 64, as said below
- out_cotangent: bfloat16 [4096, 4096], P('ctx', 'tp'), may hold values from -6 to 6
- hidden_state: bfloat16 [32768, 4096], P('ctx', 'tp'), may hold values from -4 to 4
Outputs:
- update: bfloat16 [4096, 4096], P('ctx', 'tp')
- grad_queries: bfloat16 [4096, 4096], P('ctx', 'tp')
- grad_keys: bfloat16 [4096, 1024], P('ctx', 'tp')
- grad_values: bfloat16 [4096, 1024], P('ctx', 'tp')
- grad_logit: float32 [4096], P('ctx')
- hidden_after: bfloat16 [32768, 4096], P('ctx', 'tp')
Inputs may be any that keep to these rules, and one draw needn't show every extreme that they name: `chosen_index`: in each shard's block of 64 slots, the first chosen_count entries are strictly increasing token indices; the remaining entries are 511. `chosen_count`: some shard has all 64 slots filled.
All inputs are finite; a program needn't handle non-finite values.
Results may differ from a plain program's by a relative error of at most 0.015.
Values may be sent and summed in bfloat16 or wider, within the bound.
No kernel may reach another device: no remote copies, remote signals or barrier semaphores. Data moves between devices by JAX's collectives and lax.ppermute only.
A program may use at most 128 MiB of HBM per device.

v0:
```python
import math

import jax
import jax.numpy as jnp
from jax import lax
from jax.sharding import PartitionSpec as P

HD = 128
TOK_DEV = 512


ROTARY_BASE = 500000.0
LOWEST = -1e30


def rotate(field_in, position, sign_value):
    row_count = field_in.shape[0]
    row_width = field_in.shape[1]
    head_count = row_width // HD
    half_width = HD // 2
    frequency = ROTARY_BASE ** (-(jnp.arange(half_width, dtype=jnp.float32) * 2.0 / HD))
    angles = position.astype(jnp.float32)[:, None] * frequency[None, :]
    cos_part = jnp.cos(angles)[:, None, :]
    sin_part = sign_value * jnp.sin(angles)[:, None, :]
    shaped = field_in.astype(jnp.float32).reshape(row_count, head_count, HD)
    first_half = shaped[:, :, :half_width]
    second_half = shaped[:, :, half_width:]
    turned = jnp.concatenate(
        [
            first_half * cos_part - second_half * sin_part,
            second_half * cos_part + first_half * sin_part,
        ],
        axis=2,
    )
    return turned.reshape(row_count, row_width)


def grouped(flat_rows, kv_count):
    row_count = flat_rows.shape[0]
    group_size = flat_rows.shape[1] // HD // kv_count
    shaped = flat_rows.reshape(row_count, kv_count, group_size, HD)
    return jnp.transpose(shaped, (1, 0, 2, 3)).reshape(kv_count, row_count * group_size, HD)


def ungrouped(block_in, row_count):
    kv_count = block_in.shape[0]
    group_size = block_in.shape[1] // row_count
    shaped = block_in.reshape(kv_count, row_count, group_size, HD)
    return jnp.transpose(shaped, (1, 0, 2, 3)).reshape(row_count, kv_count * group_size * HD)


def stats_table(stat_block, row_count):
    kv_count = stat_block.shape[0]
    group_size = stat_block.shape[1] // row_count
    return jnp.transpose(stat_block.reshape(kv_count, row_count, group_size), (1, 0, 2)).reshape(
        row_count, kv_count * group_size
    )


def table_stats(table_in, kv_count):
    row_count = table_in.shape[0]
    group_size = table_in.shape[1] // kv_count
    return jnp.transpose(table_in.reshape(row_count, kv_count, group_size), (1, 0, 2)).reshape(
        kv_count, row_count * group_size
    )


def keep_state(state_in):
    return state_in


def on_device(
    queries,
    key_vectors,
    value_vectors,
    out_weight,
    router_logit,
    chosen_index,
    chosen_count,
    out_cotangent,
    hidden_state,
):
    capacity = queries.shape[0]
    kv_count = key_vectors.shape[1] // HD
    group_size = queries.shape[1] // HD // kv_count
    kv_width = key_vectors.shape[1]
    shard_count = lax.axis_size("ctx")
    score_scale = 1.0 / math.sqrt(HD)
    slot_ids = jnp.arange(capacity, dtype=jnp.int32)
    position = lax.axis_index("ctx") * TOK_DEV + chosen_index
    live_slot = slot_ids < chosen_count[0]
    key_position = jnp.where(live_slot, position, TOK_DEV * shard_count)
    all_key_position, all_position = (
        lax.all_gather(key_position, "ctx", axis=0, tiled=True),
        lax.all_gather(position, "ctx", axis=0, tiled=True),
    )
    turned_queries = rotate(queries, position, 1.0).astype(jnp.bfloat16)
    turned_keys = rotate(key_vectors, position, 1.0).astype(jnp.bfloat16)
    query_block = grouped(turned_queries, kv_count)
    query_position = jnp.repeat(position, group_size)
    newest = jnp.max(position)
    row_count = capacity * group_size
    initial = (
        jnp.full((kv_count, row_count), LOWEST, jnp.float32),
        jnp.zeros((kv_count, row_count), jnp.float32),
        jnp.zeros((kv_count, row_count, HD), jnp.float32),
    )
    key_piece = lax.all_gather(turned_keys, "ctx", axis=0, tiled=True)
    value_piece = lax.all_gather(value_vectors, "ctx", axis=0, tiled=True)
    piece_rows = key_piece.shape[0]

    def attend_compute(state_in):
        row_max, row_total, summed = state_in
        key_block = key_piece.reshape(piece_rows, kv_count, HD)
        value_block = value_piece.reshape(piece_rows, kv_count, HD)
        scores = (
            jnp.einsum("gqd,kgd->gqk", query_block, key_block, preferred_element_type=jnp.float32)
            * score_scale
        )
        allowed = all_key_position[None, None, :] <= query_position[None, :, None]
        scores = jnp.where(allowed, scores, LOWEST)
        new_max = jnp.maximum(row_max, jnp.max(scores, axis=2))
        weights = jnp.where(allowed, jnp.exp(scores - new_max[:, :, None]), 0.0)
        new_total = jnp.sum(weights, axis=2)
        new_sum = jnp.einsum(
            "gqk,kgd->gqd",
            weights.astype(jnp.bfloat16),
            value_block,
            preferred_element_type=jnp.float32,
        )
        return (new_max, new_total, new_sum)

    row_max, row_total, summed = lax.cond(
        jnp.min(all_key_position) <= newest, attend_compute, keep_state, initial
    )
    attention = ungrouped(summed / row_total[:, :, None], capacity).astype(jnp.bfloat16)
    log_total = row_max + jnp.log(row_total)
    partial_proj = jnp.dot(attention, out_weight, preferred_element_type=jnp.float32)
    projection = lax.psum_scatter(partial_proj, "tp", scatter_dimension=1, tiled=True)
    gate_value = jax.nn.sigmoid(router_logit)
    kept_gate = jnp.where(live_slot, gate_value, 0.0)
    update = (kept_gate[:, None] * projection).astype(jnp.bfloat16)
    hidden_after = (
        hidden_state.astype(jnp.float32)
        .at[chosen_index]
        .add(update.astype(jnp.float32))
        .astype(jnp.bfloat16)
    )
    cotangent = out_cotangent.astype(jnp.float32)
    gate_term = jnp.where(live_slot, gate_value * (1.0 - gate_value), 0.0) * jnp.sum(
        cotangent * projection, axis=1
    )
    grad_logit = lax.psum(gate_term, "tp")
    scaled = (kept_gate[:, None] * cotangent).astype(jnp.bfloat16)
    grad_attention = lax.dot_general(
        lax.all_gather(scaled, "tp", axis=1, tiled=True),
        out_weight,
        (((1,), (1,)), ((), ())),
        preferred_element_type=jnp.float32,
    ).astype(jnp.bfloat16)
    grad_block = grouped(grad_attention, kv_count)
    attention_block = grouped(attention, kv_count)
    row_delta = jnp.sum(
        attention_block.astype(jnp.float32) * grad_block.astype(jnp.float32), axis=2
    )
    revisit_start = jnp.zeros((kv_count, row_count, HD), jnp.float32)
    revisit_key_piece = lax.all_gather(turned_keys, "ctx", axis=0, tiled=True)
    revisit_value_piece = lax.all_gather(value_vectors, "ctx", axis=0, tiled=True)
    revisit_piece_rows = revisit_key_piece.shape[0]

    def revisit_compute(state_in):
        key_block = revisit_key_piece.reshape(revisit_piece_rows, kv_count, HD)
        value_block = revisit_value_piece.reshape(revisit_piece_rows, kv_count, HD)
        scores = (
            jnp.einsum("gqd,kgd->gqk", query_block, key_block, preferred_element_type=jnp.float32)
            * score_scale
        )
        allowed = all_key_position[None, None, :] <= query_position[None, :, None]
        scores = jnp.where(allowed, scores, LOWEST)
        probability = jnp.where(allowed, jnp.exp(scores - log_total[:, :, None]), 0.0)
        grad_probs = jnp.einsum(
            "gqd,kgd->gqk", grad_block, value_block, preferred_element_type=jnp.float32
        )
        grad_score = (probability * (grad_probs - row_delta[:, :, None]) * score_scale).astype(
            jnp.bfloat16
        )
        return jnp.einsum("gqk,kgd->gqd", grad_score, key_block, preferred_element_type=jnp.float32)

    revisited = lax.cond(
        jnp.min(all_key_position) <= newest, revisit_compute, keep_state, revisit_start
    )
    grad_turned_queries = ungrouped(revisited, capacity)
    log_table = stats_table(log_total, capacity)
    delta_table = stats_table(row_delta, capacity)
    all_log, all_delta = (
        lax.all_gather(log_table, "ctx", axis=0, tiled=True),
        lax.all_gather(delta_table, "ctx", axis=0, tiled=True),
    )
    local_keys = turned_keys.reshape(capacity, kv_count, HD)
    local_values = value_vectors.reshape(capacity, kv_count, HD)
    oldest = jnp.min(key_position)
    collect_start = (
        jnp.zeros((capacity, kv_width), jnp.float32),
        jnp.zeros((capacity, kv_width), jnp.float32),
    )
    query_piece = lax.all_gather(turned_queries, "ctx", axis=0, tiled=True)
    grad_piece = lax.all_gather(grad_attention, "ctx", axis=0, tiled=True)
    rows_position = jnp.repeat(all_position, group_size)
    rows_log = table_stats(all_log, kv_count)
    rows_delta = table_stats(all_delta, kv_count)

    def collect_compute(state_in):
        remote_queries = grouped(query_piece, kv_count)
        remote_grads = grouped(grad_piece, kv_count)
        scores = (
            jnp.einsum(
                "gqd,kgd->gqk", remote_queries, local_keys, preferred_element_type=jnp.float32
            )
            * score_scale
        )
        allowed = key_position[None, None, :] <= rows_position[None, :, None]
        scores = jnp.where(allowed, scores, LOWEST)
        probability = jnp.where(allowed, jnp.exp(scores - rows_log[:, :, None]), 0.0)
        grad_probs = jnp.einsum(
            "gqd,kgd->gqk", remote_grads, local_values, preferred_element_type=jnp.float32
        )
        grad_score = (probability * (grad_probs - rows_delta[:, :, None]) * score_scale).astype(
            jnp.bfloat16
        )
        key_term = jnp.einsum(
            "gqk,gqd->kgd", grad_score, remote_queries, preferred_element_type=jnp.float32
        ).reshape(capacity, kv_width)
        value_term = jnp.einsum(
            "gqk,gqd->kgd",
            probability.astype(jnp.bfloat16),
            remote_grads,
            preferred_element_type=jnp.float32,
        ).reshape(capacity, kv_width)
        return (key_term, value_term)

    grad_turned_keys, value_grads = lax.cond(
        jnp.max(rows_position) >= oldest, collect_compute, keep_state, collect_start
    )
    grad_queries = rotate(grad_turned_queries, position, -1.0).astype(jnp.bfloat16)
    grad_keys = rotate(grad_turned_keys, position, -1.0).astype(jnp.bfloat16)
    grad_values = value_grads.astype(jnp.bfloat16)
    return (update, grad_queries, grad_keys, grad_values, grad_logit, hidden_after)


def solution(mesh):
    placed = (
        P("ctx", "tp"),
        P("ctx", "tp"),
        P("ctx", "tp"),
        P("tp", None),
        P("ctx"),
        P("ctx"),
        P("ctx"),
        P("ctx", "tp"),
        P("ctx", "tp"),
    )
    return jax.shard_map(
        on_device,
        mesh=mesh,
        in_specs=placed,
        out_specs=(
            P("ctx", "tp"),
            P("ctx", "tp"),
            P("ctx", "tp"),
            P("ctx", "tp"),
            P("ctx"),
            P("ctx", "tp"),
        ),
        check_vma=False,
    )
```

profile of v0, /device:TPU:1, one launch (start us, length us, event | category | flops | bytes accessed | tf_op | source)
XLA Modules:
  0.0 546.0 jit_solution(2008707122606452895)
XLA Ops:
  8.6 1.8 fusion.62
  15.3 247.5 %all-reduce.2 = (s32[4096]{0:T(1024)}, s32[4096]{0:T(1024)S(1)}) all-reduce(s32[4096]{0:T(1024)S(1)} %dynamic-update-slice, s32[4096]{0:T(1024)S(1)} %dynamic-update-slice.1), channel_id=1, replica_groups=mesh['ctx'=64,'tp'=8] {'ctx'}, use_global_device_ids=true, to_apply=%add | all-reduce | flops 8192 | bytes 65536
  267.6 8.1 %conditional.3 = (f32[1,256]{1,0:T(1,128)}, f32[1,256]{1,0:T(1,128)}, f32[1,256,128]{2,1,0:T(8,128)S(1)}, f32[1,256]{1,0:T(1,128)}) conditional(s32[]{:T(128)} %convert_element_type.125, () %tuple.46, (s32[4096]{0:T(1024)}, s32[64,4]{1,0:T(8,128)S(1)}, bf16[1,256,128]{2,1,0:T(8,128)(2,1)S(1)}, bf16[4096,128]{1,0:T(8,128)(2,1)}, ...), branch_computations={%region_2.3_spmd, %region_3.6_spmd} | conditional | flops 549453568 | bytes 19133500 | solution.py:133
  267.7 2.2 fusion.64
  270.4 1.7 fusion.5
  272.2 2.3 fusion.2
  276.5 4.0 fusion.68
  281.3 41.4 %reduce-scatter.2.cloned.1.call-done = f32[64,512]{1,0:T(8,128)} async-done(((f32[64,4096]{1,0:T(8,128)}), f32[64,512]{1,0:T(8,128)}) %reduce-scatter.2.cloned.1.call-update) | async-done | bytes 131088 | tf_op jit(solution)/shard_map/reduce_scatter | solution.py:139
  325.8 19.7 %all_gather.32 = bf16[64,4096]{1,0:T(8,128)(2,1)S(1)} all-gather(bf16[64,512]{1,0:T(8,128)(2,1)S(1)} %get-tuple-element.169), channel_id=1, replica_groups=mesh['ctx'=64,'tp'=8] {'tp'}, dimensions={1}, use_global_device_ids=true | all-gather | bytes 589824 | tf_op jit(solution)/shard_map/all_gather | solution.py:156
  345.5 4.2 convolution_convert_fusion
  349.8 2.5 broadcast_reduce_fusion
  355.2 1.9 fusion.61
  357.3 60.8 %all-gather.1 = f32[64,64,4]{1,2,0:T(4,128)S(1)} all-gather(f32[1,64,4]{1,2,0:T(4,128)S(1)} %copy.19), channel_id=1, replica_groups=mesh['ctx'=64,'tp'=8] {'ctx'}, dimensions={0}, use_global_device_ids=true | all-gather | bytes 66560 | tf_op jit(solution)/shard_map/all_gather | solution.py:196
  421.7 8.5 %conditional.4 = (f32[64,4,64]{2,1,0:T(4,128)}, f32[64,4,64]{2,1,0:T(4,128)}) conditional(s32[]{:T(128)} %convert_element_type.125, () %tuple.48, (s32[4096]{0:T(1024)}, s32[64,4]{1,0:T(8,128)S(1)}, bf16[1,256,128]{2,1,0:T(8,128)(2,1)}, bf16[4096,128]{1,0:T(8,128)(2,1)S(1)}, f32[1,256]{1,0:T(1,128)}, /*index=5*/bf16[1,256,128]{2,1,0:T(8,128)(2,1)S(1)}, ...), branch_computations={%region_8.9_spmd, %region_9.10_spmd} | conditional | flops 814743552 | bytes 12084268 | solution.py:189
  421.8 4.1 fusion.15
  425.9 3.4 fusion.17
  435.4 12.5 %psum.7 = f32[64]{0:T(128)} all-reduce(f32[64]{0:T(128)} %get-tuple-element.144), channel_id=1, replica_groups=mesh['ctx'=64,'tp'=8] {'tp'}, use_global_device_ids=true, to_apply=%region_15.16 | all-reduce | flops 64 | bytes 512 | tf_op jit(solution)/shard_map/psum | solution.py:153
  447.9 51.7 %all-gather.2 = f32[64,64,4]{1,2,0:T(4,128)S(1)} all-gather(f32[1,64,4]{1,2,0:T(4,128)S(1)} %copy.21), channel_id=1, replica_groups=mesh['ctx'=64,'tp'=8] {'ctx'}, dimensions={0}, use_global_device_ids=true | all-gather | bytes 66560 | tf_op jit(solution)/shard_map/all_gather | solution.py:197
  500.2 38.4 %conditional.5 = (f32[64,1,64]{2,0,1:T(8,128)S(1)}, f32[64,1,64]{2,0,1:T(8,128)S(1)}, bf16[64,128]{1,0:T(8,128)(2,1)S(1)}) conditional(s32[]{:T(128)} %convert_element_type.140, () %tuple.50, (s32[64]{0:T(128)S(1)}, s32[4096,4]{1,0:T(8,128)S(1)}, bf16[4096,512]{1,0:T(8,128)(2,1)}, bf16[64,1,128]{2,0,1:T(8,128)(2,1)S(1)}, ...), branch_computations={%region_12.13_spmd, %region_13.14_spmd} | conditional | flops 1084235776 | bytes 47137048 | solution.py:241
  506.5 7.6 %reshape.391 = bf16[16384,128]{1,0:T(8,128)(2,1)} reshape(bf16[4096,512]{1,0:T(8,128)(2,1)} %get-tuple-element.96) | data formatting | bytes 8388608 | tf_op jit(solution)/shard_map/reshape.195
  514.1 7.5 %reshape.389 = bf16[16384,128]{1,0:T(8,128)(2,1)} reshape(bf16[4096,512]{1,0:T(8,128)(2,1)} %get-tuple-element.93) | data formatting | bytes 8388608 | tf_op jit(solution)/shard_map/reshape.193
  521.6 5.7 %fusion.27 = f32[16384,64]{0,1:T(8,128)} fusion(bf16[16384,128]{1,0:T(8,128)(2,1)} %reshape.389, f32[16384]{0:T(1024)S(1)} %sub.59, s32[16384]{0:T(1024)S(1)} %le.50, s32[64]{0:T(128)S(1)} %get-tuple-element.91, bf16[64,1,128]{2,0,1:T(8,128)(2,1)S(1)} %get-tuple-element.94), kind=kOutput, calls=%fused_computation.31 | convolution fusion | flops 273678336 | bytes 8536320 | tf_op jit(solution)/shard_map/cond/branch_1_fun/gqd,kgd->gqk/dot_general | solution.py:216
  527.4 6.8 %fusion.32 = f32[64,1,128]{2,0,1:T(8,128)S(1)} fusion(bf16[16384,128]{1,0:T(8,128)(2,1)} %reshape.389, f32[16384,64]{0,1:T(8,128)} %fusion.27, bf16[16384,128]{1,0:T(8,128)(2,1)} %reshape.391, bf16[64,128]{1,0:T(8,128)(2,1)S(1)} %get-tuple-element.97, f32[16384]{0:T(1024)S(1)} %sub.62), kind=kOutput, calls=%fused_computation.36 | convolution fusion | flops 541065216 | bytes 12697600 | tf_op jit(solution)/shard_map/cond/branch_1_fun/gqk,gqd->kgd/dot_general | solution.py:230
  534.2 4.3 fusion.33
  (96 shorter events, 34.5 us)
Async XLA Ops:
  7.2 260.3 %all-gather.8.cloned.1.call-start = ((), (), s32[]{:S(2)}) async-start(), calls=%async_computation.1 | async-start | bytes 1064960 | tf_op jit(solution)/shard_map/all_gather | solution.py:109
  7.9 259.6 %all-gather.14.cloned.1.call-start = ((), (), s32[]{:S(2)}) async-start(), calls=%async_computation.5 | async-start | bytes 1064960 | tf_op jit(solution)/shard_map/all_gather | solution.py:108
  8.6 258.8 %copy-start.9 = (f32[64]{0:T(128)}, f32[64]{0:T(128)S(1)}, u32[]{:S(2)}) copy-start(f32[64]{0:T(128)S(1)} %negate_power_fusion) | copy-start | bytes 772
  10.5 255.0 %copy-start.14 = (s32[64]{0:T(128)}, s32[64]{0:T(128)S(1)}, u32[]{:S(2)}) copy-start(s32[64]{0:T(128)S(1)} %get-tuple-element.149) | copy-start | bytes 772
  11.1 256.4 %copy-start.11 = (f32[64]{0:T(128)}, f32[64]{0:T(128)S(1)}, u32[]{:S(2)}) copy-start(f32[64]{0:T(128)S(1)} %get-tuple-element.171) | copy-start | bytes 772
  12.7 309.9 %reduce-scatter.2.cloned.1.call-start = ((), (), s32[]{:S(2)}) async-start(), calls=%async_computation.2 | async-start | bytes 1179648 | tf_op jit(solution)/shard_map/reduce_scatter | solution.py:139
  267.4 13.2 %copy-start.4 = (bf16[64,4,128]{2,1,0:T(4,128)(2,1)}, bf16[64,4,128]{2,1,0:T(4,128)(2,1)S(1)}, u32[]{:S(2)}) copy-start(bf16[64,4,128]{2,1,0:T(4,128)(2,1)S(1)} %maximum_convert_fusion) | copy-start | bytes 196612
  267.6 2.9 copy-start.1
  275.6 47.0 %copy-start.3 = (bf16[64,512]{1,0:T(8,128)(2,1)S(1)}, bf16[64,512]{1,0:T(8,128)(2,1)}, u32[]{:S(2)}) copy-start(bf16[64,512]{1,0:T(8,128)(2,1)} %param.22) | copy-start | bytes 196612
  275.7 48.0 %copy-start.13 = (f32[64]{0:T(128)S(1)}, f32[64]{0:T(128)}, u32[]{:S(2)}) copy-start(f32[64]{0:T(128)} %param.19) | copy-start | bytes 772
  280.5 141.2 %copy-start = (bf16[4096,128]{1,0:T(8,128)(2,1)S(1)}, bf16[4096,128]{1,0:T(8,128)(2,1)}, u32[]{:S(2)}) copy-start(bf16[4096,128]{1,0:T(8,128)(2,1)} %all-gather.8.cloned.1.call-done) | copy-start | bytes 3145732
  280.5 141.2 %copy-start.2 = (bf16[4096,1,128]{2,0,1:T(8,128)(2,1)S(1)}, bf16[4096,1,128]{2,0,1:T(8,128)(2,1)}, u32[]{:S(2)}) copy-start(bf16[4096,1,128]{2,0,1:T(8,128)(2,1)} %all-gather.14.cloned.1.call-done) | copy-start | bytes 3145732
  280.5 219.0 %all-gather.10.cloned.1.call-start = ((), (), s32[]{:S(2)}) async-start(), calls=%async_computation.3 | async-start | bytes 4259840 | tf_op jit(solution)/shard_map/all_gather | solution.py:206
  281.3 218.3 %all-gather.12.cloned.1.call-start = ((), (), s32[]{:S(2)}) async-start(), calls=%async_computation.4 | async-start | bytes 4259840 | tf_op jit(solution)/shard_map/all_gather | solution.py:207
  421.8 4.1 copy-start.8
  430.2 70.0 %copy-start.5 = (bf16[64,128]{1,0:T(8,128)(2,1)S(1)}, bf16[64,128]{1,0:T(8,128)(2,1)}, u32[]{:S(2)}) copy-start(bf16[64,128]{1,0:T(8,128)(2,1)} %param.17) | copy-start | bytes 49156
  430.2 70.0 %copy-start.6 = (bf16[64,1,128]{2,0,1:T(8,128)(2,1)S(1)}, bf16[64,1,128]{2,0,1:T(8,128)(2,1)}, u32[]{:S(2)}) copy-start(bf16[64,1,128]{2,0,1:T(8,128)(2,1)} %maximum_convert_fusion.1) | copy-start | bytes 49156
  430.2 70.0 %copy-start.15 = (s32[64]{0:T(128)S(1)}, s32[64]{0:T(128)}, u32[]{:S(2)}) copy-start(s32[64]{0:T(128)} %copy-done.14) | copy-start | bytes 772
  500.2 38.4 %copy-start.10 = (f32[64]{0:T(128)S(1)}, f32[64]{0:T(128)}, u32[]{:S(2)}) copy-start(f32[64]{0:T(128)} %copy-done.9) | copy-start | bytes 772
  500.2 38.4 %copy-start.12 = (f32[64]{0:T(128)S(1)}, f32[64]{0:T(128)}, u32[]{:S(2)}) copy-start(f32[64]{0:T(128)} %copy-done.11) | copy-start | bytes 772
  538.6 0.9 copy-start.7
Sparse Core Ops, SparseCore 0:
  11.4 87.4 all-gather.7
  102.7 79.5 all-gather.13
  280.6 41.9 reduce-scatter.1
  325.9 87.6 all-gather.9
  416.8 81.7 all-gather.11
where the time goes:
time: 547 us; the launch traced here: 546 us
  blocking collectives  392 us (72%)
  waiting for transfers between devices  42.2 us (8%)
  matrix products  36.5 us (7%)
  local copies, waits for them, and re-layouts  32.2 us (6%)
  other arithmetic  24.8 us (5%)
  between operations  17.9 us (3%)
    unnamed x1, blocking collectives  247 us
    all_gather x1, blocking collectives, on_device(): lax.all_gather(log_table, 'ctx', axis=0, tiled=True)  60.8 us
    all_gather x1, blocking collectives, on_device(): lax.all_gather(delta_table, 'ctx', axis=0, tiled=True)  51.7 us
    reduce_scatter x1, waiting for transfers between devices, on_device(): lax.psum_scatter(partial_proj, 'tp', scatter_dimension=1, tiled=True)  41.4 us
    all_gather x1, blocking collectives, on_device(): lax.all_gather(scaled, 'tp', axis=1, tiled=True)  19.7 us
    another operation x4, local copies, waits for them, and re-layouts  16.5 us
    psum x1, blocking collectives, on_device(): grad_logit = lax.psum(gate_term, 'tp')  12.5 us
  transfers between devices with their start and end apart: 5, of which 1 were waited for; matrix products, arithmetic and copies ran while one was open for 7% of the time, Pallas kernels for 0%

commit v1 on v0

v1 whole, which is shorter than its diff:
```python
import functools
import math

import jax
import jax.numpy as jnp
from jax import lax
from jax.experimental import pallas as pl
from jax.experimental.pallas import tpu as pltpu
from jax.sharding import PartitionSpec as P

HD = 128
TOK_DEV = 512
ROTARY_BASE = 500000.0
LOWEST = -1e30
DEAD_MARK = 1024.0
DEAD_LIMIT = 512.0
F32 = jnp.float32
BF16 = jnp.bfloat16

VMEM = pl.BlockSpec(memory_space=pltpu.VMEM)
SMEM = pl.BlockSpec(memory_space=pltpu.SMEM)


def call(kernel, out_shape, in_specs, scratch=(), limit=32):
    return pl.pallas_call(
        kernel,
        out_shape=out_shape,
        in_specs=in_specs,
        out_specs=jax.tree.map(lambda _: VMEM, out_shape),
        scratch_shapes=list(scratch),
        compiler_params=pltpu.CompilerParams(vmem_limit_bytes=limit * 1024 * 1024),
    )


def turn(rows, cos_full, sin_signed):
    return rows * cos_full + pltpu.roll(rows, HD // 2, 1) * sin_signed


def matmul(a, b, dims):
    return lax.dot_general(a, b, (dims, ((), ())), preferred_element_type=F32)


def payload_kernel(key_ref, value_ref, cos_ref, sin_ref, count_ref, pay_ref):
    rows = key_ref.shape[0]
    turned = turn(key_ref[...].astype(F32), cos_ref[...], sin_ref[...])
    pay_ref[0:rows, :] = turned.astype(BF16)
    row_ids = lax.broadcasted_iota(jnp.int32, (rows, HD), 0)
    col_ids = lax.broadcasted_iota(jnp.int32, (rows, HD), 1)
    marked = (row_ids >= count_ref[0]) & (col_ids == 0)
    value = jnp.where(marked, DEAD_MARK, value_ref[...].astype(F32))
    pay_ref[rows : 2 * rows, :] = value.astype(BF16)


def cotangent_kernel(weight_ref, gate_ref, cot_ref, grad_ref):
    width = cot_ref.shape[2]
    total = None
    for step in range(cot_ref.shape[0]):
        part = matmul(cot_ref[step], weight_ref[:, step * width : (step + 1) * width], ((1,), (1,)))
        total = part if total is None else total + part
    grad_ref[...] = (total * gate_ref[...]).astype(BF16)


def attention_kernel(
    dims,
    place_ref,
    query_ref,
    cos_ref,
    sin_ref,
    col_ref,
    row_ref,
    grad_ref,
    own_ref,
    same_ref,
    other_ref,
    att_ref,
    dq_ref,
    delta_ref,
    own_out,
    same_out,
    other_out,
    score_ref,
    weight_ref,
):
    ny, nx, nc = dims
    slots = query_ref.shape[0]
    heads = query_ref.shape[1] // HD
    rows = slots * heads
    keys = ny * slots
    scale = 1.0 / math.sqrt(HD)
    cos_full, sin_signed = cos_ref[...], sin_ref[...]

    me = place_ref[0]
    my_core = lax.rem(me, nc)
    groups = [(ref, out, flip, x) for flip, (ref, out) in enumerate(((same_ref, same_out), (other_ref, other_out))) for x in range(nx)]

    turned = [
        turn(query_ref[:, h * HD : (h + 1) * HD].astype(F32), cos_full, sin_signed).astype(BF16)
        for h in range(heads)
    ]
    query_t = jnp.concatenate(turned, axis=0).astype(F32).T
    query_tb = query_t.astype(BF16)
    grads = [grad_ref[:, h * HD : (h + 1) * HD].astype(F32) for h in range(heads)]
    grad_t = jnp.concatenate(grads, axis=0).T
    grad_tb = grad_t.astype(BF16)
    own_keys, own_values = own_ref[0:slots, :], own_ref[slots : 2 * slots, :]

    def keys_of(group):
        return group[0][group[3], :, 0:slots, :].reshape(keys, HD)

    def values_of(group):
        return group[0][group[3], :, slots : 2 * slots, :].reshape(keys, HD)

    own_scores = matmul(own_keys, query_tb, ((1,), (0,)))
    dead = own_values[:, 0:1].astype(F32) > DEAD_LIMIT
    own_scores = jnp.where(col_ref[...] <= row_ref[...], own_scores, LOWEST)
    own_scores = own_scores + jnp.where(dead, LOWEST, 0.0)
    peak = jnp.max(own_scores, axis=0, keepdims=True)
    for number, group in enumerate(groups):
        core = my_core if group[2] == 0 else (nc - 1) - my_core
        scores = matmul(keys_of(group), query_tb, ((1,), (0,)))
        for y in range(ny):
            shard = (y * nx + group[3]) * nc + core
            reach = jnp.where(shard < me, 0.0, LOWEST)
            first = group[0][group[3], y, slots : 2 * slots, 0:1].astype(F32)
            bias = jnp.where(first > DEAD_LIMIT, LOWEST, reach)
            block = scores[y * slots : (y + 1) * slots, :] + bias
            score_ref[number, y * slots : (y + 1) * slots, :] = block
            peak = jnp.maximum(peak, jnp.max(block, axis=0, keepdims=True))

    factor = scale * math.log2(math.e)
    own_weights = jnp.exp2((own_scores - peak) * factor)
    total = jnp.sum(own_weights, axis=0, keepdims=True)
    own_weights = own_weights.astype(BF16)
    summed = matmul(own_values, own_weights, ((0,), (0,)))
    for number, group in enumerate(groups):
        weights = jnp.exp2((score_ref[number] - peak) * factor)
        total = total + jnp.sum(weights, axis=0, keepdims=True)
        weights = weights.astype(BF16)
        weight_ref[number] = weights
        summed = summed + matmul(values_of(group), weights, ((0,), (0,)))

    inverse = 1.0 / total
    att_t = (summed * inverse).astype(BF16).astype(F32)
    att = att_t.T.astype(BF16)
    for h in range(heads):
        att_ref[:, h * HD : (h + 1) * HD] = att[h * slots : (h + 1) * slots, :]
    delta = jnp.sum(att_t * grad_t, axis=0, keepdims=True)
    delta_ref[...] = jnp.broadcast_to(delta, delta_ref.shape)

    query_scaled = (query_t * (inverse * scale)).astype(BF16)
    grad_scaled = (grad_t * inverse).astype(BF16)

    def backward(weights, keys_in, values_in):
        grad_probs = matmul(values_in, grad_tb, ((1,), (0,)))
        grad_score = (weights.astype(F32) * (grad_probs - delta)).astype(BF16)
        key_part = matmul(grad_score, query_scaled, ((1,), (1,)))
        value_part = matmul(weights, grad_scaled, ((1,), (1,)))
        return key_part, value_part, matmul(keys_in, grad_score, ((0,), (0,)))

    key_part, value_part, dq_t = backward(own_weights, own_keys, own_values)
    own_out[0:slots, :] = key_part
    own_out[slots : 2 * slots, :] = value_part
    for number, group in enumerate(groups):
        key_part, value_part, dq_part = backward(weight_ref[number], keys_of(group), values_of(group))
        out, x = group[1], group[3]
        out[x, :, 0:slots, :] = key_part.astype(BF16).reshape(ny, slots, HD)
        out[x, :, slots : 2 * slots, :] = value_part.astype(BF16).reshape(ny, slots, HD)
        dq_t = dq_t + dq_part
    dq = (dq_t * (inverse * scale)).T
    for h in range(heads):
        back = turn(dq[h * slots : (h + 1) * slots, :], cos_full, -sin_signed)
        dq_ref[:, h * HD : (h + 1) * HD] = back.astype(BF16)


def projection_kernel(weight_ref, att_ref, delta_ref, part_ref):
    slots = att_ref.shape[0]
    width = part_ref.shape[2]
    rows = delta_ref.shape[1]
    delta = delta_ref[...]
    row_sum = delta[:, 0:slots]
    for h in range(1, rows // slots):
        row_sum = row_sum + delta[:, h * slots : (h + 1) * slots]
    high = row_sum.astype(BF16).astype(F32)
    low = row_sum - high
    extra_ids = lax.broadcasted_iota(jnp.int32, (16, slots), 0)
    high = jnp.concatenate([high, high], axis=0)
    low = jnp.concatenate([low, low], axis=0)
    extra = jnp.where(extra_ids == 0, high, jnp.where(extra_ids == 1, low, 0.0))
    extra = jnp.concatenate([extra, jnp.zeros((16, width - slots), F32)], axis=1).astype(BF16)
    att = att_ref[...]
    for step in range(part_ref.shape[0]):
        part = matmul(att, weight_ref[:, step * width : (step + 1) * width], ((1,), (0,)))
        part_ref[step, 0:slots, :] = part.astype(BF16)
        part_ref[step, slots : slots + 16, :] = extra


def added_up(stack_ref):
    total = stack_ref[0].astype(F32)
    for step in range(1, stack_ref.shape[0]):
        total = total + stack_ref[step].astype(F32)
    return total


def update_kernel(shares_ref, gate_ref, index_ref, gate_row_ref, hidden_ref, update_ref, after_ref, logit_ref):
    slots = update_ref.shape[0]
    tokens = hidden_ref.shape[0]
    total = added_up(shares_ref)
    update = (total[0:slots, :] * gate_ref[...]).astype(BF16)
    update_ref[...] = update
    token_ids = lax.broadcasted_iota(jnp.int32, (tokens, slots), 0)
    chosen = jnp.where(token_ids == index_ref[...], 1.0, 0.0).astype(BF16)
    added = matmul(chosen, update, ((1,), (0,)))
    after_ref[...] = (hidden_ref[...].astype(F32) + added).astype(BF16)
    sums = total[slots : slots + 1, 0:slots] + total[slots + 1 : slots + 2, 0:slots]
    logit_ref[...] = sums * gate_row_ref[...]


def finish_kernel(cos_ref, sin_ref, own_ref, landed_ref, dk_ref, dv_ref):
    slots = dk_ref.shape[0]
    total = own_ref[...] + added_up(landed_ref)
    dk_ref[...] = turn(total[0:slots, :], cos_ref[...], -sin_ref[...]).astype(BF16)
    dv_ref[...] = total[slots : 2 * slots, :].astype(BF16)


def on_device(
    dims,
    tp_count,
    queries,
    key_vectors,
    value_vectors,
    out_weight,
    router_logit,
    chosen_index,
    chosen_count,
    out_cotangent,
    hidden_state,
):
    ny, nx, nc = dims
    slots, width = queries.shape
    heads = width // HD

    def at(y, x, c):
        return (y * nx + x) * nc + c

    y_groups = [[at(y, x, c) for y in range(ny)] for x in range(nx) for c in range(nc)]
    x_groups = [[at(y, x, c) for x in range(nx)] for y in range(ny) for c in range(nc)]
    flips = [(i, i + 1 if i % nc == 0 else i - 1) for i in range(ny * nx * nc)]

    def exchange(array, axis, groups=None):
        return lax.all_to_all(array, axis, 0, 0, axis_index_groups=groups, tiled=True)

    def copies(array, count):
        return jnp.broadcast_to(array[None], (count,) + array.shape)

    my_shard = lax.axis_index("ctx").astype(jnp.int32)
    my_part = lax.axis_index("tp").astype(jnp.int32)
    place = jnp.stack([my_shard, my_part])
    position = my_shard * TOK_DEV + chosen_index
    half = jnp.arange(HD // 2, dtype=F32)
    frequency = ROTARY_BASE ** (-(half * 2.0 / HD))
    angles = position.astype(F32)[:, None] * jnp.concatenate([frequency, frequency])[None, :]
    sign = jnp.concatenate([jnp.full((HD // 2,), -1.0, F32), jnp.ones((HD // 2,), F32)])
    cos_full = jnp.cos(angles)
    sin_signed = jnp.sin(angles) * sign[None, :]

    cot = exchange(copies(out_cotangent, tp_count), "tp")

    payload = call(
        payload_kernel, jax.ShapeDtypeStruct((2 * slots, HD), BF16), [VMEM] * 4 + [SMEM]
    )(key_vectors, value_vectors, cos_full, sin_signed, chosen_count)

    column = exchange(copies(payload, ny), "ctx", y_groups)
    same = exchange(copies(column, nx), "ctx", x_groups)
    other = lax.ppermute(same, "ctx", flips)

    gate_value = jax.nn.sigmoid(router_logit)
    live_slot = jnp.arange(slots, dtype=jnp.int32) < chosen_count[0]
    kept_gate = jnp.where(live_slot, gate_value, 0.0)
    rest_gate = jnp.where(live_slot, 1.0 - gate_value, 0.0)

    grad_attention = call(
        cotangent_kernel, jax.ShapeDtypeStruct((slots, width), BF16), [VMEM] * 3
    )(out_weight, kept_gate[:, None], cot)

    rows = slots * heads
    half_shape = (nx, ny, 2 * slots, HD)
    attention, grad_queries, delta, own_part, same_part, other_part = call(
        functools.partial(attention_kernel, dims),
        [
            jax.ShapeDtypeStruct((slots, width), BF16),
            jax.ShapeDtypeStruct((slots, width), BF16),
            jax.ShapeDtypeStruct((8, rows), F32),
            jax.ShapeDtypeStruct((2 * slots, HD), F32),
            jax.ShapeDtypeStruct(half_shape, BF16),
            jax.ShapeDtypeStruct(half_shape, BF16),
        ],
        [SMEM] + [VMEM] * 9,
        [
            pltpu.VMEM((nx * nc, ny * slots, rows), F32),
            pltpu.VMEM((nx * nc, ny * slots, rows), BF16),
        ],
        limit=48,
    )(
        place,
        queries,
        cos_full,
        sin_signed,
        chosen_index[:, None],
        jnp.tile(chosen_index, heads)[None, :],
        grad_attention,
        payload,
        same,
        other,
    )

    paired = (same_part.astype(F32) + lax.ppermute(other_part, "ctx", flips).astype(F32)).astype(BF16)
    crossed = exchange(paired, "ctx", x_groups)
    stacked = jnp.sum(crossed.astype(F32), axis=0).astype(BF16)

    shares = call(
        projection_kernel,
        jax.ShapeDtypeStruct((tp_count, slots + 16, width), BF16),
        [VMEM] * 3,
    )(out_weight, attention, delta)
    arrived = exchange(shares, "tp")
    update, hidden_after, logit_row = call(
        update_kernel,
        [
            jax.ShapeDtypeStruct((slots, width), BF16),
            jax.ShapeDtypeStruct(hidden_state.shape, BF16),
            jax.ShapeDtypeStruct((1, slots), F32),
        ],
        [VMEM] * 5,
    )(arrived, kept_gate[:, None], chosen_index[None, :], rest_gate[None, :], hidden_state)

    landed = exchange(stacked, "ctx", y_groups)
    grad_keys, grad_values = call(
        finish_kernel, [jax.ShapeDtypeStruct((slots, HD), BF16)] * 2, [VMEM] * 4
    )(cos_full, sin_signed, own_part, landed)
    return (update, grad_queries, grad_keys, grad_values, logit_row[0], hidden_after)


def solution(mesh):
    shards, tp_count = mesh.shape["ctx"], mesh.shape["tp"]
    nc = 2
    nx = 4 if shards >= 64 else 2
    dims = (shards // (nx * nc), nx, nc)
    placed = (
        P("ctx", "tp"),
        P("ctx", "tp"),
        P("ctx", "tp"),
        P("tp", None),
        P("ctx"),
        P("ctx"),
        P("ctx"),
        P("ctx", "tp"),
        P("ctx", "tp"),
    )
    return jax.shard_map(
        functools.partial(on_device, dims, tp_count),
        mesh=mesh,
        in_specs=placed,
        out_specs=(
            P("ctx", "tp"),
            P("ctx", "tp"),
            P("ctx", "tp"),
            P("ctx", "tp"),
            P("ctx"),
            P("ctx", "tp"),
        ),
        check_vma=False,
    )
```

time: 547 us -> 149 us (0.27)
  blocking collectives: 392 us -> 33.7 us
  matrix products: 36.5 us -> 0 us
  starting transfers between devices: 0.2 us -> 28.7 us
  local copies, waits for them, and re-layouts: 32.2 us -> 7.2 us
  other arithmetic: 24.8 us -> 3.95 us
  waiting for transfers between devices: 42.2 us -> 61.4 us
  between operations: 17.9 us -> 1.45 us
  Pallas kernels: 0 us -> 11.4 us
    unnamed x1 -> x0, blocking collectives: 247 us -> none
    all_gather x3 -> x0, blocking collectives: 132 us -> none  [the longest x1 60.8 us: on_device(): lax.all_gather(log_table, 'ctx', axis=0, tiled=True)]
    all_to_all x0 -> x4, waiting for transfers between devices: none -> 59.1 us  [exchange(): lax.all_to_all(array, axis, 0, 0, axis_index_groups=groups, tiled=True)]
    reduce_scatter x1 -> x0, waiting for transfers between devices: 41.4 us -> none  [on_device(): lax.psum_scatter(partial_proj, 'tp', scatter_dimension=1, tiled=True)]
    dot_general x9 -> x0, matrix products: 36.5 us -> none  [the longest x1 6.81 us: collect_compute(): jnp.einsum('gqk,gqd->kgd', grad_score, remote_queries, preferred_element_...]
    all_to_all x0 -> x2, blocking collectives: none -> 33.7 us  [exchange(): lax.all_to_all(array, axis, 0, 0, axis_index_groups=groups, tiled=True)]
    all_to_all x0 -> x4, starting transfers between devices: none -> 20.5 us  [exchange(): lax.all_to_all(array, axis, 0, 0, axis_index_groups=groups, tiled=True)]
    another operation x5 -> x2, local copies, waits for them, and re-layouts: 17.3 us -> 0.08 us  [on_device(): jnp.tile(chosen_index, heads)[None, :]]
  transfers between devices with their start and end apart: 5 -> 6, of which waited for: 1 -> 5; matrix products, arithmetic and copies ran while one was open for 7% -> 1% of each run, Pallas kernels for 0% -> 3%
where the time goes in v1:
time: 149 us; the launch traced here: 148 us
  waiting for transfers between devices  61.4 us (41%)
  blocking collectives  33.7 us (23%)
  starting transfers between devices  28.7 us (19%)
  Pallas kernels  11.4 us (8%)
  local copies, waits for them, and re-layouts  7.2 us (5%)
  other arithmetic  3.95 us (3%)
    all_to_all x4, waiting for transfers between devices, exchange(): lax.all_to_all(array, axis, 0, 0, axis_index_groups=groups, tiled=True)  59.1 us
    all_to_all x2, blocking collectives, exchange(): lax.all_to_all(array, axis, 0, 0, axis_index_groups=groups, tiled=True)  33.7 us
    all_to_all x4, starting transfers between devices, exchange(): lax.all_to_all(array, axis, 0, 0, axis_index_groups=groups, tiled=True)  20.5 us
    pallas_call x1, Pallas kernels, on_device(): call(functools.partial(attention_kernel, dims), [jax.ShapeDtypeStruct((sl...  6.33 us
    ppermute x1, starting transfers between devices, on_device(): other = lax.ppermute(same, 'ctx', flips)  5.85 us
    unnamed x18, local copies, waits for them, and re-layouts  5.82 us
  transfers between devices with their start and end apart: 6, of which 5 were waited for; matrix products, arithmetic and copies ran while one was open for 1% of the time, Pallas kernels for 3%

profile of v1, /device:TPU:1, one launch (start us, length us, event | category | flops | bytes accessed | tf_op | source)
XLA Modules:
  0.0 147.8 jit_solution(7000654875451843783)
XLA Ops:
  2.0 0.8 fusion
  3.6 0.7 copy-done.5
  4.5 16.7 %all_to_all.30 = bf16[8,128,128]{2,1,0:T(8,128)(2,1)S(1)} all-to-all(bf16[8,128,128]{2,1,0:T(8,128)(2,1)S(1)} %broadcast_in_dim.40), channel_id=1, replica_groups={{0,64,128,192,256,320,384,448},{8,72,136,200,264,328,392,456},{16,80,14..., dimensions={0} | all-to-all | bytes 524288 | tf_op jit(solution)/shard_map/all_to_all | solution.py:250
  21.5 17.0 %all_to_all.31.same_ref = bf16[4,8,128,128]{3,2,1,0:T(8,128)(2,1)S(1)} all-to-all(bf16[4,8,128,128]{3,2,1,0:T(8,128)(2,1)S(1)} %broadcast_in_dim.41), channel_id=1, replica_groups={{0,16,32,48},{8,24,40,56},{64,80,96,112},{72,88,104,120},{128,144,160,1..., dimensions={0} | all-to-all | bytes 2097152 | tf_op jit(solution)/shard_map/all_to_all | solution.py:250
  38.4 5.9 %collective-permute-start = (bf16[4,8,128,128]{3,2,1,0:T(8,128)(2,1)S(1)}, bf16[4,8,128,128]{3,2,1,0:T(8,128)(2,1)S(1)}, u32[]{:S(2)}, u32[]{:S(2)}) collective-permute-start(bf16[4,8,128,128]{3,2,1,0:T(8,128)(2,1)S(1)} %all_to_all.31.same_ref), channel_id=1, source_target_pairs={{0,8},{8,0},{16,24},{24,16},{32,40},{40,32},{48,56},{56,48},{64,72... | collective-permute-start | bytes 3145736 | tf_op jit(solution)/shard_map/ppermute | solution.py:274
  44.3 0.8 broadcast_in_dim.20
  45.1 10.0 %all-to-all-start = ((bf16[8,64,512]{2,1,0:T(8,128)(2,1)}), bf16[8,64,512]{2,1,0:T(8,128)(2,1)S(1)}, u32[]{:S(2)}, u32[]{:S(2)}) async-start(bf16[8,64,512]{2,1,0:T(8,128)(2,1)} %broadcast_in_dim.20), calls=%async_computation | async-start | bytes 1048576 | tf_op jit(solution)/shard_map/all_to_all | solution.py:250
  55.6 17.6 %all-to-all-done.cot_ref = bf16[8,64,512]{2,1,0:T(8,128)(2,1)S(1)} async-done(((bf16[8,64,512]{2,1,0:T(8,128)(2,1)}), bf16[8,64,512]{2,1,0:T(8,128)(2,1)S(1)}, u32[]{:S(2)}, u32[]{:S(2)}) %all-to-all-start) | async-done | bytes 524320 | tf_op jit(solution)/shard_map/all_to_all | solution.py:250
  73.2 2.2 %copy-done = bf16[512,4096]{1,0:T(8,128)(2,1)S(1)} copy-done((bf16[512,4096]{1,0:T(8,128)(2,1)S(1)}, bf16[512,4096]{1,0:T(8,128)(2,1)}, u32[]{:S(2)}) %copy-start) | copy-done | bytes 4194328
  75.4 1.4 shard_map.136.grad_ref
  76.8 6.3 %shard_map.138 = (bf16[64,512]{1,0:T(8,128)(2,1)S(1)}, bf16[64,512]{1,0:T(8,128)(2,1)}, f32[8,256]{1,0:T(8,128)S(1)}, f32[128,128]{1,0:T(8,128)S(1)}, bf16[4,8,1...) custom-call(s32[2]{0:T(128)S(1)} %pad_add_fusion.place_ref, bf16[64,512]{1,0:T(8,128)(2,1)S(1)} %copy-done.3, ...), custom_call_target="tpu_custom_call" | custom-call | tf_op jit(solution)/shard_map/pallas_call | solution.py:287
  83.1 2.4 %collective-permute-start.1 = (bf16[4,8,128,128]{3,2,1,0:T(8,128)(2,1)S(1)}, bf16[4,8,128,128]{3,2,1,0:T(8,128)(2,1)S(1)}, u32[]{:S(2)}, u32[]{:S(2)}) collective-permute-start(bf16[4,8,128,128]{3,2,1,0:T(8,128)(2,1)S(1)} %get-tuple-element.23), channel_id=1, source_target_pairs={{0,8},{8,0},{16,24},{24,16},{32,40},{40,32},{48,56},{56,48},{64,72... | collective-permute-start | bytes 3145736 | tf_op jit(solution)/shard_map/ppermute | solution.py:316
  85.5 2.3 %collective-permute-done.1 = bf16[4,8,128,128]{3,2,1,0:T(8,128)(2,1)S(1)} collective-permute-done((bf16[4,8,128,128]{3,2,1,0:T(8,128)(2,1)S(1)}, bf16[4,8,128,128]{3,2,1,0:T(8,128)(2,1)S(1)}, u32[]{:S(2)}, u32[]{:S(2)}) %collective-permute-start.1) | collective-permute-done | bytes 1048608 | tf_op jit(solution)/shard_map/ppermute | solution.py:316
  87.8 1.4 add_convert_fusion
  89.1 3.5 %all-to-all-start.4 = ((bf16[4,8,128,128]{3,2,1,0:T(8,128)(2,1)}), bf16[4,8,128,128]{3,2,1,0:T(8,128)(2,1)S(1)}, u32[]{:S(2)}, u32[]{:S(2)}) async-start(bf16[4,8,128,128]{3,2,1,0:T(8,128)(2,1)} %add_convert_fusion), calls=%async_computation.4 | async-start | bytes 2097152 | tf_op jit(solution)/shard_map/all_to_all | solution.py:250
  92.7 2.2 %copy-done.1 = bf16[512,4096]{1,0:T(8,128)(2,1)S(1)} copy-done((bf16[512,4096]{1,0:T(8,128)(2,1)S(1)}, bf16[512,4096]{1,0:T(8,128)(2,1)}, u32[]{:S(2)}) %copy-start.1) | copy-done | bytes 4194328
  94.8 1.7 %shard_map.139 = bf16[8,80,512]{2,1,0:T(8,128)(2,1)} custom-call(bf16[512,4096]{1,0:T(8,128)(2,1)S(1)} %copy-done.1, bf16[64,512]{1,0:T(8,128)(2,1)S(1)} %get-tuple-element.17.att_ref, f32[8,256]{1,0:T(8,128)S(1)} %get-tuple-element.18.delta_ref), custom_call_target="tpu_custom_call" | custom-call | tf_op jit(solution)/shard_map/pallas_call | solution.py:320
  96.6 10.9 %all-to-all-done.4 = bf16[4,8,128,128]{3,2,1,0:T(8,128)(2,1)S(1)} async-done(((bf16[4,8,128,128]{3,2,1,0:T(8,128)(2,1)}), bf16[4,8,128,128]{3,2,1,0:T(8,128)(2,1)S(1)}, u32[]{:S(2)}, u32[]{:S(2)}) %all-to-all-start.4) | async-done | bytes 1048608 | tf_op jit(solution)/shard_map/all_to_all | solution.py:250
  107.5 3.5 %all-to-all-start.3 = ((bf16[8,80,512]{2,1,0:T(8,128)(2,1)}), bf16[8,80,512]{2,1,0:T(8,128)(2,1)S(1)}, u32[]{:S(2)}, u32[]{:S(2)}) async-start(bf16[8,80,512]{2,1,0:T(8,128)(2,1)} %shard_map.139), calls=%async_computation.3 | async-start | bytes 1310720 | tf_op jit(solution)/shard_map/all_to_all | solution.py:250
  111.0 0.9 reduce_sum.12
  111.9 19.8 %all-to-all-done.3.shares_ref = bf16[8,80,512]{2,1,0:T(8,128)(2,1)S(1)} async-done(((bf16[8,80,512]{2,1,0:T(8,128)(2,1)}), bf16[8,80,512]{2,1,0:T(8,128)(2,1)S(1)}, u32[]{:S(2)}, u32[]{:S(2)}) %all-to-all-start.3) | async-done | bytes 655392 | tf_op jit(solution)/shard_map/all_to_all | solution.py:250
  131.7 3.4 %all-to-all-start.5 = ((bf16[8,128,128]{2,1,0:T(8,128)(2,1)}), bf16[8,128,128]{2,1,0:T(8,128)(2,1)S(1)}, u32[]{:S(2)}, u32[]{:S(2)}) async-start(bf16[8,128,128]{2,1,0:T(8,128)(2,1)} %reduce_sum.12), calls=%async_computation.5 | async-start | bytes 524288 | tf_op jit(solution)/shard_map/all_to_all | solution.py:250
  135.1 1.1 shard_map.140
  136.3 10.8 %all-to-all-done.5.landed_ref = bf16[8,128,128]{2,1,0:T(8,128)(2,1)S(1)} async-done(((bf16[8,128,128]{2,1,0:T(8,128)(2,1)}), bf16[8,128,128]{2,1,0:T(8,128)(2,1)S(1)}, u32[]{:S(2)}, u32[]{:S(2)}) %all-to-all-start.5) | async-done | bytes 262176 | tf_op jit(solution)/shard_map/all_to_all | solution.py:250
  (30 shorter events, 2.9 us)
Async XLA Ops:
  2.9 0.7 copy-start.4
  3.6 0.7 copy-start.5
  4.4 39.9 %copy-start.7 = (bf16[64,512]{1,0:T(8,128)(2,1)S(1)}, bf16[64,512]{1,0:T(8,128)(2,1)}, u32[]{:S(2)}) copy-start(bf16[64,512]{1,0:T(8,128)(2,1)} %param.16) | copy-start | bytes 196612
  21.4 33.8 %copy-start.6 = (s32[64]{0:T(128)S(1)}, s32[64]{0:T(128)}, u32[]{:S(2)}) copy-start(s32[64]{0:T(128)} %param.14) | copy-start | bytes 772
  21.4 33.8 %copy-start.8 = (f32[64]{0:T(128)S(1)}, f32[64]{0:T(128)}, u32[]{:S(2)}) copy-start(f32[64]{0:T(128)} %param.13) | copy-start | bytes 772
  38.4 38.4 %collective-permute-start = (bf16[4,8,128,128]{3,2,1,0:T(8,128)(2,1)S(1)}, bf16[4,8,128,128]{3,2,1,0:T(8,128)(2,1)S(1)}, u32[]{:S(2)}, u32[]{:S(2)}) collective-permute-start(bf16[4,8,128,128]{3,2,1,0:T(8,128)(2,1)S(1)} %all_to_all.31.same_ref), channel_id=1, source_target_pairs={{0,8},{8,0},{16,24},{24,16},{32,40},{40,32},{48,56},{56,48},{64,72... | collective-permute-start | bytes 3145736 | tf_op jit(solution)/shard_map/ppermute | solution.py:274
  45.1 28.1 %all-to-all-start = ((bf16[8,64,512]{2,1,0:T(8,128)(2,1)}), bf16[8,64,512]{2,1,0:T(8,128)(2,1)S(1)}, u32[]{:S(2)}, u32[]{:S(2)}) async-start(bf16[8,64,512]{2,1,0:T(8,128)(2,1)} %broadcast_in_dim.20), calls=%async_computation | async-start | bytes 1048576 | tf_op jit(solution)/shard_map/all_to_all | solution.py:250
  73.2 2.2 %copy-start = (bf16[512,4096]{1,0:T(8,128)(2,1)S(1)}, bf16[512,4096]{1,0:T(8,128)(2,1)}, u32[]{:S(2)}) copy-start(bf16[512,4096]{1,0:T(8,128)(2,1)} %weight_ref.3) | copy-start | bytes 12582916
  75.4 1.4 copy-start.3
  83.1 4.6 %collective-permute-start.1 = (bf16[4,8,128,128]{3,2,1,0:T(8,128)(2,1)S(1)}, bf16[4,8,128,128]{3,2,1,0:T(8,128)(2,1)S(1)}, u32[]{:S(2)}, u32[]{:S(2)}) collective-permute-start(bf16[4,8,128,128]{3,2,1,0:T(8,128)(2,1)S(1)} %get-tuple-element.23), channel_id=1, source_target_pairs={{0,8},{8,0},{16,24},{24,16},{32,40},{40,32},{48,56},{56,48},{64,72... | collective-permute-start | bytes 3145736 | tf_op jit(solution)/shard_map/ppermute | solution.py:316
  89.1 18.3 %all-to-all-start.4 = ((bf16[4,8,128,128]{3,2,1,0:T(8,128)(2,1)}), bf16[4,8,128,128]{3,2,1,0:T(8,128)(2,1)S(1)}, u32[]{:S(2)}, u32[]{:S(2)}) async-start(bf16[4,8,128,128]{3,2,1,0:T(8,128)(2,1)} %add_convert_fusion), calls=%async_computation.4 | async-start | bytes 2097152 | tf_op jit(solution)/shard_map/all_to_all | solution.py:250
  92.6 2.2 %copy-start.1 = (bf16[512,4096]{1,0:T(8,128)(2,1)S(1)}, bf16[512,4096]{1,0:T(8,128)(2,1)}, u32[]{:S(2)}) copy-start(bf16[512,4096]{1,0:T(8,128)(2,1)} %weight_ref.3) | copy-start | bytes 12582916
  96.6 38.6 %copy-start.2 = (bf16[512,512]{1,0:T(8,128)(2,1)S(1)}, bf16[512,512]{1,0:T(8,128)(2,1)}, u32[]{:S(2)}) copy-start(bf16[512,512]{1,0:T(8,128)(2,1)} %hidden_ref.1) | copy-start | bytes 1572868
  107.5 24.2 %all-to-all-start.3 = ((bf16[8,80,512]{2,1,0:T(8,128)(2,1)}), bf16[8,80,512]{2,1,0:T(8,128)(2,1)S(1)}, u32[]{:S(2)}, u32[]{:S(2)}) async-start(bf16[8,80,512]{2,1,0:T(8,128)(2,1)} %shard_map.139), calls=%async_computation.3 | async-start | bytes 1310720 | tf_op jit(solution)/shard_map/all_to_all | solution.py:250
  131.7 15.4 %all-to-all-start.5 = ((bf16[8,128,128]{2,1,0:T(8,128)(2,1)}), bf16[8,128,128]{2,1,0:T(8,128)(2,1)S(1)}, u32[]{:S(2)}, u32[]{:S(2)}) async-start(bf16[8,128,128]{2,1,0:T(8,128)(2,1)} %reduce_sum.12), calls=%async_computation.5 | async-start | bytes 524288 | tf_op jit(solution)/shard_map/all_to_all | solution.py:250

commit v2 on v1

v2 whole, which is shorter than its diff:
```python
import functools
import math

import jax
import jax.numpy as jnp
from jax import lax
from jax.experimental import pallas as pl
from jax.experimental.pallas import tpu as pltpu
from jax.sharding import PartitionSpec as P

HD = 128
TOK_DEV = 512
ROTARY_BASE = 500000.0
LOWEST = -1e30
DEAD_MARK = 1024.0
DEAD_LIMIT = 512.0
SCALE = 1.0 / math.sqrt(HD)
FACTOR = SCALE * math.log2(math.e)
F32 = jnp.float32
BF16 = jnp.bfloat16

VMEM = pl.BlockSpec(memory_space=pltpu.VMEM)
SMEM = pl.BlockSpec(memory_space=pltpu.SMEM)
HBM = pl.BlockSpec(memory_space=pltpu.HBM)


def call(kernel, out_shape, in_specs, scratch=(), limit=32, out_specs=None):
    return pl.pallas_call(
        kernel,
        out_shape=out_shape,
        in_specs=in_specs,
        out_specs=out_specs or jax.tree.map(lambda _: VMEM, out_shape),
        scratch_shapes=list(scratch),
        compiler_params=pltpu.CompilerParams(vmem_limit_bytes=limit * 1024 * 1024),
    )


def turn(rows, cos_full, sin_signed):
    return rows * cos_full + pltpu.roll(rows, HD // 2, 1) * sin_signed


def matmul(a, b, dims):
    return lax.dot_general(a, b, (dims, ((), ())), preferred_element_type=F32)


def as_column(row):
    count = row.shape[1]
    down = lax.broadcasted_iota(jnp.int32, (count, count), 0)
    across = lax.broadcasted_iota(jnp.int32, (count, count), 1)
    return jnp.sum(jnp.where(down == across, row, 0.0), axis=1, keepdims=True)


def live_row(count_ref, slots):
    return lax.broadcasted_iota(jnp.int32, (1, slots), 1) < count_ref[0]


def stacked_heads(field):
    heads = field.shape[1] // HD
    return jnp.concatenate([field[:, h * HD : (h + 1) * HD].astype(F32) for h in range(heads)], axis=0)


def payload_kernel(count_ref, pair_ref, position_ref, frequency_ref, pay_ref, copies_ref, cos_ref, sin_ref):
    slots = cos_ref.shape[0]
    angles = as_column(position_ref[...]) * frequency_ref[...]
    col_ids = lax.broadcasted_iota(jnp.int32, (slots, HD), 1)
    row_ids = lax.broadcasted_iota(jnp.int32, (slots, HD), 0)
    cos_full = jnp.cos(angles)
    sin_signed = jnp.where(col_ids < HD // 2, -1.0, 1.0) * jnp.sin(angles)
    cos_ref[...] = cos_full
    sin_ref[...] = sin_signed
    turned = turn(pair_ref[0:slots, :].astype(F32), cos_full, sin_signed).astype(BF16)
    marked = (row_ids >= count_ref[0]) & (col_ids == 0)
    value = jnp.where(marked, DEAD_MARK, pair_ref[slots : 2 * slots, :].astype(F32)).astype(BF16)
    pay_ref[0:slots, :] = turned
    pay_ref[slots : 2 * slots, :] = value
    for i in range(copies_ref.shape[0]):
        copies_ref[i, 0:slots, :] = turned
        copies_ref[i, slots : 2 * slots, :] = value


def copies_kernel(in_ref, out_ref, sems):
    copies = [pltpu.make_async_copy(in_ref, out_ref.at[i], sems.at[i]) for i in range(out_ref.shape[0])]
    for copy in copies:
        copy.start()
    for copy in copies:
        copy.wait()


def weight_kernel(place_ref, weight_ref, held_ref, sems):
    parts, _, width = held_ref.shape
    way = 1 - 2 * lax.rem(place_ref[0], 2)
    copies = []
    for at, step in enumerate(doubling_order(parts)):
        owner = lax.rem(place_ref[1] - step * way + parts, parts)
        columns = pl.ds(pl.multiple_of(owner * width, width), width)
        copies.append(pltpu.make_async_copy(weight_ref.at[:, columns], held_ref.at[at], sems.at[at]))
    for copy in copies:
        copy.start()
    for copy in copies:
        copy.wait()


def query_kernel(query_ref, cos_ref, sin_ref, out_ref):
    cos_full, sin_signed = cos_ref[...], sin_ref[...]
    for h in range(query_ref.shape[1] // HD):
        part = query_ref[:, h * HD : (h + 1) * HD].astype(F32)
        out_ref[:, h * HD : (h + 1) * HD] = turn(part, cos_full, sin_signed).astype(BF16)


def cotangent_kernel(count_ref, held_ref, logit_ref, cot_ref, part_ref, grad_ref, bundle_ref):
    slots = grad_ref.shape[0]
    bundle_ref[0 : HD + 8, :] = part_ref[...]
    gate = jnp.where(live_row(count_ref, slots), 1.0 / (1.0 + jnp.exp(-logit_ref[...])), 0.0)
    total = None
    for step in range(held_ref.shape[0]):
        part = matmul(cot_ref[step], held_ref[step], ((1,), (1,)))
        total = part if total is None else total + part
    grad = (total * as_column(gate)).astype(BF16)
    grad_ref[...] = grad
    bundle_ref[HD + 8 : HD + 8 + slots, :] = grad.astype(F32)


def forward_kernel(dims, place_ref, index_ref, own_ref, sibling_ref, pay_ref, piece_ref, part_ref, weight_ref, score_ref):
    ny, nx, nc = dims
    slots = own_ref.shape[0]
    rows = part_ref.shape[1]
    keys = ny * slots
    me = place_ref[0]
    my_core = lax.rem(me, nc)
    my_x = lax.rem(lax.div(me, nc), nx)
    my_y = lax.div(me, nc * nx)

    query = jnp.concatenate([stacked_heads(own_ref[...]), stacked_heads(sibling_ref[...])], axis=0)
    query_t = query.T.astype(BF16)
    index_row = index_ref[...].astype(F32)
    index_col = as_column(index_row)
    beyond = jnp.where(my_core == 0, 2.0 * TOK_DEV, -1.0)
    sibling_row = jnp.full((1, rows // 2), 1.0, F32) * beyond
    own_rows = rows // 2 // slots
    limit_row = jnp.concatenate([index_row] * own_rows + [sibling_row], axis=1)

    peak = jnp.full((1, rows), LOWEST, F32)
    for x in range(nx):
        scores = matmul(piece_ref[x, :, 0:slots, :].reshape(keys, HD), query_t, ((1,), (0,)))
        for y in range(ny):
            shard = (y * nx + x) * nc + my_core
            reach = jnp.where(shard < me, 0.0, LOWEST)
            first = piece_ref[x, y, slots : 2 * slots, 0:1].astype(F32)
            bias = jnp.where(first > DEAD_LIMIT, LOWEST, reach)
            block = scores[y * slots : (y + 1) * slots, :] + bias
            score_ref[x, y * slots : (y + 1) * slots, :] = block
            peak = jnp.maximum(peak, jnp.max(block, axis=0, keepdims=True))

    own_keys, own_values = pay_ref[0:slots, :], pay_ref[slots : 2 * slots, :]
    own_scores = matmul(own_keys, query_t, ((1,), (0,)))
    own_scores = jnp.where(index_col <= limit_row, own_scores, LOWEST)
    own_scores = own_scores + jnp.where(own_values[:, 0:1].astype(F32) > DEAD_LIMIT, LOWEST, 0.0)
    own_at = pl.ds(pl.multiple_of(my_y * slots, slots), slots)
    score_ref[pl.ds(my_x, 1), own_at, :] = own_scores[None]
    peak = jnp.maximum(peak, jnp.max(own_scores, axis=0, keepdims=True))

    total = jnp.zeros((1, rows), F32)
    summed = jnp.zeros((HD, rows), F32)
    for x in range(nx):
        weights = jnp.exp2((score_ref[x] - peak) * FACTOR)
        total = total + jnp.sum(weights, axis=0, keepdims=True)
        weights = weights.astype(BF16)
        weight_ref[x] = weights
        values = piece_ref[x, :, slots : 2 * slots, :].reshape(keys, HD)
        summed = summed + matmul(values, weights, ((0,), (0,)))
    part_ref[0:HD, :] = summed
    row_ids = lax.broadcasted_iota(jnp.int32, (8, rows), 0)
    part_ref[HD : HD + 8, :] = jnp.where(row_ids == 0, peak, total)


def backward_kernel(
    dims, own_part, sibling_part, own_ref, sibling_ref, grad_ref, weight_ref, piece_ref, att_ref, delta_ref, dq_ref, dq_sibling_ref, out_ref, stage, sems
):
    ny, nx, nc = dims
    slots = own_ref.shape[0]
    rows = own_part.shape[1]
    half = rows // 2
    heads = half // slots
    keys = ny * slots

    def swapped(at):
        return jnp.concatenate([sibling_part[at, half:rows], sibling_part[at, 0:half]], axis=1)

    stats = pl.ds(HD, 8)
    mine, theirs = own_part[stats, :], swapped(stats)
    peak = jnp.maximum(mine[0:1], theirs[0:1])
    mine_factor = jnp.exp2((mine[0:1] - peak) * FACTOR)
    their_factor = jnp.exp2((theirs[0:1] - peak) * FACTOR)
    inverse = 1.0 / (mine[1:2] * mine_factor + theirs[1:2] * their_factor)
    body = pl.ds(0, HD)
    mine_factor, their_factor = mine_factor * inverse, their_factor * inverse
    att_t = own_part[body, :] * mine_factor + swapped(body) * their_factor
    att_t = att_t.astype(BF16).astype(F32)
    att = att_t[:, 0:half].T.astype(BF16)
    for h in range(heads):
        att_ref[:, h * HD : (h + 1) * HD] = att[h * slots : (h + 1) * slots, :]

    query_t = jnp.concatenate([stacked_heads(own_ref[...]), stacked_heads(sibling_ref[...])], axis=0).T
    sibling_grad = sibling_part[HD + 8 : HD + 8 + slots, :]
    grad_t = jnp.concatenate([stacked_heads(grad_ref[...]), stacked_heads(sibling_grad)], axis=0).T
    grad_tb = grad_t.astype(BF16)
    delta = jnp.sum(att_t * grad_t, axis=0, keepdims=True)
    delta_ref[...] = jnp.broadcast_to(delta[:, 0:half], delta_ref.shape)

    query_scaled = (query_t * (mine_factor * SCALE)).astype(BF16)
    grad_scaled = (grad_t * mine_factor).astype(BF16)
    dq_t = jnp.zeros((HD, rows), F32)
    copies = []
    for x in range(nx):
        weights = weight_ref[x]
        values = piece_ref[x, :, slots : 2 * slots, :].reshape(keys, HD)
        grad_probs = matmul(values, grad_tb, ((1,), (0,)))
        grad_score = (weights.astype(F32) * (grad_probs - delta)).astype(BF16)
        key_part = matmul(grad_score, query_scaled, ((1,), (1,)))
        value_part = matmul(weights, grad_scaled, ((1,), (1,)))
        stage[x, :, 0:slots, :] = key_part.astype(BF16).reshape(ny, slots, HD)
        stage[x, :, slots : 2 * slots, :] = value_part.astype(BF16).reshape(ny, slots, HD)
        copies.append(pltpu.make_async_copy(stage.at[x], out_ref.at[x], sems.at[x]))
        copies[-1].start()
        dq_t = dq_t + matmul(piece_ref[x, :, 0:slots, :].reshape(keys, HD), grad_score, ((0,), (0,)))
    dq = (dq_t * (mine_factor * SCALE)).T
    dq_ref[...] = dq[0:half, :]
    dq_sibling_ref[...] = dq[half:rows, :].astype(BF16)
    for copy in copies:
        copy.wait()


def projection_kernel(held_ref, att_ref, delta_ref, near_ref, far_ref):
    slots = att_ref.shape[0]
    half, _, width = near_ref.shape
    rows = delta_ref.shape[1]
    delta = delta_ref[...]
    row_sum = delta[:, 0:slots]
    for h in range(1, rows // slots):
        row_sum = row_sum + delta[:, h * slots : (h + 1) * slots]
    extra = jnp.concatenate([row_sum, jnp.zeros((8, width - slots), F32)], axis=1)
    extra = jnp.concatenate([extra, extra], axis=0).astype(BF16)
    att = att_ref[...]
    for step in range(held_ref.shape[0]):
        part_ref, at = (near_ref, step) if step < half else (far_ref, step - half)
        part_ref[at, 0:slots, :] = matmul(att, held_ref[step], ((1,), (0,))).astype(BF16)
        part_ref[at, slots : slots + 16, :] = extra


def added_up(stack_ref):
    total = stack_ref[0].astype(F32)
    for step in range(1, stack_ref.shape[0]):
        total = total + stack_ref[step].astype(F32)
    return total


def sum_kernel(stack_ref, out_ref):
    out_ref[...] = added_up(stack_ref).astype(BF16)


def update_kernel(count_ref, own_ref, landed_ref, logit_ref, index_ref, hidden_ref, update_ref, after_ref, grad_ref):
    slots = update_ref.shape[0]
    tokens = hidden_ref.shape[0]
    live = live_row(count_ref, slots)
    gate = 1.0 / (1.0 + jnp.exp(-logit_ref[...]))
    total = own_ref[0].astype(F32) + landed_ref[0].astype(F32)
    update = (total[0:slots, :] * as_column(jnp.where(live, gate, 0.0))).astype(BF16)
    update_ref[...] = update
    token_ids = lax.broadcasted_iota(jnp.int32, (tokens, slots), 0)
    chosen = jnp.where(token_ids == index_ref[...], 1.0, 0.0).astype(BF16)
    added = matmul(chosen, update, ((1,), (0,)))
    after_ref[...] = (hidden_ref[...].astype(F32) + added).astype(BF16)
    grad_ref[...] = jnp.where(live, total[slots : slots + 1, 0:slots] * (1.0 - gate), 0.0)


def query_grad_kernel(cos_ref, sin_ref, own_ref, arrived_ref, dq_ref):
    slots = dq_ref.shape[0]
    total = own_ref[...] + arrived_ref[...].astype(F32)
    for h in range(dq_ref.shape[1] // HD):
        back = turn(total[h * slots : (h + 1) * slots, :], cos_ref[...], -sin_ref[...])
        dq_ref[:, h * HD : (h + 1) * HD] = back.astype(BF16)


def finish_kernel(cos_ref, sin_ref, landed_ref, dk_ref, dv_ref):
    slots = dk_ref.shape[0]
    total = added_up(landed_ref)
    dk_ref[...] = turn(total[0:slots, :], cos_ref[...], -sin_ref[...]).astype(BF16)
    dv_ref[...] = total[slots : 2 * slots, :].astype(BF16)


def doubling_steps(count):
    steps = []
    step = count // 2
    while step:
        steps.append(step)
        step //= 2
    return steps


def doubling_order(count):
    order = [0]
    for step in doubling_steps(count):
        order = order + [place + step for place in order]
    return order


def on_device(
    dims,
    tp_count,
    queries,
    key_vectors,
    value_vectors,
    out_weight,
    router_logit,
    chosen_index,
    chosen_count,
    out_cotangent,
    hidden_state,
):
    ny, nx, nc = dims
    slots, width = queries.shape
    heads = width // HD
    rows = nc * heads * slots
    keys = ny * slots

    def at(y, x, c):
        return (y * nx + x) * nc + c

    y_groups = [[at(y, x, c) for y in range(ny)] for x in range(nx) for c in range(nc)]
    x_groups = [[at(y, x, c) for x in range(nx)] for y in range(ny) for c in range(nc)]

    def exchange(array, groups):
        return lax.all_to_all(array, "ctx", 0, 0, axis_index_groups=groups, tiled=True)

    def to_sibling(array):
        return lax.ppermute(array, "ctx", [(i, i ^ 1) for i in range(ny * nx * nc)])

    def tp_send(array, shift):
        pairs = []
        for shard in range(ny * nx * nc):
            for part in range(tp_count):
                to = (part + shift * (1 - 2 * (shard % nc))) % tp_count
                pairs.append((shard * tp_count + part, shard * tp_count + to))
        return lax.ppermute(array, ("ctx", "tp"), pairs)

    def summed(first, second):
        return (first.astype(F32) + second.astype(F32)).astype(BF16)

    my_shard = lax.axis_index("ctx").astype(jnp.int32)
    place = jnp.stack([my_shard, lax.axis_index("tp").astype(jnp.int32)])
    index_row = chosen_index[None, :]
    logit_row = router_logit[None, :]
    half = jnp.arange(HD // 2, dtype=F32)
    frequency = ROTARY_BASE ** (-(half * 2.0 / HD))
    frequency = jnp.concatenate([frequency, frequency])[None, :]

    payload, payloads, cos_full, sin_signed = call(
        payload_kernel,
        [
            jax.ShapeDtypeStruct((2 * slots, HD), BF16),
            jax.ShapeDtypeStruct((ny, 2 * slots, HD), BF16),
            jax.ShapeDtypeStruct((slots, HD), F32),
            jax.ShapeDtypeStruct((slots, HD), F32),
        ],
        [SMEM] + [VMEM] * 3,
    )(
        chosen_count,
        jnp.concatenate([key_vectors, value_vectors], axis=0),
        (my_shard * TOK_DEV + chosen_index).astype(F32)[None, :],
        frequency,
    )
    column = exchange(payloads, y_groups)

    own_queries = call(
        query_kernel, jax.ShapeDtypeStruct((slots, width), BF16), [VMEM] * 3
    )(queries, cos_full, sin_signed)
    sibling_queries = to_sibling(own_queries)
    column, sibling_queries = lax.optimization_barrier((column, sibling_queries))
    columns = call(
        copies_kernel,
        jax.ShapeDtypeStruct((nx,) + column.shape, BF16),
        [VMEM],
        [pltpu.SemaphoreType.DMA((nx,))],
        out_specs=HBM,
    )(column)
    pieces = exchange(columns, x_groups)

    held = call(
        weight_kernel,
        jax.ShapeDtypeStruct((tp_count, width, width), BF16),
        [SMEM, HBM],
        [pltpu.SemaphoreType.DMA((tp_count,))],
    )(place, out_weight)

    cot = out_cotangent[None]
    for step in doubling_steps(tp_count):
        if step == 1:
            cot, held = lax.optimization_barrier((cot, held))
        cot = jnp.concatenate([cot, tp_send(cot, step)], axis=0)

    part, weights = call(
        functools.partial(forward_kernel, dims),
        [
            jax.ShapeDtypeStruct((HD + 8, rows), F32),
            jax.ShapeDtypeStruct((nx, keys, rows), BF16),
        ],
        [SMEM] + [VMEM] * 5,
        [pltpu.VMEM((nx, keys, rows), F32)],
    )(place, index_row, own_queries, sibling_queries, payload, pieces)
    grad_attention, bundle = call(
        cotangent_kernel,
        [
            jax.ShapeDtypeStruct((slots, width), BF16),
            jax.ShapeDtypeStruct((HD + 8 + slots, rows), F32),
        ],
        [SMEM] + [VMEM] * 4,
    )(chosen_count, held, logit_row, cot, part)
    sibling_bundle = to_sibling(bundle)
    attention, delta, dq_own, dq_sibling, outs = call(
        functools.partial(backward_kernel, dims),
        [
            jax.ShapeDtypeStruct((slots, width), BF16),
            jax.ShapeDtypeStruct((8, rows // 2), F32),
            jax.ShapeDtypeStruct((rows // 2, HD), F32),
            jax.ShapeDtypeStruct((rows // 2, HD), BF16),
            jax.ShapeDtypeStruct((nx, ny, 2 * slots, HD), BF16),
        ],
        [VMEM] * 7,
        [pltpu.VMEM((nx, ny, 2 * slots, HD), BF16), pltpu.SemaphoreType.DMA((nx,))],
        out_specs=[VMEM] * 4 + [HBM],
    )(part, sibling_bundle, own_queries, sibling_queries, grad_attention, weights, pieces)

    crossed = exchange(outs, x_groups)
    near, far = call(
        projection_kernel,
        [jax.ShapeDtypeStruct((tp_count // 2, slots + 16, width), BF16)] * 2,
        [VMEM] * 3,
    )(held, attention, delta)
    dq_arrived = to_sibling(dq_sibling)
    grad_queries = call(
        query_grad_kernel, jax.ShapeDtypeStruct((slots, width), BF16), [VMEM] * 4
    )(cos_full, sin_signed, dq_own, dq_arrived)

    for step in reversed(doubling_steps(tp_count)):
        arrived = tp_send(far, -step)
        if step == 1:
            arrived, grad_queries = lax.optimization_barrier((arrived, grad_queries))
        if near.shape[0] > 1:
            count = near.shape[0] // 2
            far = summed(near[count:], arrived[count:])
            near = summed(near[:count], arrived[:count])
    stacked = call(sum_kernel, jax.ShapeDtypeStruct((ny, 2 * slots, HD), BF16), [VMEM])(crossed)
    landed = exchange(stacked, y_groups)
    grad_keys, grad_values = call(
        finish_kernel, [jax.ShapeDtypeStruct((slots, HD), BF16)] * 2, [VMEM] * 3
    )(cos_full, sin_signed, landed)

    update, hidden_after, grad_row = call(
        update_kernel,
        [
            jax.ShapeDtypeStruct((slots, width), BF16),
            jax.ShapeDtypeStruct(hidden_state.shape, BF16),
            jax.ShapeDtypeStruct((1, slots), F32),
        ],
        [SMEM] + [VMEM] * 5,
    )(chosen_count, near, arrived, logit_row, index_row, hidden_state)
    return (update, grad_queries, grad_keys, grad_values, grad_row[0], hidden_after)


def layout(shards):
    nx = 4 if shards >= 16 else 2
    return (shards // (nx * 2), nx, 2)


def solution(mesh):
    shards, tp_count = mesh.shape["ctx"], mesh.shape["tp"]
    placed = (
        P("ctx", "tp"),
        P("ctx", "tp"),
        P("ctx", "tp"),
        P("tp", None),
        P("ctx"),
        P("ctx"),
        P("ctx"),
        P("ctx", "tp"),
        P("ctx", "tp"),
    )
    return jax.shard_map(
        functools.partial(on_device, layout(shards), tp_count),
        mesh=mesh,
        in_specs=placed,
        out_specs=(
            P("ctx", "tp"),
            P("ctx", "tp"),
            P("ctx", "tp"),
            P("ctx", "tp"),
            P("ctx"),
            P("ctx", "tp"),
        ),
        check_vma=False,
    )
```

time: 149 us -> 107 us (0.72)
  the two profiles are of different devices: /device:TPU:1 before, /device:TPU:2 now
where the time goes in v2:
time: 107 us; the launch traced here: 106 us
  starting transfers between devices  59.4 us (56%)
  waiting for transfers between devices  19.3 us (18%)
  Pallas kernels  14.3 us (13%)
  local copies, waits for them, and re-layouts  9.36 us (9%)
  other arithmetic  1.78 us (2%)
  between operations  1.56 us (1%)
    ppermute x6, starting transfers between devices, tp_send(): return lax.ppermute(array, ('ctx', 'tp'), pairs)  32.5 us
    all_to_all x4, starting transfers between devices, exchange(): lax.all_to_all(array, 'ctx', 0, 0, axis_index_groups=groups, tiled=True)  21.2 us
    ppermute x6, waiting for transfers between devices, tp_send(): return lax.ppermute(array, ('ctx', 'tp'), pairs)  16.3 us
    unnamed x18, local copies, waits for them, and re-layouts  9.36 us
    ppermute x3, starting transfers between devices, to_sibling(): return lax.ppermute(array, 'ctx', [(i, i ^ 1) for i in range(ny * nx * nc)])  5.76 us
    ppermute x3, waiting for transfers between devices, to_sibling(): return lax.ppermute(array, 'ctx', [(i, i ^ 1) for i in range(ny * nx * nc)])  2.93 us
    pallas_call x1, Pallas kernels, on_device(): call(functools.partial(backward_kernel, dims), [jax.ShapeDtypeStruct((slo...  2.89 us
    pallas_call x1, Pallas kernels, on_device(): call(functools.partial(forward_kernel, dims), [jax.ShapeDtypeStruct((HD +...  2.38 us
  transfers between devices with their start and end apart: 13, of which 7 were waited for; matrix products, arithmetic and copies ran while one was open for 0% of the time, Pallas kernels for 6%

profile of v2, /device:TPU:2, one launch (start us, length us, event | category | flops | bytes accessed | tf_op | source)
XLA Modules:
  0.0 105.7 jit_solution(14086467205570624685)
XLA Ops:
  3.7 7.1 %all-to-all-start = ((bf16[8,128,128]{2,1,0:T(8,128)(2,1)}), bf16[8,128,128]{2,1,0:T(8,128)(2,1)S(1)}, u32[]{:S(2)}, u32[]{:S(2)}) async-start(bf16[8,128,128]{2,1,0:T(8,128)(2,1)} %get-tuple-element.35), calls=%async_computation | async-start | bytes 524288 | tf_op jit(solution)/shard_map/all_to_all | solution.py:333
  11.8 1.9 %collective-permute-start.2 = (bf16[64,512]{1,0:T(8,128)(2,1)S(1)}, bf16[64,512]{1,0:T(8,128)(2,1)S(1)}, u32[]{:S(2)}, u32[]{:S(2)}) collective-permute-start(bf16[64,512]{1,0:T(8,128)(2,1)S(1)} %shard_map.138.own_ref), channel_id=1, source_target_pairs={{0,8},{8,0},{16,24},{24,16},{32,40},{40,32},{48,56},{56,48},{64,72... | collective-permute-start | bytes 196616 | tf_op jit(solution)/shard_map/ppermute | solution.py:336
  13.7 10.9 %collective-permute-start = (bf16[1,64,512]{2,1,0:T(8,128)(2,1)}, bf16[1,64,512]{2,1,0:T(8,128)(2,1)S(1)}, u32[]{:S(2)}, u32[]{:S(2)}) collective-permute-start(bf16[1,64,512]{2,1,0:T(8,128)(2,1)} %bitcast.14), channel_id=1, source_target_pairs={{0,4},{1,5},{2,6},{3,7},{4,0},{5,1},{6,2},{7,3},{8,12},{9,13},{10,... | collective-permute-start | bytes 196616 | tf_op jit(solution)/shard_map/ppermute | solution.py:344
  25.7 4.8 %all-to-all-start.1 = ((bf16[4,8,128,128]{3,2,1,0:T(8,128)(2,1)}), bf16[4,8,128,128]{3,2,1,0:T(8,128)(2,1)S(1)}, u32[]{:S(2)}, u32[]{:S(2)}) async-start(bf16[4,8,128,128]{3,2,1,0:T(8,128)(2,1)} %shard_map.139), calls=%async_computation.1 | async-start | bytes 2097152 | tf_op jit(solution)/shard_map/all_to_all | solution.py:333
  30.6 4.3 %collective-permute-start.1 = (bf16[2,64,512]{2,1,0:T(8,128)(2,1)S(1)}, bf16[2,64,512]{2,1,0:T(8,128)(2,1)S(1)}, u32[]{:S(2)}, u32[]{:S(2)}) collective-permute-start(bf16[2,64,512]{2,1,0:T(8,128)(2,1)S(1)} %pad_maximum_fusion.2), channel_id=1, source_target_pairs={{0,2},{1,3},{2,4},{3,5},{4,6},{5,7},{6,0},{7,1},{8,14},{9,15},{10,... | collective-permute-start | bytes 393224 | tf_op jit(solution)/shard_map/ppermute | solution.py:344
  35.0 2.2 %copy-done.3 = bf16[512,4096]{1,0:T(8,128)(2,1)S(1)} copy-done((bf16[512,4096]{1,0:T(8,128)(2,1)S(1)}, bf16[512,4096]{1,0:T(8,128)(2,1)}, u32[]{:S(2)}) %copy-start.3) | copy-done | bytes 4194328
  38.5 1.9 %copy-done = bf16[8,512,512]{2,1,0:T(8,128)(2,1)} copy-done((bf16[8,512,512]{2,1,0:T(8,128)(2,1)}, bf16[8,512,512]{2,1,0:T(8,128)(2,1)S(1)}, u32[]{:S(2)}) %copy-start) | copy-done | bytes 4194328
  40.4 2.2 %collective-permute-done.1 = bf16[2,64,512]{2,1,0:T(8,128)(2,1)S(1)} collective-permute-done((bf16[2,64,512]{2,1,0:T(8,128)(2,1)S(1)}, bf16[2,64,512]{2,1,0:T(8,128)(2,1)S(1)}, u32[]{:S(2)}, u32[]{:S(2)}) %collective-permute-start.1) | collective-permute-done | bytes 131104 | tf_op jit(solution)/shard_map/ppermute | solution.py:344
  42.7 4.7 %collective-permute-start.3 = (bf16[4,64,512]{2,1,0:T(8,128)(2,1)S(1)}, bf16[4,64,512]{2,1,0:T(8,128)(2,1)S(1)}, u32[]{:S(2)}, u32[]{:S(2)}) collective-permute-start(bf16[4,64,512]{2,1,0:T(8,128)(2,1)S(1)} %pad_maximum_fusion.1), channel_id=1, source_target_pairs={{0,1},{1,2},{2,3},{3,4},{4,5},{5,6},{6,7},{7,0},{8,15},{9,8},{10,9... | collective-permute-start | bytes 786440 | tf_op jit(solution)/shard_map/ppermute | solution.py:344
  47.3 5.8 %collective-permute-done.3 = bf16[4,64,512]{2,1,0:T(8,128)(2,1)S(1)} collective-permute-done((bf16[4,64,512]{2,1,0:T(8,128)(2,1)S(1)}, bf16[4,64,512]{2,1,0:T(8,128)(2,1)S(1)}, u32[]{:S(2)}, u32[]{:S(2)}) %collective-permute-start.3) | collective-permute-done | bytes 262176 | tf_op jit(solution)/shard_map/ppermute | solution.py:344
  53.2 2.4 %shard_map.140 = (f32[136,512]{1,0:T(8,128)S(1)}, bf16[4,512,512]{2,1,0:T(8,128)(2,1)S(1)}) custom-call(s32[2]{0:T(128)S(1)} %pad_add_fusion.place_ref, s32[1,64]{1,0:T(1,128)S(1)} %bitcast.10, bf16[64,512]{1,0:T(8,128)(2,1)S(1)} %shard_map.138.own_ref, bf16[64,512]{1,0:T(8,128)(2,1)S(1)} %collective-permute-done.2.sibling_ref, ...), custom_call_target="tpu_custom_call" | custom-call | tf_op jit(solution)/shard_map/pallas_call | solution.py:401
  55.6 2.2 %copy-done.1 = bf16[8,512,512]{2,1,0:T(8,128)(2,1)S(1)} copy-done((bf16[8,512,512]{2,1,0:T(8,128)(2,1)S(1)}, bf16[8,512,512]{2,1,0:T(8,128)(2,1)}, u32[]{:S(2)}) %copy-start.1) | copy-done | bytes 4194328
  57.8 1.4 %shard_map.141 = (bf16[64,512]{1,0:T(8,128)(2,1)S(1)}, f32[200,512]{1,0:T(8,128)S(1)}) custom-call(s32[1]{0:T(128)S(6)} %copy.15.count_ref, bf16[8,512,512]{2,1,0:T(8,128)(2,1)S(1)} %copy-done.1, f32[1,64]{1,0:T(1,128)S(1)} %bitcast.12, bf16[8,64,512]{2,1,0:T(8,128)(2,1)S(1)} %pad_maximum_fusion.cot_ref, f32[136,512]{1,0:T(8,128)S(1)} %get-tuple-element.39.part_ref.own_part), custom_call_target="tpu_custom_call" | custom-call | tf_op jit(solution)/shard_map/pallas_call | solution.py:410
  59.2 1.9 %collective-permute-start.4 = (f32[200,512]{1,0:T(8,128)S(1)}, f32[200,512]{1,0:T(8,128)S(1)}, u32[]{:S(2)}, u32[]{:S(2)}) collective-permute-start(f32[200,512]{1,0:T(8,128)S(1)} %get-tuple-element.41), channel_id=1, source_target_pairs={{0,8},{8,0},{16,24},{24,16},{32,40},{40,32},{48,56},{56,48},{64,72... | collective-permute-start | bytes 1228808 | tf_op jit(solution)/shard_map/ppermute | solution.py:336
  61.1 1.7 %collective-permute-done.4.sibling_part = f32[200,512]{1,0:T(8,128)S(1)} collective-permute-done((f32[200,512]{1,0:T(8,128)S(1)}, f32[200,512]{1,0:T(8,128)S(1)}, u32[]{:S(2)}, u32[]{:S(2)}) %collective-permute-start.4) | collective-permute-done | bytes 409632 | tf_op jit(solution)/shard_map/ppermute | solution.py:336
  62.8 2.9 %shard_map.142 = (bf16[64,512]{1,0:T(8,128)(2,1)S(1)}, f32[8,256]{1,0:T(8,128)S(1)}, f32[256,128]{1,0:T(8,128)S(1)}, bf16[256,128]{1,0:T(8,128)(2,1)S(1)}, bf16[4,8,128,128]{3,2,1,0:T(8,128)(2,1)}) custom-call(f32[136,512]{1,0:T(8,128)S(1)} %get-tuple-element.39.part_ref.own_part, f32[200,512]{1,0:T(8,128)S(1)} %collective-permute-done.4.sibling_part, ...), custom_call_target="tpu_custom_call" | custom-call | tf_op jit(solution)/shard_map/pallas_call | solution.py:419
  65.7 4.9 %all-to-all-start.2 = ((bf16[4,8,128,128]{3,2,1,0:T(8,128)(2,1)}), bf16[4,8,128,128]{3,2,1,0:T(8,128)(2,1)S(1)}, u32[]{:S(2)}, u32[]{:S(2)}) async-start(bf16[4,8,128,128]{3,2,1,0:T(8,128)(2,1)} %get-tuple-element.53), calls=%async_computation.2 | async-start | bytes 2097152 | tf_op jit(solution)/shard_map/all_to_all | solution.py:333
  70.7 2.2 %copy-done.2 = bf16[8,512,512]{2,1,0:T(8,128)(2,1)S(1)} copy-done((bf16[8,512,512]{2,1,0:T(8,128)(2,1)S(1)}, bf16[8,512,512]{2,1,0:T(8,128)(2,1)}, u32[]{:S(2)}) %copy-start.2) | copy-done | bytes 4194328
  73.7 3.9 %collective-permute-start.5 = (bf16[4,80,512]{2,1,0:T(8,128)(2,1)S(1)}, bf16[4,80,512]{2,1,0:T(8,128)(2,1)S(1)}, u32[]{:S(2)}, u32[]{:S(2)}) collective-permute-start(bf16[4,80,512]{2,1,0:T(8,128)(2,1)S(1)} %get-tuple-element.47), channel_id=1, source_target_pairs={{0,7},{1,0},{2,1},{3,2},{4,3},{5,4},{6,5},{7,6},{8,9},{9,10},{10,1... | collective-permute-start | bytes 983048 | tf_op jit(solution)/shard_map/ppermute | solution.py:344
  77.6 1.9 %collective-permute-start.6 = (bf16[256,128]{1,0:T(8,128)(2,1)S(1)}, bf16[256,128]{1,0:T(8,128)(2,1)S(1)}, u32[]{:S(2)}, u32[]{:S(2)}) collective-permute-start(bf16[256,128]{1,0:T(8,128)(2,1)S(1)} %get-tuple-element.49), channel_id=1, source_target_pairs={{0,8},{8,0},{16,24},{24,16},{32,40},{40,32},{48,56},{56,48},{64,72... | collective-permute-start | bytes 196616 | tf_op jit(solution)/shard_map/ppermute | solution.py:336
  82.8 3.7 %collective-permute-start.7 = (bf16[2,80,512]{2,1,0:T(8,128)(2,1)S(1)}, bf16[2,80,512]{2,1,0:T(8,128)(2,1)S(1)}, u32[]{:S(2)}, u32[]{:S(2)}) collective-permute-start(bf16[2,80,512]{2,1,0:T(8,128)(2,1)S(1)} %get-tuple-element.59), channel_id=1, source_target_pairs={{0,6},{1,7},{2,0},{3,1},{4,2},{5,3},{6,4},{7,5},{8,10},{9,11},{10,... | collective-permute-start | bytes 491528 | tf_op jit(solution)/shard_map/ppermute | solution.py:344
  87.3 4.3 %all-to-all-start.3 = ((bf16[8,128,128]{2,1,0:T(8,128)(2,1)}), bf16[8,128,128]{2,1,0:T(8,128)(2,1)S(1)}, u32[]{:S(2)}, u32[]{:S(2)}) async-start(bf16[8,128,128]{2,1,0:T(8,128)(2,1)} %shard_map.146), calls=%async_computation.3 | async-start | bytes 524288 | tf_op jit(solution)/shard_map/all_to_all | solution.py:333
  92.5 5.0 %collective-permute-start.8 = (bf16[1,80,512]{2,1,0:T(8,128)(2,1)S(1)}, bf16[1,80,512]{2,1,0:T(8,128)(2,1)S(1)}, u32[]{:S(2)}, u32[]{:S(2)}) collective-permute-start(bf16[1,80,512]{2,1,0:T(8,128)(2,1)S(1)} %get-tuple-element.60), channel_id=1, source_target_pairs={{0,4},{1,5},{2,6},{3,7},{4,0},{5,1},{6,2},{7,3},{8,12},{9,13},{10,... | collective-permute-start | bytes 245768 | tf_op jit(solution)/shard_map/ppermute | solution.py:344
  97.6 6.3 %collective-permute-done.8.landed_ref = bf16[1,80,512]{2,1,0:T(8,128)(2,1)S(1)} collective-permute-done((bf16[1,80,512]{2,1,0:T(8,128)(2,1)S(1)}, bf16[1,80,512]{2,1,0:T(8,128)(2,1)S(1)}, u32[]{:S(2)}, u32[]{:S(2)}) %collective-permute-start.8) | collective-permute-done | bytes 81952 | tf_op jit(solution)/shard_map/ppermute | solution.py:344
  (42 shorter events, 13.6 us)
Async XLA Ops:
  0.6 29.9 %copy-start.8 = (bf16[64,512]{1,0:T(8,128)(2,1)S(1)}, bf16[64,512]{1,0:T(8,128)(2,1)}, u32[]{:S(2)}) copy-start(bf16[64,512]{1,0:T(8,128)(2,1)} %param.16) | copy-start | bytes 196612
  3.7 20.9 %all-to-all-start = ((bf16[8,128,128]{2,1,0:T(8,128)(2,1)}), bf16[8,128,128]{2,1,0:T(8,128)(2,1)S(1)}, u32[]{:S(2)}, u32[]{:S(2)}) async-start(bf16[8,128,128]{2,1,0:T(8,128)(2,1)} %get-tuple-element.35), calls=%async_computation | async-start | bytes 524288 | tf_op jit(solution)/shard_map/all_to_all | solution.py:333
  10.8 0.8 copy-start.5
  11.8 12.9 %collective-permute-start.2 = (bf16[64,512]{1,0:T(8,128)(2,1)S(1)}, bf16[64,512]{1,0:T(8,128)(2,1)S(1)}, u32[]{:S(2)}, u32[]{:S(2)}) collective-permute-start(bf16[64,512]{1,0:T(8,128)(2,1)S(1)} %shard_map.138.own_ref), channel_id=1, source_target_pairs={{0,8},{8,0},{16,24},{24,16},{32,40},{40,32},{48,56},{56,48},{64,72... | collective-permute-start | bytes 196616 | tf_op jit(solution)/shard_map/ppermute | solution.py:336
  13.7 16.9 %collective-permute-start = (bf16[1,64,512]{2,1,0:T(8,128)(2,1)}, bf16[1,64,512]{2,1,0:T(8,128)(2,1)S(1)}, u32[]{:S(2)}, u32[]{:S(2)}) collective-permute-start(bf16[1,64,512]{2,1,0:T(8,128)(2,1)} %bitcast.14), channel_id=1, source_target_pairs={{0,4},{1,5},{2,6},{3,7},{4,0},{5,1},{6,2},{7,3},{8,12},{9,13},{10,... | collective-permute-start | bytes 196616 | tf_op jit(solution)/shard_map/ppermute | solution.py:344
  25.7 27.5 %all-to-all-start.1 = ((bf16[4,8,128,128]{3,2,1,0:T(8,128)(2,1)}), bf16[4,8,128,128]{3,2,1,0:T(8,128)(2,1)S(1)}, u32[]{:S(2)}, u32[]{:S(2)}) async-start(bf16[4,8,128,128]{3,2,1,0:T(8,128)(2,1)} %shard_map.139), calls=%async_computation.1 | async-start | bytes 2097152 | tf_op jit(solution)/shard_map/all_to_all | solution.py:333
  30.6 12.0 %collective-permute-start.1 = (bf16[2,64,512]{2,1,0:T(8,128)(2,1)S(1)}, bf16[2,64,512]{2,1,0:T(8,128)(2,1)S(1)}, u32[]{:S(2)}, u32[]{:S(2)}) collective-permute-start(bf16[2,64,512]{2,1,0:T(8,128)(2,1)S(1)} %pad_maximum_fusion.2), channel_id=1, source_target_pairs={{0,2},{1,3},{2,4},{3,5},{4,6},{5,7},{6,0},{7,1},{8,14},{9,15},{10,... | collective-permute-start | bytes 393224 | tf_op jit(solution)/shard_map/ppermute | solution.py:344
  35.0 2.2 %copy-start.3 = (bf16[512,4096]{1,0:T(8,128)(2,1)S(1)}, bf16[512,4096]{1,0:T(8,128)(2,1)}, u32[]{:S(2)}) copy-start(bf16[512,4096]{1,0:T(8,128)(2,1)} %weight_ref.1) | copy-start | bytes 12582916
  37.2 16.0 %copy-start.6 = (s32[64]{0:T(128)S(1)}, s32[64]{0:T(128)}, u32[]{:S(2)}) copy-start(s32[64]{0:T(128)} %param.14) | copy-start | bytes 772
  37.2 18.4 %copy-start.7 = (f32[64]{0:T(128)S(1)}, f32[64]{0:T(128)}, u32[]{:S(2)}) copy-start(f32[64]{0:T(128)} %param.13) | copy-start | bytes 772
  38.5 2.0 %copy-start = (bf16[8,512,512]{2,1,0:T(8,128)(2,1)}, bf16[8,512,512]{2,1,0:T(8,128)(2,1)S(1)}, u32[]{:S(2)}) copy-start(bf16[8,512,512]{2,1,0:T(8,128)(2,1)S(1)} %shard_map.136.held_ref) | copy-start | bytes 12582916
  42.7 10.5 %collective-permute-start.3 = (bf16[4,64,512]{2,1,0:T(8,128)(2,1)S(1)}, bf16[4,64,512]{2,1,0:T(8,128)(2,1)S(1)}, u32[]{:S(2)}, u32[]{:S(2)}) collective-permute-start(bf16[4,64,512]{2,1,0:T(8,128)(2,1)S(1)} %pad_maximum_fusion.1), channel_id=1, source_target_pairs={{0,1},{1,2},{2,3},{3,4},{4,5},{5,6},{6,7},{7,0},{8,15},{9,8},{10,9... | collective-permute-start | bytes 786440 | tf_op jit(solution)/shard_map/ppermute | solution.py:344
  55.6 2.2 %copy-start.1 = (bf16[8,512,512]{2,1,0:T(8,128)(2,1)S(1)}, bf16[8,512,512]{2,1,0:T(8,128)(2,1)}, u32[]{:S(2)}) copy-start(bf16[8,512,512]{2,1,0:T(8,128)(2,1)} %copy-done) | copy-start | bytes 12582916
  59.2 3.6 %collective-permute-start.4 = (f32[200,512]{1,0:T(8,128)S(1)}, f32[200,512]{1,0:T(8,128)S(1)}, u32[]{:S(2)}, u32[]{:S(2)}) collective-permute-start(f32[200,512]{1,0:T(8,128)S(1)} %get-tuple-element.41), channel_id=1, source_target_pairs={{0,8},{8,0},{16,24},{24,16},{32,40},{40,32},{48,56},{56,48},{64,72... | collective-permute-start | bytes 1228808 | tf_op jit(solution)/shard_map/ppermute | solution.py:336
  65.7 38.1 %copy-start.4 = (bf16[512,512]{1,0:T(8,128)(2,1)S(1)}, bf16[512,512]{1,0:T(8,128)(2,1)}, u32[]{:S(2)}) copy-start(bf16[512,512]{1,0:T(8,128)(2,1)} %hidden_ref.1) | copy-start | bytes 1572868
  65.7 20.7 %all-to-all-start.2 = ((bf16[4,8,128,128]{3,2,1,0:T(8,128)(2,1)}), bf16[4,8,128,128]{3,2,1,0:T(8,128)(2,1)S(1)}, u32[]{:S(2)}, u32[]{:S(2)}) async-start(bf16[4,8,128,128]{3,2,1,0:T(8,128)(2,1)} %get-tuple-element.53), calls=%async_computation.2 | async-start | bytes 2097152 | tf_op jit(solution)/shard_map/all_to_all | solution.py:333
  70.7 2.2 %copy-start.2 = (bf16[8,512,512]{2,1,0:T(8,128)(2,1)S(1)}, bf16[8,512,512]{2,1,0:T(8,128)(2,1)}, u32[]{:S(2)}) copy-start(bf16[8,512,512]{2,1,0:T(8,128)(2,1)} %copy-done) | copy-start | bytes 12582916
  73.7 9.0 %collective-permute-start.5 = (bf16[4,80,512]{2,1,0:T(8,128)(2,1)S(1)}, bf16[4,80,512]{2,1,0:T(8,128)(2,1)S(1)}, u32[]{:S(2)}, u32[]{:S(2)}) collective-permute-start(bf16[4,80,512]{2,1,0:T(8,128)(2,1)S(1)} %get-tuple-element.47), channel_id=1, source_target_pairs={{0,7},{1,0},{2,1},{3,2},{4,3},{5,4},{6,5},{7,6},{8,9},{9,10},{10,1... | collective-permute-start | bytes 983048 | tf_op jit(solution)/shard_map/ppermute | solution.py:344
  77.6 3.1 %collective-permute-start.6 = (bf16[256,128]{1,0:T(8,128)(2,1)S(1)}, bf16[256,128]{1,0:T(8,128)(2,1)S(1)}, u32[]{:S(2)}, u32[]{:S(2)}) collective-permute-start(bf16[256,128]{1,0:T(8,128)(2,1)S(1)} %get-tuple-element.49), channel_id=1, source_target_pairs={{0,8},{8,0},{16,24},{24,16},{32,40},{40,32},{48,56},{56,48},{64,72... | collective-permute-start | bytes 196616 | tf_op jit(solution)/shard_map/ppermute | solution.py:336
  82.8 9.7 %collective-permute-start.7 = (bf16[2,80,512]{2,1,0:T(8,128)(2,1)S(1)}, bf16[2,80,512]{2,1,0:T(8,128)(2,1)S(1)}, u32[]{:S(2)}, u32[]{:S(2)}) collective-permute-start(bf16[2,80,512]{2,1,0:T(8,128)(2,1)S(1)} %get-tuple-element.59), channel_id=1, source_target_pairs={{0,6},{1,7},{2,0},{3,1},{4,2},{5,3},{6,4},{7,5},{8,10},{9,11},{10,... | collective-permute-start | bytes 491528 | tf_op jit(solution)/shard_map/ppermute | solution.py:344
  87.3 17.7 %all-to-all-start.3 = ((bf16[8,128,128]{2,1,0:T(8,128)(2,1)}), bf16[8,128,128]{2,1,0:T(8,128)(2,1)S(1)}, u32[]{:S(2)}, u32[]{:S(2)}) async-start(bf16[8,128,128]{2,1,0:T(8,128)(2,1)} %shard_map.146), calls=%async_computation.3 | async-start | bytes 524288 | tf_op jit(solution)/shard_map/all_to_all | solution.py:333
  92.5 11.3 %collective-permute-start.8 = (bf16[1,80,512]{2,1,0:T(8,128)(2,1)S(1)}, bf16[1,80,512]{2,1,0:T(8,128)(2,1)S(1)}, u32[]{:S(2)}, u32[]{:S(2)}) collective-permute-start(bf16[1,80,512]{2,1,0:T(8,128)(2,1)S(1)} %get-tuple-element.60), channel_id=1, source_target_pairs={{0,4},{1,5},{2,6},{3,7},{4,0},{5,1},{6,2},{7,3},{8,12},{9,13},{10,... | collective-permute-start | bytes 245768 | tf_op jit(solution)/shard_map/ppermute | solution.py:344

commit v3 on v2

--- a/solution.py
+++ b/solution.py
@@ -59,7 +59,7 @@
     return jnp.concatenate([field[:, h * HD : (h + 1) * HD].astype(F32) for h in range(heads)], axis=0)
 
 
-def payload_kernel(count_ref, pair_ref, position_ref, frequency_ref, pay_ref, copies_ref, cos_ref, sin_ref):
+def payload_kernel(count_ref, pair_ref, position_ref, frequency_ref, pay_ref, copies_ref, cos_ref, sin_ref, stage, sems):
     slots = cos_ref.shape[0]
     angles = as_column(position_ref[...]) * frequency_ref[...]
     col_ids = lax.broadcasted_iota(jnp.int32, (slots, HD), 1)
@@ -73,31 +73,24 @@
     value = jnp.where(marked, DEAD_MARK, pair_ref[slots : 2 * slots, :].astype(F32)).astype(BF16)
     pay_ref[0:slots, :] = turned
     pay_ref[slots : 2 * slots, :] = value
-    for i in range(copies_ref.shape[0]):
-        copies_ref[i, 0:slots, :] = turned
-        copies_ref[i, slots : 2 * slots, :] = value
-
-
-def copies_kernel(in_ref, out_ref, sems):
-    copies = [pltpu.make_async_copy(in_ref, out_ref.at[i], sems.at[i]) for i in range(out_ref.shape[0])]
+    chunk = stage.shape[0]
+    for i in range(chunk):
+        stage[i, 0:slots, :] = turned
+        stage[i, slots : 2 * slots, :] = value
+    copies = [
+        pltpu.make_async_copy(stage, copies_ref.at[pl.ds(i * chunk, chunk)], sems.at[i])
+        for i in range(copies_ref.shape[0] // chunk)
+    ]
     for copy in copies:
         copy.start()
     for copy in copies:
         copy.wait()
 
 
-def weight_kernel(place_ref, weight_ref, held_ref, sems):
-    parts, _, width = held_ref.shape
+def column_block(place_ref, at, parts, width):
     way = 1 - 2 * lax.rem(place_ref[0], 2)
-    copies = []
-    for at, step in enumerate(doubling_order(parts)):
-        owner = lax.rem(place_ref[1] - step * way + parts, parts)
-        columns = pl.ds(pl.multiple_of(owner * width, width), width)
-        copies.append(pltpu.make_async_copy(weight_ref.at[:, columns], held_ref.at[at], sems.at[at]))
-    for copy in copies:
-        copy.start()
-    for copy in copies:
-        copy.wait()
+    owner = lax.rem(place_ref[1] - tp_order(parts)[at] * way + 2 * parts, parts)
+    return pl.ds(pl.multiple_of(owner * width, width), width)
 
 
 def query_kernel(query_ref, cos_ref, sin_ref, out_ref):
@@ -107,28 +100,25 @@
         out_ref[:, h * HD : (h + 1) * HD] = turn(part, cos_full, sin_signed).astype(BF16)
 
 
-def cotangent_kernel(count_ref, held_ref, logit_ref, cot_ref, part_ref, grad_ref, bundle_ref):
+def cotangent_kernel(place_ref, count_ref, weight_ref, logit_ref, cot_ref, grad_ref):
     slots = grad_ref.shape[0]
-    bundle_ref[0 : HD + 8, :] = part_ref[...]
     gate = jnp.where(live_row(count_ref, slots), 1.0 / (1.0 + jnp.exp(-logit_ref[...])), 0.0)
     total = None
-    for step in range(held_ref.shape[0]):
-        part = matmul(cot_ref[step], held_ref[step], ((1,), (1,)))
+    parts, _, width = cot_ref.shape
+    for step in range(parts):
+        columns = column_block(place_ref, step, parts, width)
+        part = matmul(cot_ref[step], weight_ref[:, columns], ((1,), (1,)))
         total = part if total is None else total + part
-    grad = (total * as_column(gate)).astype(BF16)
-    grad_ref[...] = grad
-    bundle_ref[HD + 8 : HD + 8 + slots, :] = grad.astype(F32)
-
-
-def forward_kernel(dims, place_ref, index_ref, own_ref, sibling_ref, pay_ref, piece_ref, part_ref, weight_ref, score_ref):
-    ny, nx, nc = dims
+    grad_ref[...] = (total * as_column(gate)).astype(BF16)
+
+
+def forward_kernel(place_ref, index_ref, own_ref, sibling_ref, grad_ref, pay_ref, piece_ref, part_ref, weight_ref, score_ref):
     slots = own_ref.shape[0]
-    rows = part_ref.shape[1]
-    keys = ny * slots
+    groups, keys, rows = score_ref.shape
+    chunk = keys // slots
     me = place_ref[0]
-    my_core = lax.rem(me, nc)
-    my_x = lax.rem(lax.div(me, nc), nx)
-    my_y = lax.div(me, nc * nx)
+    my_core = lax.rem(me, 2)
+    my_chip = lax.div(me, 2)
 
     query = jnp.concatenate([stacked_heads(own_ref[...]), stacked_heads(sibling_ref[...])], axis=0)
     query_t = query.T.astype(BF16)
@@ -140,48 +130,49 @@
     limit_row = jnp.concatenate([index_row] * own_rows + [sibling_row], axis=1)
 
     peak = jnp.full((1, rows), LOWEST, F32)
-    for x in range(nx):
-        scores = matmul(piece_ref[x, :, 0:slots, :].reshape(keys, HD), query_t, ((1,), (0,)))
-        for y in range(ny):
-            shard = (y * nx + x) * nc + my_core
-            reach = jnp.where(shard < me, 0.0, LOWEST)
-            first = piece_ref[x, y, slots : 2 * slots, 0:1].astype(F32)
+    for group in range(groups):
+        blocks = pl.ds(group * chunk, chunk)
+        scores = matmul(piece_ref[blocks, 0:slots, :].reshape(keys, HD), query_t, ((1,), (0,)))
+        for i in range(chunk):
+            chip = group * chunk + i
+            reach = jnp.where(chip < my_chip, 0.0, LOWEST)
+            first = piece_ref[chip, slots : 2 * slots, 0:1].astype(F32)
             bias = jnp.where(first > DEAD_LIMIT, LOWEST, reach)
-            block = scores[y * slots : (y + 1) * slots, :] + bias
-            score_ref[x, y * slots : (y + 1) * slots, :] = block
+            block = scores[i * slots : (i + 1) * slots, :] + bias
+            score_ref[group, i * slots : (i + 1) * slots, :] = block
             peak = jnp.maximum(peak, jnp.max(block, axis=0, keepdims=True))
 
     own_keys, own_values = pay_ref[0:slots, :], pay_ref[slots : 2 * slots, :]
     own_scores = matmul(own_keys, query_t, ((1,), (0,)))
     own_scores = jnp.where(index_col <= limit_row, own_scores, LOWEST)
     own_scores = own_scores + jnp.where(own_values[:, 0:1].astype(F32) > DEAD_LIMIT, LOWEST, 0.0)
-    own_at = pl.ds(pl.multiple_of(my_y * slots, slots), slots)
-    score_ref[pl.ds(my_x, 1), own_at, :] = own_scores[None]
+    own_at = pl.ds(pl.multiple_of(lax.rem(my_chip, chunk) * slots, slots), slots)
+    score_ref[pl.ds(lax.div(my_chip, chunk), 1), own_at, :] = own_scores[None]
     peak = jnp.maximum(peak, jnp.max(own_scores, axis=0, keepdims=True))
 
     total = jnp.zeros((1, rows), F32)
     summed = jnp.zeros((HD, rows), F32)
-    for x in range(nx):
-        weights = jnp.exp2((score_ref[x] - peak) * FACTOR)
+    for group in range(groups):
+        weights = jnp.exp2((score_ref[group] - peak) * FACTOR)
         total = total + jnp.sum(weights, axis=0, keepdims=True)
         weights = weights.astype(BF16)
-        weight_ref[x] = weights
-        values = piece_ref[x, :, slots : 2 * slots, :].reshape(keys, HD)
+        weight_ref[group] = weights
+        values = piece_ref[pl.ds(group * chunk, chunk), slots : 2 * slots, :].reshape(keys, HD)
         summed = summed + matmul(values, weights, ((0,), (0,)))
     part_ref[0:HD, :] = summed
     row_ids = lax.broadcasted_iota(jnp.int32, (8, rows), 0)
     part_ref[HD : HD + 8, :] = jnp.where(row_ids == 0, peak, total)
+    part_ref[HD + 8 : HD + 8 + slots, :] = grad_ref[...].astype(F32)
 
 
 def backward_kernel(
-    dims, own_part, sibling_part, own_ref, sibling_ref, grad_ref, weight_ref, piece_ref, att_ref, delta_ref, dq_ref, dq_sibling_ref, out_ref, stage, sems
+    own_part, sibling_part, own_ref, sibling_ref, grad_ref, weight_ref, piece_ref, att_ref, delta_ref, dq_ref, dq_sibling_ref, out_ref, stage, sems
 ):
-    ny, nx, nc = dims
     slots = own_ref.shape[0]
-    rows = own_part.shape[1]
+    groups, keys, rows = weight_ref.shape
+    chunk = keys // slots
     half = rows // 2
     heads = half // slots
-    keys = ny * slots
 
     def swapped(at):
         return jnp.concatenate([sibling_part[at, half:rows], sibling_part[at, 0:half]], axis=1)
@@ -211,18 +202,19 @@
     grad_scaled = (grad_t * mine_factor).astype(BF16)
     dq_t = jnp.zeros((HD, rows), F32)
     copies = []
-    for x in range(nx):
-        weights = weight_ref[x]
-        values = piece_ref[x, :, slots : 2 * slots, :].reshape(keys, HD)
+    for group in range(groups):
+        blocks = pl.ds(group * chunk, chunk)
+        weights = weight_ref[group]
+        values = piece_ref[blocks, slots : 2 * slots, :].reshape(keys, HD)
         grad_probs = matmul(values, grad_tb, ((1,), (0,)))
         grad_score = (weights.astype(F32) * (grad_probs - delta)).astype(BF16)
         key_part = matmul(grad_score, query_scaled, ((1,), (1,)))
         value_part = matmul(weights, grad_scaled, ((1,), (1,)))
-        stage[x, :, 0:slots, :] = key_part.astype(BF16).reshape(ny, slots, HD)
-        stage[x, :, slots : 2 * slots, :] = value_part.astype(BF16).reshape(ny, slots, HD)
-        copies.append(pltpu.make_async_copy(stage.at[x], out_ref.at[x], sems.at[x]))
+        stage[blocks, 0:slots, :] = key_part.astype(BF16).reshape(chunk, slots, HD)
+        stage[blocks, slots : 2 * slots, :] = value_part.astype(BF16).reshape(chunk, slots, HD)
+        copies.append(pltpu.make_async_copy(stage.at[blocks], out_ref.at[blocks], sems.at[group]))
         copies[-1].start()
-        dq_t = dq_t + matmul(piece_ref[x, :, 0:slots, :].reshape(keys, HD), grad_score, ((0,), (0,)))
+        dq_t = dq_t + matmul(piece_ref[blocks, 0:slots, :].reshape(keys, HD), grad_score, ((0,), (0,)))
     dq = (dq_t * (mine_factor * SCALE)).T
     dq_ref[...] = dq[0:half, :]
     dq_sibling_ref[...] = dq[half:rows, :].astype(BF16)
@@ -230,9 +222,10 @@
         copy.wait()
 
 
-def projection_kernel(held_ref, att_ref, delta_ref, near_ref, far_ref):
+def projection_kernel(place_ref, weight_ref, att_ref, delta_ref, *part_refs):
     slots = att_ref.shape[0]
-    half, _, width = near_ref.shape
+    pair, _, width = part_refs[0].shape
+    parts = pair * len(part_refs)
     rows = delta_ref.shape[1]
     delta = delta_ref[...]
     row_sum = delta[:, 0:slots]
@@ -241,10 +234,11 @@
     extra = jnp.concatenate([row_sum, jnp.zeros((8, width - slots), F32)], axis=1)
     extra = jnp.concatenate([extra, extra], axis=0).astype(BF16)
     att = att_ref[...]
-    for step in range(held_ref.shape[0]):
-        part_ref, at = (near_ref, step) if step < half else (far_ref, step - half)
-        part_ref[at, 0:slots, :] = matmul(att, held_ref[step], ((1,), (0,))).astype(BF16)
-        part_ref[at, slots : slots + 16, :] = extra
+    for at in range(parts):
+        columns = column_block(place_ref, at, parts, width)
+        part_ref = part_refs[at // pair]
+        part_ref[at % pair, 0:slots, :] = matmul(att, weight_ref[:, columns], ((1,), (0,))).astype(BF16)
+        part_ref[at % pair, slots : slots + 16, :] = extra
 
 
 def added_up(stack_ref):
@@ -252,10 +246,6 @@
     for step in range(1, stack_ref.shape[0]):
         total = total + stack_ref[step].astype(F32)
     return total
-
-
-def sum_kernel(stack_ref, out_ref):
-    out_ref[...] = added_up(stack_ref).astype(BF16)
 
 
 def update_kernel(count_ref, own_ref, landed_ref, logit_ref, index_ref, hidden_ref, update_ref, after_ref, grad_ref):
@@ -288,20 +278,13 @@
     dv_ref[...] = total[slots : 2 * slots, :].astype(BF16)
 
 
-def doubling_steps(count):
-    steps = []
-    step = count // 2
-    while step:
-        steps.append(step)
-        step //= 2
-    return steps
-
-
-def doubling_order(count):
-    order = [0]
-    for step in doubling_steps(count):
-        order = order + [place + step for place in order]
-    return order
+def tp_shifts(parts):
+    half = parts // 2
+    return [shift if 2 * shift <= half else shift - half for shift in range(1, half)]
+
+
+def tp_order(parts):
+    return [shift + step for shift in [0] + tp_shifts(parts) for step in (0, parts // 2)]
 
 
 def on_device(
@@ -321,15 +304,11 @@
     slots, width = queries.shape
     heads = width // HD
     rows = nc * heads * slots
-    keys = ny * slots
-
-    def at(y, x, c):
-        return (y * nx + x) * nc + c
-
-    y_groups = [[at(y, x, c) for y in range(ny)] for x in range(nx) for c in range(nc)]
-    x_groups = [[at(y, x, c) for x in range(nx)] for y in range(ny) for c in range(nc)]
-
-    def exchange(array, groups):
+    blocks = ny * nx
+    chunk = min(8, blocks)
+
+    def exchange(array):
+        groups = [[chip * nc + core for chip in range(blocks)] for core in range(nc)]
         return lax.all_to_all(array, "ctx", 0, 0, axis_index_groups=groups, tiled=True)
 
     def to_sibling(array):
@@ -358,99 +337,73 @@
         payload_kernel,
         [
             jax.ShapeDtypeStruct((2 * slots, HD), BF16),
-            jax.ShapeDtypeStruct((ny, 2 * slots, HD), BF16),
+            jax.ShapeDtypeStruct((blocks, 2 * slots, HD), BF16),
             jax.ShapeDtypeStruct((slots, HD), F32),
             jax.ShapeDtypeStruct((slots, HD), F32),
         ],
         [SMEM] + [VMEM] * 3,
+        [pltpu.VMEM((chunk, 2 * slots, HD), BF16), pltpu.SemaphoreType.DMA((blocks // chunk,))],
+        out_specs=[VMEM, HBM, VMEM, VMEM],
     )(
         chosen_count,
         jnp.concatenate([key_vectors, value_vectors], axis=0),
         (my_shard * TOK_DEV + chosen_index).astype(F32)[None, :],
         frequency,
     )
-    column = exchange(payloads, y_groups)
+    pieces = exchange(payloads)
 
     own_queries = call(
         query_kernel, jax.ShapeDtypeStruct((slots, width), BF16), [VMEM] * 3
     )(queries, cos_full, sin_signed)
     sibling_queries = to_sibling(own_queries)
-    column, sibling_queries = lax.optimization_barrier((column, sibling_queries))
-    columns = call(
-        copies_kernel,
-        jax.ShapeDtypeStruct((nx,) + column.shape, BF16),
-        [VMEM],
-        [pltpu.SemaphoreType.DMA((nx,))],
-        out_specs=HBM,
-    )(column)
-    pieces = exchange(columns, x_groups)
-
-    held = call(
-        weight_kernel,
-        jax.ShapeDtypeStruct((tp_count, width, width), BF16),
-        [SMEM, HBM],
-        [pltpu.SemaphoreType.DMA((tp_count,))],
-    )(place, out_weight)
-
-    cot = out_cotangent[None]
-    for step in doubling_steps(tp_count):
-        if step == 1:
-            cot, held = lax.optimization_barrier((cot, held))
-        cot = jnp.concatenate([cot, tp_send(cot, step)], axis=0)
-
+    pair = jnp.concatenate([out_cotangent[None], tp_send(out_cotangent[None], tp_count // 2)], axis=0)
+    cot = jnp.concatenate([pair] + [tp_send(pair, shift) for shift in tp_shifts(tp_count)], axis=0)
+
+    grad_attention = call(
+        cotangent_kernel, jax.ShapeDtypeStruct((slots, width), BF16), [SMEM] * 2 + [VMEM] * 3
+    )(place, chosen_count, out_weight, logit_row, cot)
+
+    scored = (blocks // chunk, chunk * slots, rows)
     part, weights = call(
-        functools.partial(forward_kernel, dims),
+        forward_kernel,
         [
-            jax.ShapeDtypeStruct((HD + 8, rows), F32),
-            jax.ShapeDtypeStruct((nx, keys, rows), BF16),
+            jax.ShapeDtypeStruct((HD + 8 + slots, rows), F32),
+            jax.ShapeDtypeStruct(scored, BF16),
         ],
-        [SMEM] + [VMEM] * 5,
-        [pltpu.VMEM((nx, keys, rows), F32)],
-    )(place, index_row, own_queries, sibling_queries, payload, pieces)
-    grad_attention, bundle = call(
-        cotangent_kernel,
-        [
-            jax.ShapeDtypeStruct((slots, width), BF16),
-            jax.ShapeDtypeStruct((HD + 8 + slots, rows), F32),
-        ],
-        [SMEM] + [VMEM] * 4,
-    )(chosen_count, held, logit_row, cot, part)
-    sibling_bundle = to_sibling(bundle)
+        [SMEM] + [VMEM] * 6,
+        [pltpu.VMEM(scored, F32)],
+    )(place, index_row, own_queries, sibling_queries, grad_attention, payload, pieces)
+    sibling_part = to_sibling(part)
     attention, delta, dq_own, dq_sibling, outs = call(
-        functools.partial(backward_kernel, dims),
+        backward_kernel,
         [
             jax.ShapeDtypeStruct((slots, width), BF16),
             jax.ShapeDtypeStruct((8, rows // 2), F32),
             jax.ShapeDtypeStruct((rows // 2, HD), F32),
             jax.ShapeDtypeStruct((rows // 2, HD), BF16),
-            jax.ShapeDtypeStruct((nx, ny, 2 * slots, HD), BF16),
+            jax.ShapeDtypeStruct((blocks, 2 * slots, HD), BF16),
         ],
         [VMEM] * 7,
-        [pltpu.VMEM((nx, ny, 2 * slots, HD), BF16), pltpu.SemaphoreType.DMA((nx,))],
+        [pltpu.VMEM((blocks, 2 * slots, HD), BF16), pltpu.SemaphoreType.DMA((blocks // chunk,))],
         out_specs=[VMEM] * 4 + [HBM],
-    )(part, sibling_bundle, own_queries, sibling_queries, grad_attention, weights, pieces)
-
-    crossed = exchange(outs, x_groups)
-    near, far = call(
+    )(part, sibling_part, own_queries, sibling_queries, grad_attention, weights, pieces)
+    landed = exchange(outs)
+
+    shares = call(
         projection_kernel,
-        [jax.ShapeDtypeStruct((tp_count // 2, slots + 16, width), BF16)] * 2,
-        [VMEM] * 3,
-    )(held, attention, delta)
+        [jax.ShapeDtypeStruct((2, slots + 16, width), BF16)] * (tp_count // 2),
+        [SMEM] + [VMEM] * 3,
+    )(place, out_weight, attention, delta)
     dq_arrived = to_sibling(dq_sibling)
     grad_queries = call(
         query_grad_kernel, jax.ShapeDtypeStruct((slots, width), BF16), [VMEM] * 4
     )(cos_full, sin_signed, dq_own, dq_arrived)
-
-    for step in reversed(doubling_steps(tp_count)):
-        arrived = tp_send(far, -step)
-        if step == 1:
-            arrived, grad_queries = lax.optimization_barrier((arrived, grad_queries))
-        if near.shape[0] > 1:
-            count = near.shape[0] // 2
-            far = summed(near[count:], arrived[count:])
-            near = summed(near[:count], arrived[:count])
-    stacked = call(sum_kernel, jax.ShapeDtypeStruct((ny, 2 * slots, HD), BF16), [VMEM])(crossed)
-    landed = exchange(stacked, y_groups)
+    arrived = [tp_send(share, -shift) for share, shift in zip(shares[1:], tp_shifts(tp_count))]
+    arrived, grad_queries = lax.optimization_barrier((arrived, grad_queries))
+    shares = functools.reduce(jnp.add, [part.astype(F32) for part in [shares[0]] + arrived]).astype(BF16)
+    near = shares[:1]
+    arrived = tp_send(shares[1:], -(tp_count // 2))
+
     grad_keys, grad_values = call(
         finish_kernel, [jax.ShapeDtypeStruct((slots, HD), BF16)] * 2, [VMEM] * 3
     )(cos_full, sin_signed, landed)

time: 107 us -> 104 us (0.972)
  local copies, waits for them, and re-layouts: 9.36 us -> 6.77 us
  Pallas kernels: 14.3 us -> 12.6 us
    unnamed x18, local copies, waits for them, and re-layouts: 9.36 us -> 6.75 us
    pallas_call x7 -> x4, Pallas kernels: 10.7 us -> 8.59 us  [the longest x1 2.87 us: on_device(): call(backward_kernel, [jax.ShapeDtypeStruct((slots, width), BF16), jax.Sh...]
    ppermute x6 -> x8, starting transfers between devices: 32.5 us -> 33.9 us  [tp_send(): return lax.ppermute(array, ('ctx', 'tp'), pairs)]
    all_to_all x4 -> x2, starting transfers between devices: 21.2 us -> 20.2 us  [exchange(): lax.all_to_all(array, 'ctx', 0, 0, axis_index_groups=groups, tiled=True)]
    ppermute x6 -> x8, waiting for transfers between devices: 16.3 us -> 16.7 us  [tp_send(): return lax.ppermute(array, ('ctx', 'tp'), pairs)]
  transfers between devices with their start and end apart: 13 -> 13, of which waited for: 7 -> 6; matrix products, arithmetic and copies ran while one was open for 0% -> 2% of each run, Pallas kernels for 6% -> 5%
where the time goes in v3:
time: 104 us; the launch traced here: 103 us
  starting transfers between devices  59.8 us (58%)
  waiting for transfers between devices  19.7 us (19%)
  Pallas kernels  12.6 us (12%)
  local copies, waits for them, and re-layouts  6.77 us (7%)
  other arithmetic  2.5 us (2%)
  between operations  1.57 us (2%)
    ppermute x8, starting transfers between devices, tp_send(): return lax.ppermute(array, ('ctx', 'tp'), pairs)  33.9 us
    all_to_all x2, starting transfers between devices, exchange(): lax.all_to_all(array, 'ctx', 0, 0, axis_index_groups=groups, tiled=True)  20.2 us
    ppermute x8, waiting for transfers between devices, tp_send(): return lax.ppermute(array, ('ctx', 'tp'), pairs)  16.7 us
    unnamed x18, local copies, waits for them, and re-layouts  6.75 us
    ppermute x3, starting transfers between devices, to_sibling(): return lax.ppermute(array, 'ctx', [(i, i ^ 1) for i in range(ny * nx * nc)])  5.76 us
    ppermute x3, waiting for transfers between devices, to_sibling(): return lax.ppermute(array, 'ctx', [(i, i ^ 1) for i in range(ny * nx * nc)])  2.93 us
    pallas_call x1, Pallas kernels, on_device(): call(backward_kernel, [jax.ShapeDtypeStruct((slots, width), BF16), jax.Sh...  2.87 us
    pallas_call x1, Pallas kernels, on_device(): call(forward_kernel, [jax.ShapeDtypeStruct((HD + 8 + slots, rows), F32),...  2.38 us
  transfers between devices with their start and end apart: 13, of which 6 were waited for; matrix products, arithmetic and copies ran while one was open for 2% of the time, Pallas kernels for 5%

profile of v3, /device:TPU:2, one launch (start us, length us, event | category | flops | bytes accessed | tf_op | source)
XLA Modules:
  0.0 103.0 jit_solution(13897031442579348606)
XLA Ops:
  2.8 1.3 %shard_map.136 = (bf16[128,128]{1,0:T(8,128)(2,1)S(1)}, bf16[32,128,128]{2,1,0:T(8,128)(2,1)}, f32[64,128]{1,0:T(8,128)S(1)}, f32[64,128]{1,0:T(8,128)S(1)}) custom-call(s32[1]{0:T(128)S(6)} %copy.19.count_ref, bf16[128,128]{1,0:T(8,128)(2,1)S(1)} %pad_maximum_fusion.1.pair_ref, f32[1,64]{1,0:T(1,128)S(1)} %convert_bitcast_fusion.position_ref, ...), custom_call_target="tpu_custom_call" | custom-call | tf_op jit(solution)/shard_map/pallas_call | solution.py:336
  4.1 10.3 %all-to-all-start = ((bf16[32,128,128]{2,1,0:T(8,128)(2,1)}), bf16[32,128,128]{2,1,0:T(8,128)(2,1)S(1)}, u32[]{:S(2)}, u32[]{:S(2)}) async-start(bf16[32,128,128]{2,1,0:T(8,128)(2,1)} %get-tuple-element.33), calls=%async_computation | async-start | bytes 2097152 | tf_op jit(solution)/shard_map/all_to_all | solution.py:312
  14.3 10.9 %collective-permute-start.1 = (bf16[1,64,512]{2,1,0:T(8,128)(2,1)}, bf16[1,64,512]{2,1,0:T(8,128)(2,1)S(1)}, u32[]{:S(2)}, u32[]{:S(2)}) collective-permute-start(bf16[1,64,512]{2,1,0:T(8,128)(2,1)} %bitcast.15), channel_id=1, source_target_pairs={{0,4},{1,5},{2,6},{3,7},{4,0},{5,1},{6,2},{7,3},{8,12},{9,13},{10,... | collective-permute-start | bytes 196616 | tf_op jit(solution)/shard_map/ppermute | solution.py:323
  26.2 1.9 %collective-permute-start = (bf16[64,512]{1,0:T(8,128)(2,1)S(1)}, bf16[64,512]{1,0:T(8,128)(2,1)S(1)}, u32[]{:S(2)}, u32[]{:S(2)}) collective-permute-start(bf16[64,512]{1,0:T(8,128)(2,1)S(1)} %shard_map.137.own_ref), channel_id=1, source_target_pairs={{0,8},{8,0},{16,24},{24,16},{32,40},{40,32},{48,56},{56,48},{64,72... | collective-permute-start | bytes 196616 | tf_op jit(solution)/shard_map/ppermute | solution.py:315
  29.8 3.4 %collective-permute-start.2 = (bf16[2,64,512]{2,1,0:T(8,128)(2,1)S(1)}, bf16[2,64,512]{2,1,0:T(8,128)(2,1)S(1)}, u32[]{:S(2)}, u32[]{:S(2)}) collective-permute-start(bf16[2,64,512]{2,1,0:T(8,128)(2,1)S(1)} %pad_maximum_fusion), channel_id=1, source_target_pairs={{0,1},{1,2},{2,3},{3,4},{4,5},{5,6},{6,7},{7,0},{8,15},{9,8},{10,9... | collective-permute-start | bytes 393224 | tf_op jit(solution)/shard_map/ppermute | solution.py:323
  33.3 5.1 %collective-permute-start.4 = (bf16[2,64,512]{2,1,0:T(8,128)(2,1)S(1)}, bf16[2,64,512]{2,1,0:T(8,128)(2,1)S(1)}, u32[]{:S(2)}, u32[]{:S(2)}) collective-permute-start(bf16[2,64,512]{2,1,0:T(8,128)(2,1)S(1)} %pad_maximum_fusion), channel_id=1, source_target_pairs={{0,7},{1,0},{2,1},{3,2},{4,3},{5,4},{6,5},{7,6},{8,9},{9,10},{10,1... | collective-permute-start | bytes 393224 | tf_op jit(solution)/shard_map/ppermute | solution.py:323
  38.4 1.9 %collective-permute-start.3 = (bf16[2,64,512]{2,1,0:T(8,128)(2,1)S(1)}, bf16[2,64,512]{2,1,0:T(8,128)(2,1)S(1)}, u32[]{:S(2)}, u32[]{:S(2)}) collective-permute-start(bf16[2,64,512]{2,1,0:T(8,128)(2,1)S(1)} %pad_maximum_fusion), channel_id=1, source_target_pairs={{0,2},{1,3},{2,4},{3,5},{4,6},{5,7},{6,0},{7,1},{8,14},{9,15},{10,... | collective-permute-start | bytes 393224 | tf_op jit(solution)/shard_map/ppermute | solution.py:323
  40.4 7.3 %collective-permute-done.3 = bf16[2,64,512]{2,1,0:T(8,128)(2,1)S(1)} collective-permute-done((bf16[2,64,512]{2,1,0:T(8,128)(2,1)S(1)}, bf16[2,64,512]{2,1,0:T(8,128)(2,1)S(1)}, u32[]{:S(2)}, u32[]{:S(2)}) %collective-permute-start.3) | collective-permute-done | bytes 131104 | tf_op jit(solution)/shard_map/ppermute | solution.py:323
  47.7 2.2 %copy-done = bf16[512,4096]{1,0:T(8,128)(2,1)S(1)} copy-done((bf16[512,4096]{1,0:T(8,128)(2,1)S(1)}, bf16[512,4096]{1,0:T(8,128)(2,1)}, u32[]{:S(2)}) %copy-start) | copy-done | bytes 4194328
  50.6 1.9 %shard_map.138.grad_ref = bf16[64,512]{1,0:T(8,128)(2,1)S(1)} custom-call(s32[2]{0:T(128)S(1)} %pad_add_fusion.place_ref, s32[1]{0:T(128)S(6)} %copy.19.count_ref, bf16[512,4096]{1,0:T(8,128)(2,1)S(1)} %copy-done, f32[1,64]{1,0:T(1,128)S(1)} %bitcast.13, bf16[8,64,512]{2,1,0:T(8,128)(2,1)S(1)} %constant_dynamic-update-slice_fusion.cot_ref), custom_call_target="tpu_custom_call" | custom-call | tf_op jit(solution)/shard_map/pallas_call | solution.py:362
  52.5 2.4 %shard_map.139 = (f32[200,512]{1,0:T(8,128)S(1)}, bf16[4,512,512]{2,1,0:T(8,128)(2,1)S(1)}) custom-call(s32[2]{0:T(128)S(1)} %pad_add_fusion.place_ref, s32[1,64]{1,0:T(1,128)S(1)} %bitcast.11, bf16[64,512]{1,0:T(8,128)(2,1)S(1)} %shard_map.137.own_ref, bf16[64,512]{1,0:T(8,128)(2,1)S(1)} %collective-permute-done.sibling_ref, ...), custom_call_target="tpu_custom_call" | custom-call | tf_op jit(solution)/shard_map/pallas_call | solution.py:367
  54.9 1.9 %collective-permute-start.5 = (f32[200,512]{1,0:T(8,128)S(1)}, f32[200,512]{1,0:T(8,128)S(1)}, u32[]{:S(2)}, u32[]{:S(2)}) collective-permute-start(f32[200,512]{1,0:T(8,128)S(1)} %get-tuple-element.34.own_part), channel_id=1, source_target_pairs={{0,8},{8,0},{16,24},{24,16},{32,40},{40,32},{48,56},{56,48},{64,72... | collective-permute-start | bytes 1228808 | tf_op jit(solution)/shard_map/ppermute | solution.py:315
  56.8 1.7 %collective-permute-done.5.sibling_part = f32[200,512]{1,0:T(8,128)S(1)} collective-permute-done((f32[200,512]{1,0:T(8,128)S(1)}, f32[200,512]{1,0:T(8,128)S(1)}, u32[]{:S(2)}, u32[]{:S(2)}) %collective-permute-start.5) | collective-permute-done | bytes 409632 | tf_op jit(solution)/shard_map/ppermute | solution.py:315
  58.6 2.9 %shard_map.140 = (bf16[64,512]{1,0:T(8,128)(2,1)S(1)}, f32[8,256]{1,0:T(8,128)S(1)}, f32[256,128]{1,0:T(8,128)S(1)}, bf16[256,128]{1,0:T(8,128)(2,1)S(1)}, bf16[32,128,128]{2,1,0:T(8,128)(2,1)}) custom-call(f32[200,512]{1,0:T(8,128)S(1)} %get-tuple-element.34.own_part, f32[200,512]{1,0:T(8,128)S(1)} %collective-permute-done.5.sibling_part, ...), custom_call_target="tpu_custom_call" | custom-call | tf_op jit(solution)/shard_map/pallas_call | solution.py:377
  61.5 9.9 %all-to-all-start.1 = ((bf16[32,128,128]{2,1,0:T(8,128)(2,1)}), bf16[32,128,128]{2,1,0:T(8,128)(2,1)S(1)}, u32[]{:S(2)}, u32[]{:S(2)}) async-start(bf16[32,128,128]{2,1,0:T(8,128)(2,1)} %get-tuple-element.49), calls=%async_computation.1 | async-start | bytes 2097152 | tf_op jit(solution)/shard_map/all_to_all | solution.py:312
  71.4 2.2 %copy-done.1 = bf16[512,4096]{1,0:T(8,128)(2,1)S(1)} copy-done((bf16[512,4096]{1,0:T(8,128)(2,1)S(1)}, bf16[512,4096]{1,0:T(8,128)(2,1)}, u32[]{:S(2)}) %copy-start.1) | copy-done | bytes 4194328
  73.6 1.4 %shard_map.141 = (bf16[2,80,512]{2,1,0:T(8,128)(2,1)S(1)}, bf16[2,80,512]{2,1,0:T(8,128)(2,1)S(1)}, bf16[2,80,512]{2,1,0:T(8,128)(2,1)S(1)}, bf16[2,80,512]{2,1,0:T(8,128)(2,1)S(1)}) custom-call(s32[2]{0:T(128)S(1)} %pad_add_fusion.place_ref, bf16[512,4096]{1,0:T(8,128)(2,1)S(1)} %copy-done.1, bf16[64,512]{1,0:T(8,128)(2,1)S(1)} %get-tuple-element.36.att_ref, ...), custom_call_target="tpu_custom_call" | custom-call | tf_op jit(solution)/shard_map/pallas_call | solution.py:392
  75.0 3.8 %collective-permute-start.6 = (bf16[2,80,512]{2,1,0:T(8,128)(2,1)S(1)}, bf16[2,80,512]{2,1,0:T(8,128)(2,1)S(1)}, u32[]{:S(2)}, u32[]{:S(2)}) collective-permute-start(bf16[2,80,512]{2,1,0:T(8,128)(2,1)S(1)} %get-tuple-element.39), channel_id=1, source_target_pairs={{0,7},{1,0},{2,1},{3,2},{4,3},{5,4},{6,5},{7,6},{8,9},{9,10},{10,1... | collective-permute-start | bytes 491528 | tf_op jit(solution)/shard_map/ppermute | solution.py:323
  78.8 3.0 %collective-permute-start.7 = (bf16[2,80,512]{2,1,0:T(8,128)(2,1)S(1)}, bf16[2,80,512]{2,1,0:T(8,128)(2,1)S(1)}, u32[]{:S(2)}, u32[]{:S(2)}) collective-permute-start(bf16[2,80,512]{2,1,0:T(8,128)(2,1)S(1)} %get-tuple-element.40), channel_id=1, source_target_pairs={{0,6},{1,7},{2,0},{3,1},{4,2},{5,3},{6,4},{7,5},{8,10},{9,11},{10,... | collective-permute-start | bytes 491528 | tf_op jit(solution)/shard_map/ppermute | solution.py:323
  81.8 2.3 %collective-permute-start.8 = (bf16[2,80,512]{2,1,0:T(8,128)(2,1)S(1)}, bf16[2,80,512]{2,1,0:T(8,128)(2,1)S(1)}, u32[]{:S(2)}, u32[]{:S(2)}) collective-permute-start(bf16[2,80,512]{2,1,0:T(8,128)(2,1)S(1)} %get-tuple-element.41), channel_id=1, source_target_pairs={{0,1},{1,2},{2,3},{3,4},{4,5},{5,6},{6,7},{7,0},{8,15},{9,8},{10,9... | collective-permute-start | bytes 491528 | tf_op jit(solution)/shard_map/ppermute | solution.py:323
  84.1 1.9 %collective-permute-start.9 = (bf16[256,128]{1,0:T(8,128)(2,1)S(1)}, bf16[256,128]{1,0:T(8,128)(2,1)S(1)}, u32[]{:S(2)}, u32[]{:S(2)}) collective-permute-start(bf16[256,128]{1,0:T(8,128)(2,1)S(1)} %get-tuple-element.43), channel_id=1, source_target_pairs={{0,8},{8,0},{16,24},{24,16},{32,40},{40,32},{48,56},{56,48},{64,72... | collective-permute-start | bytes 196616 | tf_op jit(solution)/shard_map/ppermute | solution.py:315
  89.0 1.2 %collective-permute-done.8 = bf16[2,80,512]{2,1,0:T(8,128)(2,1)S(1)} collective-permute-done((bf16[2,80,512]{2,1,0:T(8,128)(2,1)S(1)}, bf16[2,80,512]{2,1,0:T(8,128)(2,1)S(1)}, u32[]{:S(2)}, u32[]{:S(2)}) %collective-permute-start.8) | collective-permute-done | bytes 163872 | tf_op jit(solution)/shard_map/ppermute | solution.py:323
  90.4 3.4 %collective-permute-start.10 = (bf16[1,80,512]{2,1,0:T(8,128)(2,1)S(1)}, bf16[1,80,512]{2,1,0:T(8,128)(2,1)S(1)}, u32[]{:S(2)}, u32[]{:S(2)}) collective-permute-start(bf16[1,80,512]{2,1,0:T(8,128)(2,1)S(1)} %get-tuple-element.54), channel_id=1, source_target_pairs={{0,4},{1,5},{2,6},{3,7},{4,0},{5,1},{6,2},{7,3},{8,12},{9,13},{10,... | collective-permute-start | bytes 245768 | tf_op jit(solution)/shard_map/ppermute | solution.py:323
  93.8 7.2 %collective-permute-done.10.landed_ref = bf16[1,80,512]{2,1,0:T(8,128)(2,1)S(1)} collective-permute-done((bf16[1,80,512]{2,1,0:T(8,128)(2,1)S(1)}, bf16[1,80,512]{2,1,0:T(8,128)(2,1)S(1)}, u32[]{:S(2)}, u32[]{:S(2)}) %collective-permute-start.10) | collective-permute-done | bytes 81952 | tf_op jit(solution)/shard_map/ppermute | solution.py:323
  (38 shorter events, 9.9 us)
Async XLA Ops:
  4.0 48.5 %copy-start.4 = (s32[64]{0:T(128)S(1)}, s32[64]{0:T(128)}, u32[]{:S(2)}) copy-start(s32[64]{0:T(128)} %param.14) | copy-start | bytes 772
  4.1 48.5 %all-to-all-start = ((bf16[32,128,128]{2,1,0:T(8,128)(2,1)}), bf16[32,128,128]{2,1,0:T(8,128)(2,1)S(1)}, u32[]{:S(2)}, u32[]{:S(2)}) async-start(bf16[32,128,128]{2,1,0:T(8,128)(2,1)} %get-tuple-element.33), calls=%async_computation | async-start | bytes 2097152 | tf_op jit(solution)/shard_map/all_to_all | solution.py:312
  14.3 14.6 %collective-permute-start.1 = (bf16[1,64,512]{2,1,0:T(8,128)(2,1)}, bf16[1,64,512]{2,1,0:T(8,128)(2,1)S(1)}, u32[]{:S(2)}, u32[]{:S(2)}) collective-permute-start(bf16[1,64,512]{2,1,0:T(8,128)(2,1)} %bitcast.15), channel_id=1, source_target_pairs={{0,4},{1,5},{2,6},{3,7},{4,0},{5,1},{6,2},{7,3},{8,12},{9,13},{10,... | collective-permute-start | bytes 196616 | tf_op jit(solution)/shard_map/ppermute | solution.py:323
  25.2 0.8 copy-start.3
  26.2 26.3 %collective-permute-start = (bf16[64,512]{1,0:T(8,128)(2,1)S(1)}, bf16[64,512]{1,0:T(8,128)(2,1)S(1)}, u32[]{:S(2)}, u32[]{:S(2)}) collective-permute-start(bf16[64,512]{1,0:T(8,128)(2,1)S(1)} %shard_map.137.own_ref), channel_id=1, source_target_pairs={{0,8},{8,0},{16,24},{24,16},{32,40},{40,32},{48,56},{56,48},{64,72... | collective-permute-start | bytes 196616 | tf_op jit(solution)/shard_map/ppermute | solution.py:315
  29.8 10.5 %collective-permute-start.2 = (bf16[2,64,512]{2,1,0:T(8,128)(2,1)S(1)}, bf16[2,64,512]{2,1,0:T(8,128)(2,1)S(1)}, u32[]{:S(2)}, u32[]{:S(2)}) collective-permute-start(bf16[2,64,512]{2,1,0:T(8,128)(2,1)S(1)} %pad_maximum_fusion), channel_id=1, source_target_pairs={{0,1},{1,2},{2,3},{3,4},{4,5},{5,6},{6,7},{7,0},{8,15},{9,8},{10,9... | collective-permute-start | bytes 393224 | tf_op jit(solution)/shard_map/ppermute | solution.py:323
  33.3 14.4 %collective-permute-start.4 = (bf16[2,64,512]{2,1,0:T(8,128)(2,1)S(1)}, bf16[2,64,512]{2,1,0:T(8,128)(2,1)S(1)}, u32[]{:S(2)}, u32[]{:S(2)}) collective-permute-start(bf16[2,64,512]{2,1,0:T(8,128)(2,1)S(1)} %pad_maximum_fusion), channel_id=1, source_target_pairs={{0,7},{1,0},{2,1},{3,2},{4,3},{5,4},{6,5},{7,6},{8,9},{9,10},{10,1... | collective-permute-start | bytes 393224 | tf_op jit(solution)/shard_map/ppermute | solution.py:323
  38.4 9.3 %collective-permute-start.3 = (bf16[2,64,512]{2,1,0:T(8,128)(2,1)S(1)}, bf16[2,64,512]{2,1,0:T(8,128)(2,1)S(1)}, u32[]{:S(2)}, u32[]{:S(2)}) collective-permute-start(bf16[2,64,512]{2,1,0:T(8,128)(2,1)S(1)} %pad_maximum_fusion), channel_id=1, source_target_pairs={{0,2},{1,3},{2,4},{3,5},{4,6},{5,7},{6,0},{7,1},{8,14},{9,15},{10,... | collective-permute-start | bytes 393224 | tf_op jit(solution)/shard_map/ppermute | solution.py:323
  47.7 2.2 %copy-start = (bf16[512,4096]{1,0:T(8,128)(2,1)S(1)}, bf16[512,4096]{1,0:T(8,128)(2,1)}, u32[]{:S(2)}) copy-start(bf16[512,4096]{1,0:T(8,128)(2,1)} %weight_ref.3) | copy-start | bytes 12582916
  49.9 0.7 copy-start.5
  54.9 3.6 %collective-permute-start.5 = (f32[200,512]{1,0:T(8,128)S(1)}, f32[200,512]{1,0:T(8,128)S(1)}, u32[]{:S(2)}, u32[]{:S(2)}) collective-permute-start(f32[200,512]{1,0:T(8,128)S(1)} %get-tuple-element.34.own_part), channel_id=1, source_target_pairs={{0,8},{8,0},{16,24},{24,16},{32,40},{40,32},{48,56},{56,48},{64,72... | collective-permute-start | bytes 1228808 | tf_op jit(solution)/shard_map/ppermute | solution.py:315
  61.4 39.6 %copy-start.2 = (bf16[512,512]{1,0:T(8,128)(2,1)S(1)}, bf16[512,512]{1,0:T(8,128)(2,1)}, u32[]{:S(2)}) copy-start(bf16[512,512]{1,0:T(8,128)(2,1)} %hidden_ref.1) | copy-start | bytes 1572868
  61.4 39.6 %copy-start.6 = (f32[64]{0:T(128)S(1)}, f32[64]{0:T(128)}, u32[]{:S(2)}) copy-start(f32[64]{0:T(128)} %param.13) | copy-start | bytes 772
  61.5 40.7 %all-to-all-start.1 = ((bf16[32,128,128]{2,1,0:T(8,128)(2,1)}), bf16[32,128,128]{2,1,0:T(8,128)(2,1)S(1)}, u32[]{:S(2)}, u32[]{:S(2)}) async-start(bf16[32,128,128]{2,1,0:T(8,128)(2,1)} %get-tuple-element.49), calls=%async_computation.1 | async-start | bytes 2097152 | tf_op jit(solution)/shard_map/all_to_all | solution.py:312
  71.4 2.2 %copy-start.1 = (bf16[512,4096]{1,0:T(8,128)(2,1)S(1)}, bf16[512,4096]{1,0:T(8,128)(2,1)}, u32[]{:S(2)}) copy-start(bf16[512,4096]{1,0:T(8,128)(2,1)} %weight_ref.3) | copy-start | bytes 12582916
  75.0 13.0 %collective-permute-start.6 = (bf16[2,80,512]{2,1,0:T(8,128)(2,1)S(1)}, bf16[2,80,512]{2,1,0:T(8,128)(2,1)S(1)}, u32[]{:S(2)}, u32[]{:S(2)}) collective-permute-start(bf16[2,80,512]{2,1,0:T(8,128)(2,1)S(1)} %get-tuple-element.39), channel_id=1, source_target_pairs={{0,7},{1,0},{2,1},{3,2},{4,3},{5,4},{6,5},{7,6},{8,9},{9,10},{10,1... | collective-permute-start | bytes 491528 | tf_op jit(solution)/shard_map/ppermute | solution.py:323
  78.8 10.2 %collective-permute-start.7 = (bf16[2,80,512]{2,1,0:T(8,128)(2,1)S(1)}, bf16[2,80,512]{2,1,0:T(8,128)(2,1)S(1)}, u32[]{:S(2)}, u32[]{:S(2)}) collective-permute-start(bf16[2,80,512]{2,1,0:T(8,128)(2,1)S(1)} %get-tuple-element.40), channel_id=1, source_target_pairs={{0,6},{1,7},{2,0},{3,1},{4,2},{5,3},{6,4},{7,5},{8,10},{9,11},{10,... | collective-permute-start | bytes 491528 | tf_op jit(solution)/shard_map/ppermute | solution.py:323
  81.8 8.4 %collective-permute-start.8 = (bf16[2,80,512]{2,1,0:T(8,128)(2,1)S(1)}, bf16[2,80,512]{2,1,0:T(8,128)(2,1)S(1)}, u32[]{:S(2)}, u32[]{:S(2)}) collective-permute-start(bf16[2,80,512]{2,1,0:T(8,128)(2,1)S(1)} %get-tuple-element.41), channel_id=1, source_target_pairs={{0,1},{1,2},{2,3},{3,4},{4,5},{5,6},{6,7},{7,0},{8,15},{9,8},{10,9... | collective-permute-start | bytes 491528 | tf_op jit(solution)/shard_map/ppermute | solution.py:323
  84.1 3.1 %collective-permute-start.9 = (bf16[256,128]{1,0:T(8,128)(2,1)S(1)}, bf16[256,128]{1,0:T(8,128)(2,1)S(1)}, u32[]{:S(2)}, u32[]{:S(2)}) collective-permute-start(bf16[256,128]{1,0:T(8,128)(2,1)S(1)} %get-tuple-element.43), channel_id=1, source_target_pairs={{0,8},{8,0},{16,24},{24,16},{32,40},{40,32},{48,56},{56,48},{64,72... | collective-permute-start | bytes 196616 | tf_op jit(solution)/shard_map/ppermute | solution.py:315
  90.4 10.6 %collective-permute-start.10 = (bf16[1,80,512]{2,1,0:T(8,128)(2,1)S(1)}, bf16[1,80,512]{2,1,0:T(8,128)(2,1)S(1)}, u32[]{:S(2)}, u32[]{:S(2)}) collective-permute-start(bf16[1,80,512]{2,1,0:T(8,128)(2,1)S(1)} %get-tuple-element.54), channel_id=1, source_target_pairs={{0,4},{1,5},{2,6},{3,7},{4,0},{5,1},{6,2},{7,3},{8,12},{9,13},{10,... | collective-permute-start | bytes 245768 | tf_op jit(solution)/shard_map/ppermute | solution.py:323

commit v4 on v3

--- a/solution.py
+++ b/solution.py
@@ -87,29 +87,33 @@
         copy.wait()
 
 
-def column_block(place_ref, at, parts, width):
+def column_block(place_ref, shift, parts, width):
     way = 1 - 2 * lax.rem(place_ref[0], 2)
-    owner = lax.rem(place_ref[1] - tp_order(parts)[at] * way + 2 * parts, parts)
+    owner = lax.rem(place_ref[1] - shift * way + 2 * parts, parts)
     return pl.ds(pl.multiple_of(owner * width, width), width)
 
 
-def query_kernel(query_ref, cos_ref, sin_ref, out_ref):
+def query_kernel(count_ref, query_ref, cos_ref, sin_ref, logit_ref, cot_ref, out_ref, gate_ref, cot_out):
     cos_full, sin_signed = cos_ref[...], sin_ref[...]
     for h in range(query_ref.shape[1] // HD):
         part = query_ref[:, h * HD : (h + 1) * HD].astype(F32)
         out_ref[:, h * HD : (h + 1) * HD] = turn(part, cos_full, sin_signed).astype(BF16)
-
-
-def cotangent_kernel(place_ref, count_ref, weight_ref, logit_ref, cot_ref, grad_ref):
-    slots = grad_ref.shape[0]
+    slots = query_ref.shape[0]
     gate = jnp.where(live_row(count_ref, slots), 1.0 / (1.0 + jnp.exp(-logit_ref[...])), 0.0)
+    gate_ref[...] = jnp.broadcast_to(as_column(gate), gate_ref.shape)
+    cot_out[...] = cot_ref[...]
+
+
+def cotangent_kernel(place_ref, weight_ref, gate_ref, *refs):
+    pieces, grad_ref = refs[:-1], refs[-1]
+    parts = len(pieces)
+    width = grad_ref.shape[1]
     total = None
-    parts, _, width = cot_ref.shape
-    for step in range(parts):
-        columns = column_block(place_ref, step, parts, width)
-        part = matmul(cot_ref[step], weight_ref[:, columns], ((1,), (1,)))
+    for piece, shift in zip(pieces, [0] + direct_shifts(parts)):
+        columns = column_block(place_ref, shift, parts, width)
+        part = matmul(piece[...], weight_ref[:, columns], ((1,), (1,)))
         total = part if total is None else total + part
-    grad_ref[...] = (total * as_column(gate)).astype(BF16)
+    grad_ref[...] = (total * gate_ref[:, 0:1]).astype(BF16)
 
 
 def forward_kernel(place_ref, index_ref, own_ref, sibling_ref, grad_ref, pay_ref, piece_ref, part_ref, weight_ref, score_ref):
@@ -235,7 +239,7 @@
     extra = jnp.concatenate([extra, extra], axis=0).astype(BF16)
     att = att_ref[...]
     for at in range(parts):
-        columns = column_block(place_ref, at, parts, width)
+        columns = column_block(place_ref, tp_order(parts)[at], parts, width)
         part_ref = part_refs[at // pair]
         part_ref[at % pair, 0:slots, :] = matmul(att, weight_ref[:, columns], ((1,), (0,))).astype(BF16)
         part_ref[at % pair, slots : slots + 16, :] = extra
@@ -276,6 +280,13 @@
     total = added_up(landed_ref)
     dk_ref[...] = turn(total[0:slots, :], cos_ref[...], -sin_ref[...]).astype(BF16)
     dv_ref[...] = total[slots : 2 * slots, :].astype(BF16)
+
+
+def direct_shifts(parts):
+    shifts = []
+    for distance in range(parts // 2, 0, -1):
+        shifts += [distance] if 2 * distance == parts else [distance, -distance]
+    return shifts
 
 
 def tp_shifts(parts):
@@ -352,16 +363,23 @@
     )
     pieces = exchange(payloads)
 
-    own_queries = call(
-        query_kernel, jax.ShapeDtypeStruct((slots, width), BF16), [VMEM] * 3
-    )(queries, cos_full, sin_signed)
+    own_queries, gate, own_cot = call(
+        query_kernel,
+        [
+            jax.ShapeDtypeStruct((slots, width), BF16),
+            jax.ShapeDtypeStruct((slots, HD), F32),
+            jax.ShapeDtypeStruct((slots, width), BF16),
+        ],
+        [SMEM] + [VMEM] * 5,
+    )(chosen_count, queries, cos_full, sin_signed, logit_row, out_cotangent)
     sibling_queries = to_sibling(own_queries)
-    pair = jnp.concatenate([out_cotangent[None], tp_send(out_cotangent[None], tp_count // 2)], axis=0)
-    cot = jnp.concatenate([pair] + [tp_send(pair, shift) for shift in tp_shifts(tp_count)], axis=0)
-
+
+    cot = [own_cot] + [tp_send(out_cotangent, shift) for shift in direct_shifts(tp_count)]
     grad_attention = call(
-        cotangent_kernel, jax.ShapeDtypeStruct((slots, width), BF16), [SMEM] * 2 + [VMEM] * 3
-    )(place, chosen_count, out_weight, logit_row, cot)
+        cotangent_kernel,
+        jax.ShapeDtypeStruct((slots, width), BF16),
+        [SMEM] + [VMEM] * (2 + tp_count),
+    )(place, out_weight, gate, *cot)
 
     scored = (blocks // chunk, chunk * slots, rows)
     part, weights = call(
@@ -399,7 +417,6 @@
         query_grad_kernel, jax.ShapeDtypeStruct((slots, width), BF16), [VMEM] * 4
     )(cos_full, sin_signed, dq_own, dq_arrived)
     arrived = [tp_send(share, -shift) for share, shift in zip(shares[1:], tp_shifts(tp_count))]
-    arrived, grad_queries = lax.optimization_barrier((arrived, grad_queries))
     shares = functools.reduce(jnp.add, [part.astype(F32) for part in [shares[0]] + arrived]).astype(BF16)
     near = shares[:1]
     arrived = tp_send(shares[1:], -(tp_count // 2))

time: 104 us -> 110 us (1.058)
  the two profiles are of different devices: /device:TPU:2 before, /device:TPU:1 now
where the time goes in v4:
time: 110 us; the launch traced here: 109 us
  starting transfers between devices  78.3 us (71%)
  Pallas kernels  12.6 us (11%)
  waiting for transfers between devices  7.73 us (7%)
  local copies, waits for them, and re-layouts  6.73 us (6%)
  other arithmetic  1.65 us (2%)
  between operations  1.59 us (1%)
    ppermute x11, starting transfers between devices, tp_send(): return lax.ppermute(array, ('ctx', 'tp'), pairs)  47.1 us
    all_to_all x2, starting transfers between devices, exchange(): lax.all_to_all(array, 'ctx', 0, 0, axis_index_groups=groups, tiled=True)  20.1 us
    ppermute x3, starting transfers between devices, to_sibling(): return lax.ppermute(array, 'ctx', [(i, i ^ 1) for i in range(ny * nx * nc)])  11.1 us
    unnamed x16, local copies, waits for them, and re-layouts  6.71 us
    ppermute x11, waiting for transfers between devices, tp_send(): return lax.ppermute(array, ('ctx', 'tp'), pairs)  5.49 us
    pallas_call x1, Pallas kernels, on_device(): call(backward_kernel, [jax.ShapeDtypeStruct((slots, width), BF16), jax.Sh...  2.87 us
    pallas_call x1, Pallas kernels, on_device(): call(forward_kernel, [jax.ShapeDtypeStruct((HD + 8 + slots, rows), F32),...  2.37 us
    ppermute x3, waiting for transfers between devices, to_sibling(): return lax.ppermute(array, 'ctx', [(i, i ^ 1) for i in range(ny * nx * nc)])  2.23 us
  transfers between devices with their start and end apart: 16, of which 4 were waited for; matrix products, arithmetic and copies ran while one was open for 0% of the time, Pallas kernels for 5%

profile of v4, /device:TPU:1, one launch (start us, length us, event | category | flops | bytes accessed | tf_op | source)
XLA Modules:
  0.0 108.6 jit_solution(12728560103624950875)
XLA Ops:
  4.0 10.5 %all-to-all-start = ((bf16[32,128,128]{2,1,0:T(8,128)(2,1)}), bf16[32,128,128]{2,1,0:T(8,128)(2,1)S(1)}, u32[]{:S(2)}, u32[]{:S(2)}) async-start(bf16[32,128,128]{2,1,0:T(8,128)(2,1)} %get-tuple-element.35), calls=%async_computation | async-start | bytes 2097152 | tf_op jit(solution)/shard_map/all_to_all | solution.py:323
  14.5 5.8 %collective-permute-start.5 = (bf16[64,512]{1,0:T(8,128)(2,1)}, bf16[64,512]{1,0:T(8,128)(2,1)S(1)}, u32[]{:S(2)}, u32[]{:S(2)}) collective-permute-start(bf16[64,512]{1,0:T(8,128)(2,1)} %cot_ref.1), channel_id=1, source_target_pairs={{0,6},{1,7},{2,0},{3,1},{4,2},{5,3},{6,4},{7,5},{8,10},{9,11},{10,... | collective-permute-start | bytes 196616 | tf_op jit(solution)/shard_map/ppermute | solution.py:334
  20.4 6.8 %collective-permute-start.4 = (bf16[64,512]{1,0:T(8,128)(2,1)}, bf16[64,512]{1,0:T(8,128)(2,1)S(1)}, u32[]{:S(2)}, u32[]{:S(2)}) collective-permute-start(bf16[64,512]{1,0:T(8,128)(2,1)} %cot_ref.1), channel_id=1, source_target_pairs={{0,2},{1,3},{2,4},{3,5},{4,6},{5,7},{6,0},{7,1},{8,14},{9,15},{10,... | collective-permute-start | bytes 196616 | tf_op jit(solution)/shard_map/ppermute | solution.py:334
  27.1 3.1 %collective-permute-start.3 = (bf16[64,512]{1,0:T(8,128)(2,1)}, bf16[64,512]{1,0:T(8,128)(2,1)S(1)}, u32[]{:S(2)}, u32[]{:S(2)}) collective-permute-start(bf16[64,512]{1,0:T(8,128)(2,1)} %cot_ref.1), channel_id=1, source_target_pairs={{0,5},{1,6},{2,7},{3,0},{4,1},{5,2},{6,3},{7,4},{8,11},{9,12},{10,... | collective-permute-start | bytes 196616 | tf_op jit(solution)/shard_map/ppermute | solution.py:334
  30.2 5.2 %collective-permute-start.2 = (bf16[64,512]{1,0:T(8,128)(2,1)}, bf16[64,512]{1,0:T(8,128)(2,1)S(1)}, u32[]{:S(2)}, u32[]{:S(2)}) collective-permute-start(bf16[64,512]{1,0:T(8,128)(2,1)} %cot_ref.1), channel_id=1, source_target_pairs={{0,3},{1,4},{2,5},{3,6},{4,7},{5,0},{6,1},{7,2},{8,13},{9,14},{10,... | collective-permute-start | bytes 196616 | tf_op jit(solution)/shard_map/ppermute | solution.py:334
  35.4 5.5 %collective-permute-start.1 = (bf16[64,512]{1,0:T(8,128)(2,1)}, bf16[64,512]{1,0:T(8,128)(2,1)S(1)}, u32[]{:S(2)}, u32[]{:S(2)}) collective-permute-start(bf16[64,512]{1,0:T(8,128)(2,1)} %cot_ref.1), channel_id=1, source_target_pairs={{0,4},{1,5},{2,6},{3,7},{4,0},{5,1},{6,2},{7,3},{8,12},{9,13},{10,... | collective-permute-start | bytes 196616 | tf_op jit(solution)/shard_map/ppermute | solution.py:334
  43.4 3.1 %collective-permute-start.7 = (bf16[64,512]{1,0:T(8,128)(2,1)S(1)}, bf16[64,512]{1,0:T(8,128)(2,1)S(1)}, u32[]{:S(2)}, u32[]{:S(2)}) collective-permute-start(bf16[64,512]{1,0:T(8,128)(2,1)S(1)} %copy-done.4), channel_id=1, source_target_pairs={{0,7},{1,0},{2,1},{3,2},{4,3},{5,4},{6,5},{7,6},{8,9},{9,10},{10,1... | collective-permute-start | bytes 196616 | tf_op jit(solution)/shard_map/ppermute | solution.py:334
  46.5 3.4 %collective-permute-start.6 = (bf16[64,512]{1,0:T(8,128)(2,1)S(1)}, bf16[64,512]{1,0:T(8,128)(2,1)S(1)}, u32[]{:S(2)}, u32[]{:S(2)}) collective-permute-start(bf16[64,512]{1,0:T(8,128)(2,1)S(1)} %copy-done.4), channel_id=1, source_target_pairs={{0,1},{1,2},{2,3},{3,4},{4,5},{5,6},{6,7},{7,0},{8,15},{9,8},{10,9... | collective-permute-start | bytes 196616 | tf_op jit(solution)/shard_map/ppermute | solution.py:334
  49.9 1.9 %collective-permute-start = (bf16[64,512]{1,0:T(8,128)(2,1)S(1)}, bf16[64,512]{1,0:T(8,128)(2,1)S(1)}, u32[]{:S(2)}, u32[]{:S(2)}) collective-permute-start(bf16[64,512]{1,0:T(8,128)(2,1)S(1)} %get-tuple-element.31.own_ref), channel_id=1, source_target_pairs={{0,8},{8,0},{16,24},{24,16},{32,40},{40,32},{48,56},{56,48},{64,72... | collective-permute-start | bytes 196616 | tf_op jit(solution)/shard_map/ppermute | solution.py:326
  52.0 2.2 %copy-done = bf16[512,4096]{1,0:T(8,128)(2,1)S(1)} copy-done((bf16[512,4096]{1,0:T(8,128)(2,1)S(1)}, bf16[512,4096]{1,0:T(8,128)(2,1)}, u32[]{:S(2)}) %copy-start) | copy-done | bytes 4194328
  54.1 1.9 %shard_map.138.grad_ref = bf16[64,512]{1,0:T(8,128)(2,1)S(1)} custom-call(s32[2]{0:T(128)S(1)} %pad_add_fusion.place_ref, bf16[512,4096]{1,0:T(8,128)(2,1)S(1)} %copy-done, f32[64,128]{1,0:T(8,128)S(1)} %get-tuple-element.32.gate_ref, bf16[64,512]{1,0:T(8,128)(2,1)S(1)} %get-tuple-element.33.refs_0_, bf16[64,512]{1,0:T(8,128)(2,1)S(1)} %collective-permute-done.1.refs_1_, ...), custom_call_target="tpu_custom_call" | custom-call | tf_op jit(solution)/shard_map/pallas_call | solution.py:378
  56.1 2.4 %shard_map.139 = (f32[200,512]{1,0:T(8,128)S(1)}, bf16[4,512,512]{2,1,0:T(8,128)(2,1)S(1)}) custom-call(s32[2]{0:T(128)S(1)} %pad_add_fusion.place_ref, s32[1,64]{1,0:T(1,128)S(1)} %bitcast.9, bf16[64,512]{1,0:T(8,128)(2,1)S(1)} %get-tuple-element.31.own_ref, bf16[64,512]{1,0:T(8,128)(2,1)S(1)} %collective-permute-done.sibling_ref, ...), custom_call_target="tpu_custom_call" | custom-call | tf_op jit(solution)/shard_map/pallas_call | solution.py:385
  58.5 5.0 %collective-permute-start.8 = (f32[200,512]{1,0:T(8,128)S(1)}, f32[200,512]{1,0:T(8,128)S(1)}, u32[]{:S(2)}, u32[]{:S(2)}) collective-permute-start(f32[200,512]{1,0:T(8,128)S(1)} %get-tuple-element.36.own_part), channel_id=1, source_target_pairs={{0,8},{8,0},{16,24},{24,16},{32,40},{40,32},{48,56},{56,48},{64,72... | collective-permute-start | bytes 1228808 | tf_op jit(solution)/shard_map/ppermute | solution.py:326
  64.9 2.9 %shard_map.140 = (bf16[64,512]{1,0:T(8,128)(2,1)S(1)}, f32[8,256]{1,0:T(8,128)S(1)}, f32[256,128]{1,0:T(8,128)S(1)}, bf16[256,128]{1,0:T(8,128)(2,1)S(1)}, bf16[32,128,128]{2,1,0:T(8,128)(2,1)}) custom-call(f32[200,512]{1,0:T(8,128)S(1)} %get-tuple-element.36.own_part, f32[200,512]{1,0:T(8,128)S(1)} %collective-permute-done.8.sibling_part, ...), custom_call_target="tpu_custom_call" | custom-call | tf_op jit(solution)/shard_map/pallas_call | solution.py:395
  67.8 9.6 %all-to-all-start.1 = ((bf16[32,128,128]{2,1,0:T(8,128)(2,1)}), bf16[32,128,128]{2,1,0:T(8,128)(2,1)S(1)}, u32[]{:S(2)}, u32[]{:S(2)}) async-start(bf16[32,128,128]{2,1,0:T(8,128)(2,1)} %get-tuple-element.47), calls=%async_computation.1 | async-start | bytes 2097152 | tf_op jit(solution)/shard_map/all_to_all | solution.py:323
  77.4 2.2 %copy-done.1 = bf16[512,4096]{1,0:T(8,128)(2,1)S(1)} copy-done((bf16[512,4096]{1,0:T(8,128)(2,1)S(1)}, bf16[512,4096]{1,0:T(8,128)(2,1)}, u32[]{:S(2)}) %copy-start.1) | copy-done | bytes 4194328
  79.6 1.4 %shard_map.141 = (bf16[2,80,512]{2,1,0:T(8,128)(2,1)S(1)}, bf16[2,80,512]{2,1,0:T(8,128)(2,1)S(1)}, bf16[2,80,512]{2,1,0:T(8,128)(2,1)S(1)}, bf16[2,80,512]{2,1,0:T(8,128)(2,1)S(1)}) custom-call(s32[2]{0:T(128)S(1)} %pad_add_fusion.place_ref, bf16[512,4096]{1,0:T(8,128)(2,1)S(1)} %copy-done.1, bf16[64,512]{1,0:T(8,128)(2,1)S(1)} %get-tuple-element.38.att_ref, ...), custom_call_target="tpu_custom_call" | custom-call | tf_op jit(solution)/shard_map/pallas_call | solution.py:410
  81.0 1.9 %collective-permute-start.9 = (bf16[2,80,512]{2,1,0:T(8,128)(2,1)S(1)}, bf16[2,80,512]{2,1,0:T(8,128)(2,1)S(1)}, u32[]{:S(2)}, u32[]{:S(2)}) collective-permute-start(bf16[2,80,512]{2,1,0:T(8,128)(2,1)S(1)} %get-tuple-element.41), channel_id=1, source_target_pairs={{0,7},{1,0},{2,1},{3,2},{4,3},{5,4},{6,5},{7,6},{8,9},{9,10},{10,1... | collective-permute-start | bytes 491528 | tf_op jit(solution)/shard_map/ppermute | solution.py:334
  83.0 5.3 %collective-permute-start.10 = (bf16[2,80,512]{2,1,0:T(8,128)(2,1)S(1)}, bf16[2,80,512]{2,1,0:T(8,128)(2,1)S(1)}, u32[]{:S(2)}, u32[]{:S(2)}) collective-permute-start(bf16[2,80,512]{2,1,0:T(8,128)(2,1)S(1)} %get-tuple-element.42), channel_id=1, source_target_pairs={{0,6},{1,7},{2,0},{3,1},{4,2},{5,3},{6,4},{7,5},{8,10},{9,11},{10,... | collective-permute-start | bytes 491528 | tf_op jit(solution)/shard_map/ppermute | solution.py:334
  88.3 2.2 %collective-permute-start.11 = (bf16[2,80,512]{2,1,0:T(8,128)(2,1)S(1)}, bf16[2,80,512]{2,1,0:T(8,128)(2,1)S(1)}, u32[]{:S(2)}, u32[]{:S(2)}) collective-permute-start(bf16[2,80,512]{2,1,0:T(8,128)(2,1)S(1)} %get-tuple-element.43), channel_id=1, source_target_pairs={{0,1},{1,2},{2,3},{3,4},{4,5},{5,6},{6,7},{7,0},{8,15},{9,8},{10,9... | collective-permute-start | bytes 491528 | tf_op jit(solution)/shard_map/ppermute | solution.py:334
  90.5 1.9 %collective-permute-done.10 = bf16[2,80,512]{2,1,0:T(8,128)(2,1)S(1)} collective-permute-done((bf16[2,80,512]{2,1,0:T(8,128)(2,1)S(1)}, bf16[2,80,512]{2,1,0:T(8,128)(2,1)S(1)}, u32[]{:S(2)}, u32[]{:S(2)}) %collective-permute-start.10) | collective-permute-done | bytes 163872 | tf_op jit(solution)/shard_map/ppermute | solution.py:334
  92.4 3.5 %collective-permute-done.11 = bf16[2,80,512]{2,1,0:T(8,128)(2,1)S(1)} collective-permute-done((bf16[2,80,512]{2,1,0:T(8,128)(2,1)S(1)}, bf16[2,80,512]{2,1,0:T(8,128)(2,1)S(1)}, u32[]{:S(2)}, u32[]{:S(2)}) %collective-permute-start.11) | collective-permute-done | bytes 163872 | tf_op jit(solution)/shard_map/ppermute | solution.py:334
  96.1 4.8 %collective-permute-start.12 = (bf16[1,80,512]{2,1,0:T(8,128)(2,1)S(1)}, bf16[1,80,512]{2,1,0:T(8,128)(2,1)S(1)}, u32[]{:S(2)}, u32[]{:S(2)}) collective-permute-start(bf16[1,80,512]{2,1,0:T(8,128)(2,1)S(1)} %get-tuple-element.52), channel_id=1, source_target_pairs={{0,4},{1,5},{2,6},{3,7},{4,0},{5,1},{6,2},{7,3},{8,12},{9,13},{10,... | collective-permute-start | bytes 245768 | tf_op jit(solution)/shard_map/ppermute | solution.py:334
  100.9 4.1 %collective-permute-start.13 = (bf16[256,128]{1,0:T(8,128)(2,1)S(1)}, bf16[256,128]{1,0:T(8,128)(2,1)S(1)}, u32[]{:S(2)}, u32[]{:S(2)}) collective-permute-start(bf16[256,128]{1,0:T(8,128)(2,1)S(1)} %get-tuple-element.46), channel_id=1, source_target_pairs={{0,8},{8,0},{16,24},{24,16},{32,40},{40,32},{48,56},{56,48},{64,72... | collective-permute-start | bytes 196616 | tf_op jit(solution)/shard_map/ppermute | solution.py:326
  (40 shorter events, 10.3 us)
Async XLA Ops:
  0.6 55.5 %copy-start.5 = (s32[64]{0:T(128)S(1)}, s32[64]{0:T(128)}, u32[]{:S(2)}) copy-start(s32[64]{0:T(128)} %param.14) | copy-start | bytes 772
  4.0 52.1 %all-to-all-start = ((bf16[32,128,128]{2,1,0:T(8,128)(2,1)}), bf16[32,128,128]{2,1,0:T(8,128)(2,1)S(1)}, u32[]{:S(2)}, u32[]{:S(2)}) async-start(bf16[32,128,128]{2,1,0:T(8,128)(2,1)} %get-tuple-element.35), calls=%async_computation | async-start | bytes 2097152 | tf_op jit(solution)/shard_map/all_to_all | solution.py:323
  14.5 28.8 %collective-permute-start.5 = (bf16[64,512]{1,0:T(8,128)(2,1)}, bf16[64,512]{1,0:T(8,128)(2,1)S(1)}, u32[]{:S(2)}, u32[]{:S(2)}) collective-permute-start(bf16[64,512]{1,0:T(8,128)(2,1)} %cot_ref.1), channel_id=1, source_target_pairs={{0,6},{1,7},{2,0},{3,1},{4,2},{5,3},{6,4},{7,5},{8,10},{9,11},{10,... | collective-permute-start | bytes 196616 | tf_op jit(solution)/shard_map/ppermute | solution.py:334
  20.4 26.1 %collective-permute-start.4 = (bf16[64,512]{1,0:T(8,128)(2,1)}, bf16[64,512]{1,0:T(8,128)(2,1)S(1)}, u32[]{:S(2)}, u32[]{:S(2)}) collective-permute-start(bf16[64,512]{1,0:T(8,128)(2,1)} %cot_ref.1), channel_id=1, source_target_pairs={{0,2},{1,3},{2,4},{3,5},{4,6},{5,7},{6,0},{7,1},{8,14},{9,15},{10,... | collective-permute-start | bytes 196616 | tf_op jit(solution)/shard_map/ppermute | solution.py:334
  27.1 22.8 %collective-permute-start.3 = (bf16[64,512]{1,0:T(8,128)(2,1)}, bf16[64,512]{1,0:T(8,128)(2,1)S(1)}, u32[]{:S(2)}, u32[]{:S(2)}) collective-permute-start(bf16[64,512]{1,0:T(8,128)(2,1)} %cot_ref.1), channel_id=1, source_target_pairs={{0,5},{1,6},{2,7},{3,0},{4,1},{5,2},{6,3},{7,4},{8,11},{9,12},{10,... | collective-permute-start | bytes 196616 | tf_op jit(solution)/shard_map/ppermute | solution.py:334
  30.2 21.7 %collective-permute-start.2 = (bf16[64,512]{1,0:T(8,128)(2,1)}, bf16[64,512]{1,0:T(8,128)(2,1)S(1)}, u32[]{:S(2)}, u32[]{:S(2)}) collective-permute-start(bf16[64,512]{1,0:T(8,128)(2,1)} %cot_ref.1), channel_id=1, source_target_pairs={{0,3},{1,4},{2,5},{3,6},{4,7},{5,0},{6,1},{7,2},{8,13},{9,14},{10,... | collective-permute-start | bytes 196616 | tf_op jit(solution)/shard_map/ppermute | solution.py:334
  35.4 16.5 %collective-permute-start.1 = (bf16[64,512]{1,0:T(8,128)(2,1)}, bf16[64,512]{1,0:T(8,128)(2,1)S(1)}, u32[]{:S(2)}, u32[]{:S(2)}) collective-permute-start(bf16[64,512]{1,0:T(8,128)(2,1)} %cot_ref.1), channel_id=1, source_target_pairs={{0,4},{1,5},{2,6},{3,7},{4,0},{5,1},{6,2},{7,3},{8,12},{9,13},{10,... | collective-permute-start | bytes 196616 | tf_op jit(solution)/shard_map/ppermute | solution.py:334
  40.9 0.8 copy-start.3
  41.7 0.8 copy-start.4
  42.6 0.7 copy-start.6
  43.4 8.5 %collective-permute-start.7 = (bf16[64,512]{1,0:T(8,128)(2,1)S(1)}, bf16[64,512]{1,0:T(8,128)(2,1)S(1)}, u32[]{:S(2)}, u32[]{:S(2)}) collective-permute-start(bf16[64,512]{1,0:T(8,128)(2,1)S(1)} %copy-done.4), channel_id=1, source_target_pairs={{0,7},{1,0},{2,1},{3,2},{4,3},{5,4},{6,5},{7,6},{8,9},{9,10},{10,1... | collective-permute-start | bytes 196616 | tf_op jit(solution)/shard_map/ppermute | solution.py:334
  46.5 5.4 %collective-permute-start.6 = (bf16[64,512]{1,0:T(8,128)(2,1)S(1)}, bf16[64,512]{1,0:T(8,128)(2,1)S(1)}, u32[]{:S(2)}, u32[]{:S(2)}) collective-permute-start(bf16[64,512]{1,0:T(8,128)(2,1)S(1)} %copy-done.4), channel_id=1, source_target_pairs={{0,1},{1,2},{2,3},{3,4},{4,5},{5,6},{6,7},{7,0},{8,15},{9,8},{10,9... | collective-permute-start | bytes 196616 | tf_op jit(solution)/shard_map/ppermute | solution.py:334
  49.9 6.2 %collective-permute-start = (bf16[64,512]{1,0:T(8,128)(2,1)S(1)}, bf16[64,512]{1,0:T(8,128)(2,1)S(1)}, u32[]{:S(2)}, u32[]{:S(2)}) collective-permute-start(bf16[64,512]{1,0:T(8,128)(2,1)S(1)} %get-tuple-element.31.own_ref), channel_id=1, source_target_pairs={{0,8},{8,0},{16,24},{24,16},{32,40},{40,32},{48,56},{56,48},{64,72... | collective-permute-start | bytes 196616 | tf_op jit(solution)/shard_map/ppermute | solution.py:326
  51.9 2.2 %copy-start = (bf16[512,4096]{1,0:T(8,128)(2,1)S(1)}, bf16[512,4096]{1,0:T(8,128)(2,1)}, u32[]{:S(2)}) copy-start(bf16[512,4096]{1,0:T(8,128)(2,1)} %weight_ref.3) | copy-start | bytes 12582916
  58.5 6.4 %collective-permute-start.8 = (f32[200,512]{1,0:T(8,128)S(1)}, f32[200,512]{1,0:T(8,128)S(1)}, u32[]{:S(2)}, u32[]{:S(2)}) collective-permute-start(f32[200,512]{1,0:T(8,128)S(1)} %get-tuple-element.36.own_part), channel_id=1, source_target_pairs={{0,8},{8,0},{16,24},{24,16},{32,40},{40,32},{48,56},{56,48},{64,72... | collective-permute-start | bytes 1228808 | tf_op jit(solution)/shard_map/ppermute | solution.py:326
  67.8 38.9 %copy-start.2 = (bf16[512,512]{1,0:T(8,128)(2,1)S(1)}, bf16[512,512]{1,0:T(8,128)(2,1)}, u32[]{:S(2)}) copy-start(bf16[512,512]{1,0:T(8,128)(2,1)} %hidden_ref.1) | copy-start | bytes 1572868
  67.8 38.9 %copy-start.7 = (f32[64]{0:T(128)S(1)}, f32[64]{0:T(128)}, u32[]{:S(2)}) copy-start(f32[64]{0:T(128)} %param.13) | copy-start | bytes 772
  67.8 40.0 %all-to-all-start.1 = ((bf16[32,128,128]{2,1,0:T(8,128)(2,1)}), bf16[32,128,128]{2,1,0:T(8,128)(2,1)S(1)}, u32[]{:S(2)}, u32[]{:S(2)}) async-start(bf16[32,128,128]{2,1,0:T(8,128)(2,1)} %get-tuple-element.47), calls=%async_computation.1 | async-start | bytes 2097152 | tf_op jit(solution)/shard_map/all_to_all | solution.py:323
  77.4 2.2 %copy-start.1 = (bf16[512,4096]{1,0:T(8,128)(2,1)S(1)}, bf16[512,4096]{1,0:T(8,128)(2,1)}, u32[]{:S(2)}) copy-start(bf16[512,4096]{1,0:T(8,128)(2,1)} %weight_ref.3) | copy-start | bytes 12582916
  81.0 9.5 %collective-permute-start.9 = (bf16[2,80,512]{2,1,0:T(8,128)(2,1)S(1)}, bf16[2,80,512]{2,1,0:T(8,128)(2,1)S(1)}, u32[]{:S(2)}, u32[]{:S(2)}) collective-permute-start(bf16[2,80,512]{2,1,0:T(8,128)(2,1)S(1)} %get-tuple-element.41), channel_id=1, source_target_pairs={{0,7},{1,0},{2,1},{3,2},{4,3},{5,4},{6,5},{7,6},{8,9},{9,10},{10,1... | collective-permute-start | bytes 491528 | tf_op jit(solution)/shard_map/ppermute | solution.py:334
  83.0 9.5 %collective-permute-start.10 = (bf16[2,80,512]{2,1,0:T(8,128)(2,1)S(1)}, bf16[2,80,512]{2,1,0:T(8,128)(2,1)S(1)}, u32[]{:S(2)}, u32[]{:S(2)}) collective-permute-start(bf16[2,80,512]{2,1,0:T(8,128)(2,1)S(1)} %get-tuple-element.42), channel_id=1, source_target_pairs={{0,6},{1,7},{2,0},{3,1},{4,2},{5,3},{6,4},{7,5},{8,10},{9,11},{10,... | collective-permute-start | bytes 491528 | tf_op jit(solution)/shard_map/ppermute | solution.py:334
  88.3 7.7 %collective-permute-start.11 = (bf16[2,80,512]{2,1,0:T(8,128)(2,1)S(1)}, bf16[2,80,512]{2,1,0:T(8,128)(2,1)S(1)}, u32[]{:S(2)}, u32[]{:S(2)}) collective-permute-start(bf16[2,80,512]{2,1,0:T(8,128)(2,1)S(1)} %get-tuple-element.43), channel_id=1, source_target_pairs={{0,1},{1,2},{2,3},{3,4},{4,5},{5,6},{6,7},{7,0},{8,15},{9,8},{10,9... | collective-permute-start | bytes 491528 | tf_op jit(solution)/shard_map/ppermute | solution.py:334
  96.1 10.5 %collective-permute-start.12 = (bf16[1,80,512]{2,1,0:T(8,128)(2,1)S(1)}, bf16[1,80,512]{2,1,0:T(8,128)(2,1)S(1)}, u32[]{:S(2)}, u32[]{:S(2)}) collective-permute-start(bf16[1,80,512]{2,1,0:T(8,128)(2,1)S(1)} %get-tuple-element.52), channel_id=1, source_target_pairs={{0,4},{1,5},{2,6},{3,7},{4,0},{5,1},{6,2},{7,3},{8,12},{9,13},{10,... | collective-permute-start | bytes 245768 | tf_op jit(solution)/shard_map/ppermute | solution.py:334
  100.9 5.0 %collective-permute-start.13 = (bf16[256,128]{1,0:T(8,128)(2,1)S(1)}, bf16[256,128]{1,0:T(8,128)(2,1)S(1)}, u32[]{:S(2)}, u32[]{:S(2)}) collective-permute-start(bf16[256,128]{1,0:T(8,128)(2,1)S(1)} %get-tuple-element.46), channel_id=1, source_target_pairs={{0,8},{8,0},{16,24},{24,16},{32,40},{40,32},{48,56},{56,48},{64,72... | collective-permute-start | bytes 196616 | tf_op jit(solution)/shard_map/ppermute | solution.py:326

commit v5 on v4

--- a/solution.py
+++ b/solution.py
@@ -59,9 +59,11 @@
     return jnp.concatenate([field[:, h * HD : (h + 1) * HD].astype(F32) for h in range(heads)], axis=0)
 
 
-def payload_kernel(count_ref, pair_ref, position_ref, frequency_ref, pay_ref, copies_ref, cos_ref, sin_ref, stage, sems):
+def payload_kernel(place_ref, count_ref, pair_ref, frequency_ref, pay_ref, copies_ref, cos_ref, sin_ref, stage, sems):
     slots = cos_ref.shape[0]
-    angles = as_column(position_ref[...]) * frequency_ref[...]
+    index = pair_ref[2 * slots : 2 * slots + 8, 0:slots].astype(F32)
+    position = 2.0 * index[0:1] + index[1:2] + (place_ref[0] * TOK_DEV).astype(F32)
+    angles = as_column(position) * frequency_ref[...]
     col_ids = lax.broadcasted_iota(jnp.int32, (slots, HD), 1)
     row_ids = lax.broadcasted_iota(jnp.int32, (slots, HD), 0)
     cos_full = jnp.cos(angles)
@@ -93,7 +95,7 @@
     return pl.ds(pl.multiple_of(owner * width, width), width)
 
 
-def query_kernel(count_ref, query_ref, cos_ref, sin_ref, logit_ref, cot_ref, out_ref, gate_ref, cot_out):
+def query_kernel(count_ref, query_ref, cos_ref, sin_ref, logit_ref, out_ref, gate_ref):
     cos_full, sin_signed = cos_ref[...], sin_ref[...]
     for h in range(query_ref.shape[1] // HD):
         part = query_ref[:, h * HD : (h + 1) * HD].astype(F32)
@@ -101,17 +103,26 @@
     slots = query_ref.shape[0]
     gate = jnp.where(live_row(count_ref, slots), 1.0 / (1.0 + jnp.exp(-logit_ref[...])), 0.0)
     gate_ref[...] = jnp.broadcast_to(as_column(gate), gate_ref.shape)
-    cot_out[...] = cot_ref[...]
-
-
-def cotangent_kernel(place_ref, weight_ref, gate_ref, *refs):
-    pieces, grad_ref = refs[:-1], refs[-1]
-    parts = len(pieces)
-    width = grad_ref.shape[1]
+
+
+def weight_copies(place_ref, weight_ref, held, sems):
+    parts, _, width = held.shape
+    copies = []
+    for at, shift in enumerate(tp_order(parts)):
+        columns = column_block(place_ref, shift, parts, width)
+        copies.append(pltpu.make_async_copy(weight_ref.at[:, columns], held.at[at], sems.at[at]))
+    for copy in copies:
+        copy.start()
+    return copies
+
+
+def cotangent_kernel(place_ref, weight_ref, gate_ref, pair_ref, *refs):
+    pieces, (grad_ref, held, sems) = (pair_ref,) + refs[:-3], refs[-3:]
+    copies = weight_copies(place_ref, weight_ref, held, sems)
     total = None
-    for piece, shift in zip(pieces, [0] + direct_shifts(parts)):
-        columns = column_block(place_ref, shift, parts, width)
-        part = matmul(piece[...], weight_ref[:, columns], ((1,), (1,)))
+    for at, copy in enumerate(copies):
+        copy.wait()
+        part = matmul(pieces[at // 2][at % 2], held[at], ((1,), (1,)))
         total = part if total is None else total + part
     grad_ref[...] = (total * gate_ref[:, 0:1]).astype(BF16)
 
@@ -226,10 +237,11 @@
         copy.wait()
 
 
-def projection_kernel(place_ref, weight_ref, att_ref, delta_ref, *part_refs):
+def projection_kernel(place_ref, weight_ref, att_ref, delta_ref, *refs):
+    part_refs, (held, sems) = refs[:-2], refs[-2:]
+    copies = weight_copies(place_ref, weight_ref, held, sems)
     slots = att_ref.shape[0]
     pair, _, width = part_refs[0].shape
-    parts = pair * len(part_refs)
     rows = delta_ref.shape[1]
     delta = delta_ref[...]
     row_sum = delta[:, 0:slots]
@@ -238,10 +250,10 @@
     extra = jnp.concatenate([row_sum, jnp.zeros((8, width - slots), F32)], axis=1)
     extra = jnp.concatenate([extra, extra], axis=0).astype(BF16)
     att = att_ref[...]
-    for at in range(parts):
-        columns = column_block(place_ref, tp_order(parts)[at], parts, width)
+    for at, copy in enumerate(copies):
+        copy.wait()
         part_ref = part_refs[at // pair]
-        part_ref[at % pair, 0:slots, :] = matmul(att, weight_ref[:, columns], ((1,), (0,))).astype(BF16)
+        part_ref[at % pair, 0:slots, :] = matmul(att, held[at], ((1,), (0,))).astype(BF16)
         part_ref[at % pair, slots : slots + 16, :] = extra
 
 
@@ -280,13 +292,6 @@
     total = added_up(landed_ref)
     dk_ref[...] = turn(total[0:slots, :], cos_ref[...], -sin_ref[...]).astype(BF16)
     dv_ref[...] = total[slots : 2 * slots, :].astype(BF16)
-
-
-def direct_shifts(parts):
-    shifts = []
-    for distance in range(parts // 2, 0, -1):
-        shifts += [distance] if 2 * distance == parts else [distance, -distance]
-    return shifts
 
 
 def tp_shifts(parts):
@@ -339,6 +344,8 @@
     my_shard = lax.axis_index("ctx").astype(jnp.int32)
     place = jnp.stack([my_shard, lax.axis_index("tp").astype(jnp.int32)])
     index_row = chosen_index[None, :]
+    index_rows = jnp.stack([chosen_index // 2, chosen_index % 2]).astype(BF16)
+    index_rows = jnp.pad(index_rows, ((0, 14), (0, HD - slots)))
     logit_row = router_logit[None, :]
     half = jnp.arange(HD // 2, dtype=F32)
     frequency = ROTARY_BASE ** (-(half * 2.0 / HD))
@@ -352,33 +359,38 @@
             jax.ShapeDtypeStruct((slots, HD), F32),
             jax.ShapeDtypeStruct((slots, HD), F32),
         ],
-        [SMEM] + [VMEM] * 3,
+        [SMEM] * 2 + [VMEM] * 2,
         [pltpu.VMEM((chunk, 2 * slots, HD), BF16), pltpu.SemaphoreType.DMA((blocks // chunk,))],
         out_specs=[VMEM, HBM, VMEM, VMEM],
     )(
+        place,
         chosen_count,
-        jnp.concatenate([key_vectors, value_vectors], axis=0),
-        (my_shard * TOK_DEV + chosen_index).astype(F32)[None, :],
+        jnp.concatenate([key_vectors, value_vectors, index_rows], axis=0),
         frequency,
     )
+    first_arrival = tp_send(out_cotangent[None], tp_count // 2)
+    payloads, first_arrival = lax.optimization_barrier((payloads, first_arrival))
     pieces = exchange(payloads)
 
-    own_queries, gate, own_cot = call(
+    own_queries, gate = call(
         query_kernel,
-        [
-            jax.ShapeDtypeStruct((slots, width), BF16),
-            jax.ShapeDtypeStruct((slots, HD), F32),
-            jax.ShapeDtypeStruct((slots, width), BF16),
-        ],
-        [SMEM] + [VMEM] * 5,
-    )(chosen_count, queries, cos_full, sin_signed, logit_row, out_cotangent)
+        [jax.ShapeDtypeStruct((slots, width), BF16), jax.ShapeDtypeStruct((slots, HD), F32)],
+        [SMEM] + [VMEM] * 4,
+    )(chosen_count, queries, cos_full, sin_signed, logit_row)
     sibling_queries = to_sibling(own_queries)
 
-    cot = [own_cot] + [tp_send(out_cotangent, shift) for shift in direct_shifts(tp_count)]
+    held = [
+        pltpu.VMEM((tp_count, width, width), BF16),
+        pltpu.SemaphoreType.DMA((tp_count,)),
+    ]
+    pair = jnp.concatenate([out_cotangent[None], first_arrival], axis=0)
+    cot = [pair] + [tp_send(pair, shift) for shift in tp_shifts(tp_count)]
     grad_attention = call(
         cotangent_kernel,
         jax.ShapeDtypeStruct((slots, width), BF16),
-        [SMEM] + [VMEM] * (2 + tp_count),
+        [SMEM, HBM] + [VMEM] * (1 + len(cot)),
+        held,
+        limit=50,
     )(place, out_weight, gate, *cot)
 
     scored = (blocks // chunk, chunk * slots, rows)
@@ -410,13 +422,16 @@
     shares = call(
         projection_kernel,
         [jax.ShapeDtypeStruct((2, slots + 16, width), BF16)] * (tp_count // 2),
-        [SMEM] + [VMEM] * 3,
+        [SMEM, HBM] + [VMEM] * 2,
+        held,
+        limit=50,
     )(place, out_weight, attention, delta)
     dq_arrived = to_sibling(dq_sibling)
     grad_queries = call(
         query_grad_kernel, jax.ShapeDtypeStruct((slots, width), BF16), [VMEM] * 4
     )(cos_full, sin_signed, dq_own, dq_arrived)
     arrived = [tp_send(share, -shift) for share, shift in zip(shares[1:], tp_shifts(tp_count))]
+    arrived, grad_queries = lax.optimization_barrier((arrived, grad_queries))
     shares = functools.reduce(jnp.add, [part.astype(F32) for part in [shares[0]] + arrived]).astype(BF16)
     near = shares[:1]
     arrived = tp_send(shares[1:], -(tp_count // 2))

time: 110 us -> 103 us (0.936)
  starting transfers between devices: 78.3 us -> 64.6 us
  waiting for transfers between devices: 7.73 us -> 15.8 us
  local copies, waits for them, and re-layouts: 6.73 us -> 1.52 us
  Pallas kernels: 12.6 us -> 16.5 us
    ppermute x11 -> x8, starting transfers between devices: 47.1 us -> 37.9 us  [tp_send(): return lax.ppermute(array, ('ctx', 'tp'), pairs)]
    all_to_all x2, waiting for transfers between devices: 0.01 us -> 6.31 us  [exchange(): lax.all_to_all(array, 'ctx', 0, 0, axis_index_groups=groups, tiled=True)]
    unnamed x16 -> x10, local copies, waits for them, and re-layouts: 6.71 us -> 1.51 us
    all_to_all x2, starting transfers between devices: 20.1 us -> 15.1 us  [exchange(): lax.all_to_all(array, 'ctx', 0, 0, axis_index_groups=groups, tiled=True)]
    pallas_call x1, Pallas kernels: 1.4 us -> 3.34 us  [on_device(): call(projection_kernel, [jax.ShapeDtypeStruct((2, slots + 16, width), BF1...]
    ppermute x11 -> x8, waiting for transfers between devices: 5.49 us -> 7.3 us  [tp_send(): return lax.ppermute(array, ('ctx', 'tp'), pairs)]
    pallas_call x1, Pallas kernels: 1.94 us -> 3.3 us  [on_device(): call(cotangent_kernel, jax.ShapeDtypeStruct((slots, width), BF16), [SMEM,...]
  transfers between devices with their start and end apart: 16 -> 13, of which waited for: 4 -> 4; matrix products, arithmetic and copies ran while one was open for 0% -> 2% of each run, Pallas kernels for 5% -> 10%
where the time goes in v5:
time: 103 us
  starting transfers between devices  64.6 us (63%)
  Pallas kernels  16.5 us (16%)
  waiting for transfers between devices  15.8 us (15%)
  other arithmetic  2.52 us (2%)
  between operations  1.54 us (1%)
  local copies, waits for them, and re-layouts  1.52 us (1%)
    ppermute x8, starting transfers between devices, tp_send(): return lax.ppermute(array, ('ctx', 'tp'), pairs)  37.9 us
    all_to_all x2, starting transfers between devices, exchange(): lax.all_to_all(array, 'ctx', 0, 0, axis_index_groups=groups, tiled=True)  15.1 us
    ppermute x3, starting transfers between devices, to_sibling(): return lax.ppermute(array, 'ctx', [(i, i ^ 1) for i in range(ny * nx * nc)])  11.6 us
    ppermute x8, waiting for transfers between devices, tp_send(): return lax.ppermute(array, ('ctx', 'tp'), pairs)  7.3 us
    all_to_all x2, waiting for transfers between devices, exchange(): lax.all_to_all(array, 'ctx', 0, 0, axis_index_groups=groups, tiled=True)  6.31 us
    pallas_call x1, Pallas kernels, on_device(): call(projection_kernel, [jax.ShapeDtypeStruct((2, slots + 16, width), BF1...  3.34 us
    pallas_call x1, Pallas kernels, on_device(): call(cotangent_kernel, jax.ShapeDtypeStruct((slots, width), BF16), [SMEM,...  3.3 us
    pallas_call x1, Pallas kernels, on_device(): call(backward_kernel, [jax.ShapeDtypeStruct((slots, width), BF16), jax.Sh...  2.87 us
  transfers between devices with their start and end apart: 13, of which 4 were waited for; matrix products, arithmetic and copies ran while one was open for 2% of the time, Pallas kernels for 10%

profile of v5, /device:TPU:1, one launch (start us, length us, event | category | flops | bytes accessed | tf_op | source)
XLA Modules:
  0.0 102.5 jit_solution(12671213668714734432)
XLA Ops:
  0.6 11.5 %collective-permute-start.1 = (bf16[1,64,512]{2,1,0:T(8,128)(2,1)}, bf16[1,64,512]{2,1,0:T(8,128)(2,1)S(1)}, u32[]{:S(2)}, u32[]{:S(2)}) collective-permute-start(bf16[1,64,512]{2,1,0:T(8,128)(2,1)} %bitcast.16), channel_id=1, source_target_pairs={{0,4},{1,5},{2,6},{3,7},{4,0},{5,1},{6,2},{7,3},{8,12},{9,13},{10,... | collective-permute-start | bytes 196616 | tf_op jit(solution)/shard_map/ppermute | solution.py:339
  14.4 1.8 %shard_map.136 = (bf16[128,128]{1,0:T(8,128)(2,1)S(1)}, bf16[32,128,128]{2,1,0:T(8,128)(2,1)}, f32[64,128]{1,0:T(8,128)S(1)}, f32[64,128]{1,0:T(8,128)S(1)}) custom-call(s32[2]{0:T(128)S(1)} %pad_add_fusion.place_ref, s32[1]{0:T(128)S(6)} %copy.15.count_ref, bf16[144,128]{1,0:T(8,128)(2,1)S(1)} %pad_maximum_fusion.1.pair_ref, ...), custom_call_target="tpu_custom_call" | custom-call | tf_op jit(solution)/shard_map/pallas_call | solution.py:354
  16.2 9.7 %all-to-all-start = ((bf16[32,128,128]{2,1,0:T(8,128)(2,1)}), bf16[32,128,128]{2,1,0:T(8,128)(2,1)S(1)}, u32[]{:S(2)}, u32[]{:S(2)}) async-start(bf16[32,128,128]{2,1,0:T(8,128)(2,1)} %get-tuple-element.41), calls=%async_computation | async-start | bytes 2097152 | tf_op jit(solution)/shard_map/all_to_all | solution.py:328
  25.9 0.9 pad_maximum_fusion.pair_ref
  26.7 3.1 %collective-permute-start.4 = (bf16[2,64,512]{2,1,0:T(8,128)(2,1)S(1)}, bf16[2,64,512]{2,1,0:T(8,128)(2,1)S(1)}, u32[]{:S(2)}, u32[]{:S(2)}) collective-permute-start(bf16[2,64,512]{2,1,0:T(8,128)(2,1)S(1)} %pad_maximum_fusion.pair_ref), channel_id=1, source_target_pairs={{0,7},{1,0},{2,1},{3,2},{4,3},{5,4},{6,5},{7,6},{8,9},{9,10},{10,1... | collective-permute-start | bytes 393224 | tf_op jit(solution)/shard_map/ppermute | solution.py:339
  29.8 5.4 %collective-permute-start.3 = (bf16[2,64,512]{2,1,0:T(8,128)(2,1)S(1)}, bf16[2,64,512]{2,1,0:T(8,128)(2,1)S(1)}, u32[]{:S(2)}, u32[]{:S(2)}) collective-permute-start(bf16[2,64,512]{2,1,0:T(8,128)(2,1)S(1)} %pad_maximum_fusion.pair_ref), channel_id=1, source_target_pairs={{0,2},{1,3},{2,4},{3,5},{4,6},{5,7},{6,0},{7,1},{8,14},{9,15},{10,... | collective-permute-start | bytes 393224 | tf_op jit(solution)/shard_map/ppermute | solution.py:339
  35.2 3.4 %collective-permute-start.2 = (bf16[2,64,512]{2,1,0:T(8,128)(2,1)S(1)}, bf16[2,64,512]{2,1,0:T(8,128)(2,1)S(1)}, u32[]{:S(2)}, u32[]{:S(2)}) collective-permute-start(bf16[2,64,512]{2,1,0:T(8,128)(2,1)S(1)} %pad_maximum_fusion.pair_ref), channel_id=1, source_target_pairs={{0,1},{1,2},{2,3},{3,4},{4,5},{5,6},{6,7},{7,0},{8,15},{9,8},{10,9... | collective-permute-start | bytes 393224 | tf_op jit(solution)/shard_map/ppermute | solution.py:339
  40.2 1.9 %collective-permute-start = (bf16[64,512]{1,0:T(8,128)(2,1)S(1)}, bf16[64,512]{1,0:T(8,128)(2,1)S(1)}, u32[]{:S(2)}, u32[]{:S(2)}) collective-permute-start(bf16[64,512]{1,0:T(8,128)(2,1)S(1)} %get-tuple-element.36.own_ref), channel_id=1, source_target_pairs={{0,8},{8,0},{16,24},{24,16},{32,40},{40,32},{48,56},{56,48},{64,72... | collective-permute-start | bytes 196616 | tf_op jit(solution)/shard_map/ppermute | solution.py:331
  42.2 3.3 %shard_map.138.grad_ref = bf16[64,512]{1,0:T(8,128)(2,1)S(1)} custom-call(s32[2]{0:T(128)S(1)} %pad_add_fusion.place_ref, bf16[512,4096]{1,0:T(8,128)(2,1)} %weight_ref.3, f32[64,128]{1,0:T(8,128)S(1)} %get-tuple-element.37.gate_ref, bf16[2,64,512]{2,1,0:T(8,128)(2,1)S(1)} %pad_maximum_fusion.pair_ref, ...), custom_call_target="tpu_custom_call" | custom-call | tf_op jit(solution)/shard_map/pallas_call | solution.py:388
  45.5 6.3 %all-to-all-done.piece_ref = bf16[32,128,128]{2,1,0:T(8,128)(2,1)S(1)} async-done(((bf16[32,128,128]{2,1,0:T(8,128)(2,1)}), bf16[32,128,128]{2,1,0:T(8,128)(2,1)S(1)}, u32[]{:S(2)}, u32[]{:S(2)}) %all-to-all-start) | async-done | bytes 1048608 | tf_op jit(solution)/shard_map/all_to_all | solution.py:328
  51.8 2.4 %shard_map.139 = (f32[200,512]{1,0:T(8,128)S(1)}, bf16[4,512,512]{2,1,0:T(8,128)(2,1)S(1)}) custom-call(s32[2]{0:T(128)S(1)} %pad_add_fusion.place_ref, s32[1,64]{1,0:T(1,128)S(1)} %bitcast.12, bf16[64,512]{1,0:T(8,128)(2,1)S(1)} %get-tuple-element.36.own_ref, bf16[64,512]{1,0:T(8,128)(2,1)S(1)} %collective-permute-done.sibling_ref, ...), custom_call_target="tpu_custom_call" | custom-call | tf_op jit(solution)/shard_map/pallas_call | solution.py:397
  54.2 5.0 %collective-permute-start.5 = (f32[200,512]{1,0:T(8,128)S(1)}, f32[200,512]{1,0:T(8,128)S(1)}, u32[]{:S(2)}, u32[]{:S(2)}) collective-permute-start(f32[200,512]{1,0:T(8,128)S(1)} %get-tuple-element.42.own_part), channel_id=1, source_target_pairs={{0,8},{8,0},{16,24},{24,16},{32,40},{40,32},{48,56},{56,48},{64,72... | collective-permute-start | bytes 1228808 | tf_op jit(solution)/shard_map/ppermute | solution.py:331
  59.2 1.4 %collective-permute-done.5.sibling_part = f32[200,512]{1,0:T(8,128)S(1)} collective-permute-done((f32[200,512]{1,0:T(8,128)S(1)}, f32[200,512]{1,0:T(8,128)S(1)}, u32[]{:S(2)}, u32[]{:S(2)}) %collective-permute-start.5) | collective-permute-done | bytes 409632 | tf_op jit(solution)/shard_map/ppermute | solution.py:331
  60.5 2.9 %shard_map.140 = (bf16[64,512]{1,0:T(8,128)(2,1)S(1)}, f32[8,256]{1,0:T(8,128)S(1)}, f32[256,128]{1,0:T(8,128)S(1)}, bf16[256,128]{1,0:T(8,128)(2,1)S(1)}, bf16[32,128,128]{2,1,0:T(8,128)(2,1)}) custom-call(f32[200,512]{1,0:T(8,128)S(1)} %get-tuple-element.42.own_part, f32[200,512]{1,0:T(8,128)S(1)} %collective-permute-done.5.sibling_part, ...), custom_call_target="tpu_custom_call" | custom-call | tf_op jit(solution)/shard_map/pallas_call | solution.py:407
  63.4 5.4 %all-to-all-start.1 = ((bf16[32,128,128]{2,1,0:T(8,128)(2,1)}), bf16[32,128,128]{2,1,0:T(8,128)(2,1)S(1)}, u32[]{:S(2)}, u32[]{:S(2)}) async-start(bf16[32,128,128]{2,1,0:T(8,128)(2,1)} %get-tuple-element.57), calls=%async_computation.1 | async-start | bytes 2097152 | tf_op jit(solution)/shard_map/all_to_all | solution.py:328
  68.9 3.3 %shard_map.141 = (bf16[2,80,512]{2,1,0:T(8,128)(2,1)S(1)}, bf16[2,80,512]{2,1,0:T(8,128)(2,1)S(1)}, bf16[2,80,512]{2,1,0:T(8,128)(2,1)S(1)}, bf16[2,80,512]{2,1,0:T(8,128)(2,1)S(1)}) custom-call(s32[2]{0:T(128)S(1)} %pad_add_fusion.place_ref, bf16[512,4096]{1,0:T(8,128)(2,1)} %weight_ref.3, bf16[64,512]{1,0:T(8,128)(2,1)S(1)} %get-tuple-element.44.att_ref, ...), custom_call_target="tpu_custom_call" | custom-call | tf_op jit(solution)/shard_map/pallas_call | solution.py:422
  72.2 3.1 %collective-permute-start.6 = (bf16[2,80,512]{2,1,0:T(8,128)(2,1)S(1)}, bf16[2,80,512]{2,1,0:T(8,128)(2,1)S(1)}, u32[]{:S(2)}, u32[]{:S(2)}) collective-permute-start(bf16[2,80,512]{2,1,0:T(8,128)(2,1)S(1)} %get-tuple-element.47), channel_id=1, source_target_pairs={{0,7},{1,0},{2,1},{3,2},{4,3},{5,4},{6,5},{7,6},{8,9},{9,10},{10,1... | collective-permute-start | bytes 491528 | tf_op jit(solution)/shard_map/ppermute | solution.py:339
  75.3 4.0 %collective-permute-start.7 = (bf16[2,80,512]{2,1,0:T(8,128)(2,1)S(1)}, bf16[2,80,512]{2,1,0:T(8,128)(2,1)S(1)}, u32[]{:S(2)}, u32[]{:S(2)}) collective-permute-start(bf16[2,80,512]{2,1,0:T(8,128)(2,1)S(1)} %get-tuple-element.48), channel_id=1, source_target_pairs={{0,6},{1,7},{2,0},{3,1},{4,2},{5,3},{6,4},{7,5},{8,10},{9,11},{10,... | collective-permute-start | bytes 491528 | tf_op jit(solution)/shard_map/ppermute | solution.py:339
  79.4 3.4 %collective-permute-start.8 = (bf16[2,80,512]{2,1,0:T(8,128)(2,1)S(1)}, bf16[2,80,512]{2,1,0:T(8,128)(2,1)S(1)}, u32[]{:S(2)}, u32[]{:S(2)}) collective-permute-start(bf16[2,80,512]{2,1,0:T(8,128)(2,1)S(1)} %get-tuple-element.49), channel_id=1, source_target_pairs={{0,1},{1,2},{2,3},{3,4},{4,5},{5,6},{6,7},{7,0},{8,15},{9,8},{10,9... | collective-permute-start | bytes 491528 | tf_op jit(solution)/shard_map/ppermute | solution.py:339
  82.8 4.7 %collective-permute-start.9 = (bf16[256,128]{1,0:T(8,128)(2,1)S(1)}, bf16[256,128]{1,0:T(8,128)(2,1)S(1)}, u32[]{:S(2)}, u32[]{:S(2)}) collective-permute-start(bf16[256,128]{1,0:T(8,128)(2,1)S(1)} %get-tuple-element.51), channel_id=1, source_target_pairs={{0,8},{8,0},{16,24},{24,16},{32,40},{40,32},{48,56},{56,48},{64,72... | collective-permute-start | bytes 196616 | tf_op jit(solution)/shard_map/ppermute | solution.py:331
  87.5 0.9 collective-permute-done.9.arrived_ref
  89.2 4.1 %collective-permute-start.10 = (bf16[1,80,512]{2,1,0:T(8,128)(2,1)S(1)}, bf16[1,80,512]{2,1,0:T(8,128)(2,1)S(1)}, u32[]{:S(2)}, u32[]{:S(2)}) collective-permute-start(bf16[1,80,512]{2,1,0:T(8,128)(2,1)S(1)} %get-tuple-element.62), channel_id=1, source_target_pairs={{0,4},{1,5},{2,6},{3,7},{4,0},{5,1},{6,2},{7,3},{8,12},{9,13},{10,... | collective-permute-start | bytes 245768 | tf_op jit(solution)/shard_map/ppermute | solution.py:339
  93.3 7.3 %collective-permute-done.10.landed_ref = bf16[1,80,512]{2,1,0:T(8,128)(2,1)S(1)} collective-permute-done((bf16[1,80,512]{2,1,0:T(8,128)(2,1)S(1)}, bf16[1,80,512]{2,1,0:T(8,128)(2,1)S(1)}, u32[]{:S(2)}, u32[]{:S(2)}) %collective-permute-start.10) | collective-permute-done | bytes 81952 | tf_op jit(solution)/shard_map/ppermute | solution.py:339
  100.6 1.2 %shard_map.143 = (bf16[64,512]{1,0:T(8,128)(2,1)}, bf16[512,512]{1,0:T(8,128)(2,1)}, f32[1,64]{1,0:T(1,128)}) custom-call(s32[1]{0:T(128)S(6)} %copy.15.count_ref, bf16[1,80,512]{2,1,0:T(8,128)(2,1)S(1)} %get-tuple-element.63.own_ref, bf16[1,80,512]{2,1,0:T(8,128)(2,1)S(1)} %collective-permute-done.10.landed_ref, f32[1,64]{1,0:T(1,128)S(1)} %bitcast.15, ...), custom_call_target="tpu_custom_call" | custom-call | tf_op jit(solution)/shard_map/pallas_call | solution.py:443
  (30 shorter events, 4.8 us)
Async XLA Ops:
  0.6 51.2 %copy-start.2 = (s32[64]{0:T(128)S(1)}, s32[64]{0:T(128)}, u32[]{:S(2)}) copy-start(s32[64]{0:T(128)} %param.14) | copy-start | bytes 772
  0.6 15.5 %collective-permute-start.1 = (bf16[1,64,512]{2,1,0:T(8,128)(2,1)}, bf16[1,64,512]{2,1,0:T(8,128)(2,1)S(1)}, u32[]{:S(2)}, u32[]{:S(2)}) collective-permute-start(bf16[1,64,512]{2,1,0:T(8,128)(2,1)} %bitcast.16), channel_id=1, source_target_pairs={{0,4},{1,5},{2,6},{3,7},{4,0},{5,1},{6,2},{7,3},{8,12},{9,13},{10,... | collective-permute-start | bytes 196616 | tf_op jit(solution)/shard_map/ppermute | solution.py:339
  16.2 35.6 %all-to-all-start = ((bf16[32,128,128]{2,1,0:T(8,128)(2,1)}), bf16[32,128,128]{2,1,0:T(8,128)(2,1)S(1)}, u32[]{:S(2)}, u32[]{:S(2)}) async-start(bf16[32,128,128]{2,1,0:T(8,128)(2,1)} %get-tuple-element.41), calls=%async_computation | async-start | bytes 2097152 | tf_op jit(solution)/shard_map/all_to_all | solution.py:328
  26.7 15.4 %collective-permute-start.4 = (bf16[2,64,512]{2,1,0:T(8,128)(2,1)S(1)}, bf16[2,64,512]{2,1,0:T(8,128)(2,1)S(1)}, u32[]{:S(2)}, u32[]{:S(2)}) collective-permute-start(bf16[2,64,512]{2,1,0:T(8,128)(2,1)S(1)} %pad_maximum_fusion.pair_ref), channel_id=1, source_target_pairs={{0,7},{1,0},{2,1},{3,2},{4,3},{5,4},{6,5},{7,6},{8,9},{9,10},{10,1... | collective-permute-start | bytes 393224 | tf_op jit(solution)/shard_map/ppermute | solution.py:339
  29.8 12.3 %collective-permute-start.3 = (bf16[2,64,512]{2,1,0:T(8,128)(2,1)S(1)}, bf16[2,64,512]{2,1,0:T(8,128)(2,1)S(1)}, u32[]{:S(2)}, u32[]{:S(2)}) collective-permute-start(bf16[2,64,512]{2,1,0:T(8,128)(2,1)S(1)} %pad_maximum_fusion.pair_ref), channel_id=1, source_target_pairs={{0,2},{1,3},{2,4},{3,5},{4,6},{5,7},{6,0},{7,1},{8,14},{9,15},{10,... | collective-permute-start | bytes 393224 | tf_op jit(solution)/shard_map/ppermute | solution.py:339
  35.2 6.9 %collective-permute-start.2 = (bf16[2,64,512]{2,1,0:T(8,128)(2,1)S(1)}, bf16[2,64,512]{2,1,0:T(8,128)(2,1)S(1)}, u32[]{:S(2)}, u32[]{:S(2)}) collective-permute-start(bf16[2,64,512]{2,1,0:T(8,128)(2,1)S(1)} %pad_maximum_fusion.pair_ref), channel_id=1, source_target_pairs={{0,1},{1,2},{2,3},{3,4},{4,5},{5,6},{6,7},{7,0},{8,15},{9,8},{10,9... | collective-permute-start | bytes 393224 | tf_op jit(solution)/shard_map/ppermute | solution.py:339
  38.6 0.8 copy-start.1
  39.4 0.7 copy-start.3
  40.2 5.3 %collective-permute-start = (bf16[64,512]{1,0:T(8,128)(2,1)S(1)}, bf16[64,512]{1,0:T(8,128)(2,1)S(1)}, u32[]{:S(2)}, u32[]{:S(2)}) collective-permute-start(bf16[64,512]{1,0:T(8,128)(2,1)S(1)} %get-tuple-element.36.own_ref), channel_id=1, source_target_pairs={{0,8},{8,0},{16,24},{24,16},{32,40},{40,32},{48,56},{56,48},{64,72... | collective-permute-start | bytes 196616 | tf_op jit(solution)/shard_map/ppermute | solution.py:331
  54.2 6.3 %collective-permute-start.5 = (f32[200,512]{1,0:T(8,128)S(1)}, f32[200,512]{1,0:T(8,128)S(1)}, u32[]{:S(2)}, u32[]{:S(2)}) collective-permute-start(f32[200,512]{1,0:T(8,128)S(1)} %get-tuple-element.42.own_part), channel_id=1, source_target_pairs={{0,8},{8,0},{16,24},{24,16},{32,40},{40,32},{48,56},{56,48},{64,72... | collective-permute-start | bytes 1228808 | tf_op jit(solution)/shard_map/ppermute | solution.py:331
  63.4 37.2 %copy-start = (bf16[512,512]{1,0:T(8,128)(2,1)S(1)}, bf16[512,512]{1,0:T(8,128)(2,1)}, u32[]{:S(2)}) copy-start(bf16[512,512]{1,0:T(8,128)(2,1)} %hidden_ref.1) | copy-start | bytes 1572868
  63.4 37.2 %copy-start.4 = (f32[64]{0:T(128)S(1)}, f32[64]{0:T(128)}, u32[]{:S(2)}) copy-start(f32[64]{0:T(128)} %param.13) | copy-start | bytes 772
  63.4 38.3 %all-to-all-start.1 = ((bf16[32,128,128]{2,1,0:T(8,128)(2,1)}), bf16[32,128,128]{2,1,0:T(8,128)(2,1)S(1)}, u32[]{:S(2)}, u32[]{:S(2)}) async-start(bf16[32,128,128]{2,1,0:T(8,128)(2,1)} %get-tuple-element.57), calls=%async_computation.1 | async-start | bytes 2097152 | tf_op jit(solution)/shard_map/all_to_all | solution.py:328
  72.2 16.9 %collective-permute-start.6 = (bf16[2,80,512]{2,1,0:T(8,128)(2,1)S(1)}, bf16[2,80,512]{2,1,0:T(8,128)(2,1)S(1)}, u32[]{:S(2)}, u32[]{:S(2)}) collective-permute-start(bf16[2,80,512]{2,1,0:T(8,128)(2,1)S(1)} %get-tuple-element.47), channel_id=1, source_target_pairs={{0,7},{1,0},{2,1},{3,2},{4,3},{5,4},{6,5},{7,6},{8,9},{9,10},{10,1... | collective-permute-start | bytes 491528 | tf_op jit(solution)/shard_map/ppermute | solution.py:339
  75.3 13.8 %collective-permute-start.7 = (bf16[2,80,512]{2,1,0:T(8,128)(2,1)S(1)}, bf16[2,80,512]{2,1,0:T(8,128)(2,1)S(1)}, u32[]{:S(2)}, u32[]{:S(2)}) collective-permute-start(bf16[2,80,512]{2,1,0:T(8,128)(2,1)S(1)} %get-tuple-element.48), channel_id=1, source_target_pairs={{0,6},{1,7},{2,0},{3,1},{4,2},{5,3},{6,4},{7,5},{8,10},{9,11},{10,... | collective-permute-start | bytes 491528 | tf_op jit(solution)/shard_map/ppermute | solution.py:339
  79.4 9.8 %collective-permute-start.8 = (bf16[2,80,512]{2,1,0:T(8,128)(2,1)S(1)}, bf16[2,80,512]{2,1,0:T(8,128)(2,1)S(1)}, u32[]{:S(2)}, u32[]{:S(2)}) collective-permute-start(bf16[2,80,512]{2,1,0:T(8,128)(2,1)S(1)} %get-tuple-element.49), channel_id=1, source_target_pairs={{0,1},{1,2},{2,3},{3,4},{4,5},{5,6},{6,7},{7,0},{8,15},{9,8},{10,9... | collective-permute-start | bytes 491528 | tf_op jit(solution)/shard_map/ppermute | solution.py:339
  82.8 5.6 %collective-permute-start.9 = (bf16[256,128]{1,0:T(8,128)(2,1)S(1)}, bf16[256,128]{1,0:T(8,128)(2,1)S(1)}, u32[]{:S(2)}, u32[]{:S(2)}) collective-permute-start(bf16[256,128]{1,0:T(8,128)(2,1)S(1)} %get-tuple-element.51), channel_id=1, source_target_pairs={{0,8},{8,0},{16,24},{24,16},{32,40},{40,32},{48,56},{56,48},{64,72... | collective-permute-start | bytes 196616 | tf_op jit(solution)/shard_map/ppermute | solution.py:331
  89.2 11.3 %collective-permute-start.10 = (bf16[1,80,512]{2,1,0:T(8,128)(2,1)S(1)}, bf16[1,80,512]{2,1,0:T(8,128)(2,1)S(1)}, u32[]{:S(2)}, u32[]{:S(2)}) collective-permute-start(bf16[1,80,512]{2,1,0:T(8,128)(2,1)S(1)} %get-tuple-element.62), channel_id=1, source_target_pairs={{0,4},{1,5},{2,6},{3,7},{4,0},{5,1},{6,2},{7,3},{8,12},{9,13},{10,... | collective-permute-start | bytes 245768 | tf_op jit(solution)/shard_map/ppermute | solution.py:339

commit v6 on v5

--- a/solution.py
+++ b/solution.py
@@ -59,11 +59,9 @@
     return jnp.concatenate([field[:, h * HD : (h + 1) * HD].astype(F32) for h in range(heads)], axis=0)
 
 
-def payload_kernel(place_ref, count_ref, pair_ref, frequency_ref, pay_ref, copies_ref, cos_ref, sin_ref, stage, sems):
+def payload_kernel(count_ref, pair_ref, position_ref, frequency_ref, pay_ref, copies_ref, cos_ref, sin_ref, stage, sems):
     slots = cos_ref.shape[0]
-    index = pair_ref[2 * slots : 2 * slots + 8, 0:slots].astype(F32)
-    position = 2.0 * index[0:1] + index[1:2] + (place_ref[0] * TOK_DEV).astype(F32)
-    angles = as_column(position) * frequency_ref[...]
+    angles = as_column(position_ref[...]) * frequency_ref[...]
     col_ids = lax.broadcasted_iota(jnp.int32, (slots, HD), 1)
     row_ids = lax.broadcasted_iota(jnp.int32, (slots, HD), 0)
     cos_full = jnp.cos(angles)
@@ -149,9 +147,9 @@
         blocks = pl.ds(group * chunk, chunk)
         scores = matmul(piece_ref[blocks, 0:slots, :].reshape(keys, HD), query_t, ((1,), (0,)))
         for i in range(chunk):
-            chip = group * chunk + i
+            chip = i * groups + group
             reach = jnp.where(chip < my_chip, 0.0, LOWEST)
-            first = piece_ref[chip, slots : 2 * slots, 0:1].astype(F32)
+            first = piece_ref[group * chunk + i, slots : 2 * slots, 0:1].astype(F32)
             bias = jnp.where(first > DEAD_LIMIT, LOWEST, reach)
             block = scores[i * slots : (i + 1) * slots, :] + bias
             score_ref[group, i * slots : (i + 1) * slots, :] = block
@@ -161,8 +159,8 @@
     own_scores = matmul(own_keys, query_t, ((1,), (0,)))
     own_scores = jnp.where(index_col <= limit_row, own_scores, LOWEST)
     own_scores = own_scores + jnp.where(own_values[:, 0:1].astype(F32) > DEAD_LIMIT, LOWEST, 0.0)
-    own_at = pl.ds(pl.multiple_of(lax.rem(my_chip, chunk) * slots, slots), slots)
-    score_ref[pl.ds(lax.div(my_chip, chunk), 1), own_at, :] = own_scores[None]
+    own_at = pl.ds(pl.multiple_of(lax.div(my_chip, groups) * slots, slots), slots)
+    score_ref[pl.ds(lax.rem(my_chip, groups), 1), own_at, :] = own_scores[None]
     peak = jnp.maximum(peak, jnp.max(own_scores, axis=0, keepdims=True))
 
     total = jnp.zeros((1, rows), F32)
@@ -264,6 +262,10 @@
     return total
 
 
+def sum_kernel(stack_ref, out_ref):
+    out_ref[...] = added_up(stack_ref).astype(BF16)
+
+
 def update_kernel(count_ref, own_ref, landed_ref, logit_ref, index_ref, hidden_ref, update_ref, after_ref, grad_ref):
     slots = update_ref.shape[0]
     tokens = hidden_ref.shape[0]
@@ -321,10 +323,15 @@
     heads = width // HD
     rows = nc * heads * slots
     blocks = ny * nx
-    chunk = min(8, blocks)
-
-    def exchange(array):
-        groups = [[chip * nc + core for chip in range(blocks)] for core in range(nc)]
+
+    def at(y, x, c):
+        return (y * nx + x) * nc + c
+
+    y_groups = [[at(y, x, c) for y in range(ny)] for x in range(nx) for c in range(nc)]
+    all_groups = [[at(y, x, c) for x in range(nx) for y in range(ny)] for c in range(nc)]
+    x_groups = [[at(y, x, c) for x in range(nx)] for y in range(ny) for c in range(nc)]
+
+    def exchange(array, groups):
         return lax.all_to_all(array, "ctx", 0, 0, axis_index_groups=groups, tiled=True)
 
     def to_sibling(array):
@@ -344,8 +351,6 @@
     my_shard = lax.axis_index("ctx").astype(jnp.int32)
     place = jnp.stack([my_shard, lax.axis_index("tp").astype(jnp.int32)])
     index_row = chosen_index[None, :]
-    index_rows = jnp.stack([chosen_index // 2, chosen_index % 2]).astype(BF16)
-    index_rows = jnp.pad(index_rows, ((0, 14), (0, HD - slots)))
     logit_row = router_logit[None, :]
     half = jnp.arange(HD // 2, dtype=F32)
     frequency = ROTARY_BASE ** (-(half * 2.0 / HD))
@@ -359,18 +364,17 @@
             jax.ShapeDtypeStruct((slots, HD), F32),
             jax.ShapeDtypeStruct((slots, HD), F32),
         ],
-        [SMEM] * 2 + [VMEM] * 2,
-        [pltpu.VMEM((chunk, 2 * slots, HD), BF16), pltpu.SemaphoreType.DMA((blocks // chunk,))],
+        [SMEM] + [VMEM] * 3,
+        [pltpu.VMEM((ny, 2 * slots, HD), BF16), pltpu.SemaphoreType.DMA((nx,))],
         out_specs=[VMEM, HBM, VMEM, VMEM],
     )(
-        place,
         chosen_count,
-        jnp.concatenate([key_vectors, value_vectors, index_rows], axis=0),
+        jnp.concatenate([key_vectors, value_vectors], axis=0),
+        (my_shard * TOK_DEV + chosen_index).astype(F32)[None, :],
         frequency,
     )
     first_arrival = tp_send(out_cotangent[None], tp_count // 2)
-    payloads, first_arrival = lax.optimization_barrier((payloads, first_arrival))
-    pieces = exchange(payloads)
+    pieces = exchange(payloads, all_groups)
 
     own_queries, gate = call(
         query_kernel,
@@ -393,7 +397,7 @@
         limit=50,
     )(place, out_weight, gate, *cot)
 
-    scored = (blocks // chunk, chunk * slots, rows)
+    scored = (nx, ny * slots, rows)
     part, weights = call(
         forward_kernel,
         [
@@ -414,10 +418,12 @@
             jax.ShapeDtypeStruct((blocks, 2 * slots, HD), BF16),
         ],
         [VMEM] * 7,
-        [pltpu.VMEM((blocks, 2 * slots, HD), BF16), pltpu.SemaphoreType.DMA((blocks // chunk,))],
+        [pltpu.VMEM((blocks, 2 * slots, HD), BF16), pltpu.SemaphoreType.DMA((nx,))],
         out_specs=[VMEM] * 4 + [HBM],
     )(part, sibling_part, own_queries, sibling_queries, grad_attention, weights, pieces)
-    landed = exchange(outs)
+    crossed = exchange(outs.reshape(nx, ny, 2 * slots, HD), x_groups)
+    stacked = call(sum_kernel, jax.ShapeDtypeStruct((ny, 2 * slots, HD), BF16), [VMEM])(crossed)
+    landed = exchange(stacked, y_groups)
 
     shares = call(
         projection_kernel,
@@ -431,10 +437,10 @@
         query_grad_kernel, jax.ShapeDtypeStruct((slots, width), BF16), [VMEM] * 4
     )(cos_full, sin_signed, dq_own, dq_arrived)
     arrived = [tp_send(share, -shift) for share, shift in zip(shares[1:], tp_shifts(tp_count))]
-    arrived, grad_queries = lax.optimization_barrier((arrived, grad_queries))
     shares = functools.reduce(jnp.add, [part.astype(F32) for part in [shares[0]] + arrived]).astype(BF16)
-    near = shares[:1]
-    arrived = tp_send(shares[1:], -(tp_count // 2))
+    near, far = shares[:1], shares[1:]
+    far, _ = lax.optimization_barrier((far, stacked))
+    arrived = tp_send(far, -(tp_count // 2))
 
     grad_keys, grad_values = call(
         finish_kernel, [jax.ShapeDtypeStruct((slots, HD), BF16)] * 2, [VMEM] * 3

time: 103 us -> 99.9 us (0.970); the launches traced: 103 us -> 98.4 us
  waiting for transfers between devices: 15.8 us -> 6.7 us
  starting transfers between devices: 64.6 us -> 69.4 us
    all_to_all x2 -> x3, starting transfers between devices: 15.1 us -> 21.2 us  [exchange(): lax.all_to_all(array, 'ctx', 0, 0, axis_index_groups=groups, tiled=True)]
    ppermute x8, waiting for transfers between devices: 7.3 us -> 2.16 us  [tp_send(): return lax.ppermute(array, ('ctx', 'tp'), pairs)]
    all_to_all x2 -> x3, waiting for transfers between devices: 6.31 us -> 2.31 us  [exchange(): lax.all_to_all(array, 'ctx', 0, 0, axis_index_groups=groups, tiled=True)]
  transfers between devices with their start and end apart: 13 -> 14, of which waited for: 4 -> 4; matrix products, arithmetic and copies ran while one was open for 2% -> 1% of each run, Pallas kernels for 10% -> 10%
where the time goes in v6:
time: 99.9 us; the launch traced here: 98.4 us
  starting transfers between devices  69.4 us (69%)
  Pallas kernels  16.7 us (17%)
  waiting for transfers between devices  6.7 us (7%)
  other arithmetic  2.5 us (3%)
  between operations  1.53 us (2%)
  local copies, waits for them, and re-layouts  1.52 us (2%)
    ppermute x8, starting transfers between devices, tp_send(): return lax.ppermute(array, ('ctx', 'tp'), pairs)  37.3 us
    all_to_all x3, starting transfers between devices, exchange(): lax.all_to_all(array, 'ctx', 0, 0, axis_index_groups=groups, tiled=True)  21.2 us
    ppermute x3, starting transfers between devices, to_sibling(): return lax.ppermute(array, 'ctx', [(i, i ^ 1) for i in range(ny * nx * nc)])  11 us
    pallas_call x1, Pallas kernels, on_device(): call(projection_kernel, [jax.ShapeDtypeStruct((2, slots + 16, width), BF1...  3.34 us
    pallas_call x1, Pallas kernels, on_device(): call(cotangent_kernel, jax.ShapeDtypeStruct((slots, width), BF16), [SMEM,...  3.3 us
    pallas_call x1, Pallas kernels, on_device(): call(backward_kernel, [jax.ShapeDtypeStruct((slots, width), BF16), jax.Sh...  2.87 us
    pallas_call x1, Pallas kernels, on_device(): call(forward_kernel, [jax.ShapeDtypeStruct((HD + 8 + slots, rows), F32),...  2.38 us
    all_to_all x3, waiting for transfers between devices, exchange(): lax.all_to_all(array, 'ctx', 0, 0, axis_index_groups=groups, tiled=True)  2.31 us
  transfers between devices with their start and end apart: 14, of which 4 were waited for; matrix products, arithmetic and copies ran while one was open for 1% of the time, Pallas kernels for 10%

profile of v6, /device:TPU:1, one launch (start us, length us, event | category | flops | bytes accessed | tf_op | source)
XLA Modules:
  0.0 98.4 jit_solution(935538532160942496)
XLA Ops:
  2.8 1.2 %shard_map.136 = (bf16[128,128]{1,0:T(8,128)(2,1)S(1)}, bf16[32,128,128]{2,1,0:T(8,128)(2,1)}, f32[64,128]{1,0:T(8,128)S(1)}, f32[64,128]{1,0:T(8,128)S(1)}) custom-call(s32[1]{0:T(128)S(6)} %copy.15.count_ref, bf16[128,128]{1,0:T(8,128)(2,1)S(1)} %pad_maximum_fusion.1.pair_ref, f32[1,64]{1,0:T(1,128)S(1)} %convert_bitcast_fusion.position_ref, ...), custom_call_target="tpu_custom_call" | custom-call | tf_op jit(solution)/shard_map/pallas_call | solution.py:359
  4.0 10.5 %all-to-all-start = ((bf16[32,128,128]{2,1,0:T(8,128)(2,1)}), bf16[32,128,128]{2,1,0:T(8,128)(2,1)S(1)}, u32[]{:S(2)}, u32[]{:S(2)}) async-start(bf16[32,128,128]{2,1,0:T(8,128)(2,1)} %get-tuple-element.34), calls=%async_computation | async-start | bytes 2097152 | tf_op jit(solution)/shard_map/all_to_all | solution.py:335
  14.6 10.6 %collective-permute-start.1 = (bf16[1,64,512]{2,1,0:T(8,128)(2,1)}, bf16[1,64,512]{2,1,0:T(8,128)(2,1)S(1)}, u32[]{:S(2)}, u32[]{:S(2)}) collective-permute-start(bf16[1,64,512]{2,1,0:T(8,128)(2,1)} %bitcast.15), channel_id=1, source_target_pairs={{0,4},{1,5},{2,6},{3,7},{4,0},{5,1},{6,2},{7,3},{8,12},{9,13},{10,... | collective-permute-start | bytes 196616 | tf_op jit(solution)/shard_map/ppermute | solution.py:346
  25.2 2.1 %collective-permute-done.1 = bf16[1,64,512]{2,1,0:T(8,128)(2,1)S(1)} collective-permute-done((bf16[1,64,512]{2,1,0:T(8,128)(2,1)}, bf16[1,64,512]{2,1,0:T(8,128)(2,1)S(1)}, u32[]{:S(2)}, u32[]{:S(2)}) %collective-permute-start.1) | collective-permute-done | bytes 65568 | tf_op jit(solution)/shard_map/ppermute | solution.py:346
  28.2 3.1 %collective-permute-start.4 = (bf16[2,64,512]{2,1,0:T(8,128)(2,1)S(1)}, bf16[2,64,512]{2,1,0:T(8,128)(2,1)S(1)}, u32[]{:S(2)}, u32[]{:S(2)}) collective-permute-start(bf16[2,64,512]{2,1,0:T(8,128)(2,1)S(1)} %pad_maximum_fusion.pair_ref), channel_id=1, source_target_pairs={{0,7},{1,0},{2,1},{3,2},{4,3},{5,4},{6,5},{7,6},{8,9},{9,10},{10,1... | collective-permute-start | bytes 393224 | tf_op jit(solution)/shard_map/ppermute | solution.py:346
  31.3 7.1 %collective-permute-start.3 = (bf16[2,64,512]{2,1,0:T(8,128)(2,1)S(1)}, bf16[2,64,512]{2,1,0:T(8,128)(2,1)S(1)}, u32[]{:S(2)}, u32[]{:S(2)}) collective-permute-start(bf16[2,64,512]{2,1,0:T(8,128)(2,1)S(1)} %pad_maximum_fusion.pair_ref), channel_id=1, source_target_pairs={{0,2},{1,3},{2,4},{3,5},{4,6},{5,7},{6,0},{7,1},{8,14},{9,15},{10,... | collective-permute-start | bytes 393224 | tf_op jit(solution)/shard_map/ppermute | solution.py:346
  38.4 2.8 %collective-permute-start.2 = (bf16[2,64,512]{2,1,0:T(8,128)(2,1)S(1)}, bf16[2,64,512]{2,1,0:T(8,128)(2,1)S(1)}, u32[]{:S(2)}, u32[]{:S(2)}) collective-permute-start(bf16[2,64,512]{2,1,0:T(8,128)(2,1)S(1)} %pad_maximum_fusion.pair_ref), channel_id=1, source_target_pairs={{0,1},{1,2},{2,3},{3,4},{4,5},{5,6},{6,7},{7,0},{8,15},{9,8},{10,9... | collective-permute-start | bytes 393224 | tf_op jit(solution)/shard_map/ppermute | solution.py:346
  42.8 2.2 %collective-permute-start = (bf16[64,512]{1,0:T(8,128)(2,1)S(1)}, bf16[64,512]{1,0:T(8,128)(2,1)S(1)}, u32[]{:S(2)}, u32[]{:S(2)}) collective-permute-start(bf16[64,512]{1,0:T(8,128)(2,1)S(1)} %get-tuple-element.31.own_ref), channel_id=1, source_target_pairs={{0,8},{8,0},{16,24},{24,16},{32,40},{40,32},{48,56},{56,48},{64,72... | collective-permute-start | bytes 196616 | tf_op jit(solution)/shard_map/ppermute | solution.py:338
  45.1 3.3 %shard_map.138.grad_ref = bf16[64,512]{1,0:T(8,128)(2,1)S(1)} custom-call(s32[2]{0:T(128)S(1)} %pad_add_fusion.place_ref, bf16[512,4096]{1,0:T(8,128)(2,1)} %weight_ref.3, f32[64,128]{1,0:T(8,128)S(1)} %get-tuple-element.32.gate_ref, bf16[2,64,512]{2,1,0:T(8,128)(2,1)S(1)} %pad_maximum_fusion.pair_ref, ...), custom_call_target="tpu_custom_call" | custom-call | tf_op jit(solution)/shard_map/pallas_call | solution.py:392
  48.4 2.4 %shard_map.139 = (f32[200,512]{1,0:T(8,128)S(1)}, bf16[4,512,512]{2,1,0:T(8,128)(2,1)S(1)}) custom-call(s32[2]{0:T(128)S(1)} %pad_add_fusion.place_ref, s32[1,64]{1,0:T(1,128)S(1)} %bitcast.11, bf16[64,512]{1,0:T(8,128)(2,1)S(1)} %get-tuple-element.31.own_ref, bf16[64,512]{1,0:T(8,128)(2,1)S(1)} %collective-permute-done.sibling_ref, ...), custom_call_target="tpu_custom_call" | custom-call | tf_op jit(solution)/shard_map/pallas_call | solution.py:401
  50.8 4.8 %collective-permute-start.5 = (f32[200,512]{1,0:T(8,128)S(1)}, f32[200,512]{1,0:T(8,128)S(1)}, u32[]{:S(2)}, u32[]{:S(2)}) collective-permute-start(f32[200,512]{1,0:T(8,128)S(1)} %get-tuple-element.35.own_part), channel_id=1, source_target_pairs={{0,8},{8,0},{16,24},{24,16},{32,40},{40,32},{48,56},{56,48},{64,72... | collective-permute-start | bytes 1228808 | tf_op jit(solution)/shard_map/ppermute | solution.py:338
  55.6 1.4 %collective-permute-done.5.sibling_part = f32[200,512]{1,0:T(8,128)S(1)} collective-permute-done((f32[200,512]{1,0:T(8,128)S(1)}, f32[200,512]{1,0:T(8,128)S(1)}, u32[]{:S(2)}, u32[]{:S(2)}) %collective-permute-start.5) | collective-permute-done | bytes 409632 | tf_op jit(solution)/shard_map/ppermute | solution.py:338
  57.0 2.9 %shard_map.140 = (bf16[64,512]{1,0:T(8,128)(2,1)S(1)}, f32[8,256]{1,0:T(8,128)S(1)}, f32[256,128]{1,0:T(8,128)S(1)}, bf16[256,128]{1,0:T(8,128)(2,1)S(1)}, bf16[32,128,128]{2,1,0:T(8,128)(2,1)}) custom-call(f32[200,512]{1,0:T(8,128)S(1)} %get-tuple-element.35.own_part, f32[200,512]{1,0:T(8,128)S(1)} %collective-permute-done.5.sibling_part, ...), custom_call_target="tpu_custom_call" | custom-call | tf_op jit(solution)/shard_map/pallas_call | solution.py:411
  59.8 4.3 %all-to-all-start.1 = ((bf16[4,8,128,128]{3,2,1,0:T(8,128)(2,1)}), bf16[4,8,128,128]{3,2,1,0:T(8,128)(2,1)S(1)}, u32[]{:S(2)}, u32[]{:S(2)}) async-start(bf16[4,8,128,128]{3,2,1,0:T(8,128)(2,1)} %bitcast.7), calls=%async_computation.1 | async-start | bytes 2097152 | tf_op jit(solution)/shard_map/all_to_all | solution.py:335
  64.2 3.3 %shard_map.141 = (bf16[2,80,512]{2,1,0:T(8,128)(2,1)S(1)}, bf16[2,80,512]{2,1,0:T(8,128)(2,1)S(1)}, bf16[2,80,512]{2,1,0:T(8,128)(2,1)S(1)}, bf16[2,80,512]{2,1,0:T(8,128)(2,1)S(1)}) custom-call(s32[2]{0:T(128)S(1)} %pad_add_fusion.place_ref, bf16[512,4096]{1,0:T(8,128)(2,1)} %weight_ref.3, bf16[64,512]{1,0:T(8,128)(2,1)S(1)} %get-tuple-element.37.att_ref, ...), custom_call_target="tpu_custom_call" | custom-call | tf_op jit(solution)/shard_map/pallas_call | solution.py:428
  67.5 1.9 %collective-permute-start.6 = (bf16[2,80,512]{2,1,0:T(8,128)(2,1)S(1)}, bf16[2,80,512]{2,1,0:T(8,128)(2,1)S(1)}, u32[]{:S(2)}, u32[]{:S(2)}) collective-permute-start(bf16[2,80,512]{2,1,0:T(8,128)(2,1)S(1)} %get-tuple-element.40), channel_id=1, source_target_pairs={{0,7},{1,0},{2,1},{3,2},{4,3},{5,4},{6,5},{7,6},{8,9},{9,10},{10,1... | collective-permute-start | bytes 491528 | tf_op jit(solution)/shard_map/ppermute | solution.py:346
  69.4 3.5 %collective-permute-start.7 = (bf16[2,80,512]{2,1,0:T(8,128)(2,1)S(1)}, bf16[2,80,512]{2,1,0:T(8,128)(2,1)S(1)}, u32[]{:S(2)}, u32[]{:S(2)}) collective-permute-start(bf16[2,80,512]{2,1,0:T(8,128)(2,1)S(1)} %get-tuple-element.41), channel_id=1, source_target_pairs={{0,6},{1,7},{2,0},{3,1},{4,2},{5,3},{6,4},{7,5},{8,10},{9,11},{10,... | collective-permute-start | bytes 491528 | tf_op jit(solution)/shard_map/ppermute | solution.py:346
  73.0 3.4 %collective-permute-start.8 = (bf16[2,80,512]{2,1,0:T(8,128)(2,1)S(1)}, bf16[2,80,512]{2,1,0:T(8,128)(2,1)S(1)}, u32[]{:S(2)}, u32[]{:S(2)}) collective-permute-start(bf16[2,80,512]{2,1,0:T(8,128)(2,1)S(1)} %get-tuple-element.42), channel_id=1, source_target_pairs={{0,1},{1,2},{2,3},{3,4},{4,5},{5,6},{6,7},{7,0},{8,15},{9,8},{10,9... | collective-permute-start | bytes 491528 | tf_op jit(solution)/shard_map/ppermute | solution.py:346
  76.4 2.3 %all-to-all-done.1.stack_ref = bf16[4,8,128,128]{3,2,1,0:T(8,128)(2,1)S(1)} async-done(((bf16[4,8,128,128]{3,2,1,0:T(8,128)(2,1)}), bf16[4,8,128,128]{3,2,1,0:T(8,128)(2,1)S(1)}, u32[]{:S(2)}, u32[]{:S(2)}) %all-to-all-start.1) | async-done | bytes 1048608 | tf_op jit(solution)/shard_map/all_to_all | solution.py:335
  79.5 6.4 %all-to-all-start.2 = ((bf16[8,128,128]{2,1,0:T(8,128)(2,1)}), bf16[8,128,128]{2,1,0:T(8,128)(2,1)S(1)}, u32[]{:S(2)}, u32[]{:S(2)}) async-start(bf16[8,128,128]{2,1,0:T(8,128)(2,1)} %shard_map.142), calls=%async_computation.2 | async-start | bytes 524288 | tf_op jit(solution)/shard_map/all_to_all | solution.py:335
  86.0 4.8 %collective-permute-start.9 = (bf16[1,80,512]{2,1,0:T(8,128)(2,1)S(1)}, bf16[1,80,512]{2,1,0:T(8,128)(2,1)S(1)}, u32[]{:S(2)}, u32[]{:S(2)}) collective-permute-start(bf16[1,80,512]{2,1,0:T(8,128)(2,1)S(1)} %get-tuple-element.44), channel_id=1, source_target_pairs={{0,4},{1,5},{2,6},{3,7},{4,0},{5,1},{6,2},{7,3},{8,12},{9,13},{10,... | collective-permute-start | bytes 245768 | tf_op jit(solution)/shard_map/ppermute | solution.py:346
  90.9 4.0 %collective-permute-start.10 = (bf16[256,128]{1,0:T(8,128)(2,1)S(1)}, bf16[256,128]{1,0:T(8,128)(2,1)S(1)}, u32[]{:S(2)}, u32[]{:S(2)}) collective-permute-start(bf16[256,128]{1,0:T(8,128)(2,1)S(1)} %get-tuple-element.47), channel_id=1, source_target_pairs={{0,8},{8,0},{16,24},{24,16},{32,40},{40,32},{48,56},{56,48},{64,72... | collective-permute-start | bytes 196616 | tf_op jit(solution)/shard_map/ppermute | solution.py:338
  94.9 0.9 collective-permute-done.10.arrived_ref
  96.5 1.2 %shard_map.143 = (bf16[64,512]{1,0:T(8,128)(2,1)}, bf16[512,512]{1,0:T(8,128)(2,1)}, f32[1,64]{1,0:T(1,128)}) custom-call(s32[1]{0:T(128)S(6)} %copy.15.count_ref, bf16[1,80,512]{2,1,0:T(8,128)(2,1)S(1)} %get-tuple-element.53.own_ref, bf16[1,80,512]{2,1,0:T(8,128)(2,1)S(1)} %collective-permute-done.9.landed_ref, f32[1,64]{1,0:T(1,128)S(1)} %bitcast.14, ...), custom_call_target="tpu_custom_call" | custom-call | tf_op jit(solution)/shard_map/pallas_call | solution.py:449
  (32 shorter events, 6.4 us)
Async XLA Ops:
  0.6 47.8 %copy-start.2 = (s32[64]{0:T(128)S(1)}, s32[64]{0:T(128)}, u32[]{:S(2)}) copy-start(s32[64]{0:T(128)} %param.14) | copy-start | bytes 772
  4.0 44.4 %all-to-all-start = ((bf16[32,128,128]{2,1,0:T(8,128)(2,1)}), bf16[32,128,128]{2,1,0:T(8,128)(2,1)S(1)}, u32[]{:S(2)}, u32[]{:S(2)}) async-start(bf16[32,128,128]{2,1,0:T(8,128)(2,1)} %get-tuple-element.34), calls=%async_computation | async-start | bytes 2097152 | tf_op jit(solution)/shard_map/all_to_all | solution.py:335
  14.6 12.8 %collective-permute-start.1 = (bf16[1,64,512]{2,1,0:T(8,128)(2,1)}, bf16[1,64,512]{2,1,0:T(8,128)(2,1)S(1)}, u32[]{:S(2)}, u32[]{:S(2)}) collective-permute-start(bf16[1,64,512]{2,1,0:T(8,128)(2,1)} %bitcast.15), channel_id=1, source_target_pairs={{0,4},{1,5},{2,6},{3,7},{4,0},{5,1},{6,2},{7,3},{8,12},{9,13},{10,... | collective-permute-start | bytes 196616 | tf_op jit(solution)/shard_map/ppermute | solution.py:346
  28.2 16.9 %collective-permute-start.4 = (bf16[2,64,512]{2,1,0:T(8,128)(2,1)S(1)}, bf16[2,64,512]{2,1,0:T(8,128)(2,1)S(1)}, u32[]{:S(2)}, u32[]{:S(2)}) collective-permute-start(bf16[2,64,512]{2,1,0:T(8,128)(2,1)S(1)} %pad_maximum_fusion.pair_ref), channel_id=1, source_target_pairs={{0,7},{1,0},{2,1},{3,2},{4,3},{5,4},{6,5},{7,6},{8,9},{9,10},{10,1... | collective-permute-start | bytes 393224 | tf_op jit(solution)/shard_map/ppermute | solution.py:346
  31.3 13.8 %collective-permute-start.3 = (bf16[2,64,512]{2,1,0:T(8,128)(2,1)S(1)}, bf16[2,64,512]{2,1,0:T(8,128)(2,1)S(1)}, u32[]{:S(2)}, u32[]{:S(2)}) collective-permute-start(bf16[2,64,512]{2,1,0:T(8,128)(2,1)S(1)} %pad_maximum_fusion.pair_ref), channel_id=1, source_target_pairs={{0,2},{1,3},{2,4},{3,5},{4,6},{5,7},{6,0},{7,1},{8,14},{9,15},{10,... | collective-permute-start | bytes 393224 | tf_op jit(solution)/shard_map/ppermute | solution.py:346
  38.4 6.7 %collective-permute-start.2 = (bf16[2,64,512]{2,1,0:T(8,128)(2,1)S(1)}, bf16[2,64,512]{2,1,0:T(8,128)(2,1)S(1)}, u32[]{:S(2)}, u32[]{:S(2)}) collective-permute-start(bf16[2,64,512]{2,1,0:T(8,128)(2,1)S(1)} %pad_maximum_fusion.pair_ref), channel_id=1, source_target_pairs={{0,1},{1,2},{2,3},{3,4},{4,5},{5,6},{6,7},{7,0},{8,15},{9,8},{10,9... | collective-permute-start | bytes 393224 | tf_op jit(solution)/shard_map/ppermute | solution.py:346
  41.2 0.8 copy-start.1
  42.0 0.7 copy-start.3
  42.8 5.6 %collective-permute-start = (bf16[64,512]{1,0:T(8,128)(2,1)S(1)}, bf16[64,512]{1,0:T(8,128)(2,1)S(1)}, u32[]{:S(2)}, u32[]{:S(2)}) collective-permute-start(bf16[64,512]{1,0:T(8,128)(2,1)S(1)} %get-tuple-element.31.own_ref), channel_id=1, source_target_pairs={{0,8},{8,0},{16,24},{24,16},{32,40},{40,32},{48,56},{56,48},{64,72... | collective-permute-start | bytes 196616 | tf_op jit(solution)/shard_map/ppermute | solution.py:338
  50.8 6.1 %collective-permute-start.5 = (f32[200,512]{1,0:T(8,128)S(1)}, f32[200,512]{1,0:T(8,128)S(1)}, u32[]{:S(2)}, u32[]{:S(2)}) collective-permute-start(f32[200,512]{1,0:T(8,128)S(1)} %get-tuple-element.35.own_part), channel_id=1, source_target_pairs={{0,8},{8,0},{16,24},{24,16},{32,40},{40,32},{48,56},{56,48},{64,72... | collective-permute-start | bytes 1228808 | tf_op jit(solution)/shard_map/ppermute | solution.py:338
  59.8 18.8 %all-to-all-start.1 = ((bf16[4,8,128,128]{3,2,1,0:T(8,128)(2,1)}), bf16[4,8,128,128]{3,2,1,0:T(8,128)(2,1)S(1)}, u32[]{:S(2)}, u32[]{:S(2)}) async-start(bf16[4,8,128,128]{3,2,1,0:T(8,128)(2,1)} %bitcast.7), calls=%async_computation.1 | async-start | bytes 2097152 | tf_op jit(solution)/shard_map/all_to_all | solution.py:335
  64.2 32.3 %copy-start = (bf16[512,512]{1,0:T(8,128)(2,1)S(1)}, bf16[512,512]{1,0:T(8,128)(2,1)}, u32[]{:S(2)}) copy-start(bf16[512,512]{1,0:T(8,128)(2,1)} %hidden_ref.1) | copy-start | bytes 1572868
  64.2 32.3 %copy-start.4 = (f32[64]{0:T(128)S(1)}, f32[64]{0:T(128)}, u32[]{:S(2)}) copy-start(f32[64]{0:T(128)} %param.13) | copy-start | bytes 772
  67.5 18.4 %collective-permute-start.6 = (bf16[2,80,512]{2,1,0:T(8,128)(2,1)S(1)}, bf16[2,80,512]{2,1,0:T(8,128)(2,1)S(1)}, u32[]{:S(2)}, u32[]{:S(2)}) collective-permute-start(bf16[2,80,512]{2,1,0:T(8,128)(2,1)S(1)} %get-tuple-element.40), channel_id=1, source_target_pairs={{0,7},{1,0},{2,1},{3,2},{4,3},{5,4},{6,5},{7,6},{8,9},{9,10},{10,1... | collective-permute-start | bytes 491528 | tf_op jit(solution)/shard_map/ppermute | solution.py:346
  69.4 16.4 %collective-permute-start.7 = (bf16[2,80,512]{2,1,0:T(8,128)(2,1)S(1)}, bf16[2,80,512]{2,1,0:T(8,128)(2,1)S(1)}, u32[]{:S(2)}, u32[]{:S(2)}) collective-permute-start(bf16[2,80,512]{2,1,0:T(8,128)(2,1)S(1)} %get-tuple-element.41), channel_id=1, source_target_pairs={{0,6},{1,7},{2,0},{3,1},{4,2},{5,3},{6,4},{7,5},{8,10},{9,11},{10,... | collective-permute-start | bytes 491528 | tf_op jit(solution)/shard_map/ppermute | solution.py:346
  73.0 12.9 %collective-permute-start.8 = (bf16[2,80,512]{2,1,0:T(8,128)(2,1)S(1)}, bf16[2,80,512]{2,1,0:T(8,128)(2,1)S(1)}, u32[]{:S(2)}, u32[]{:S(2)}) collective-permute-start(bf16[2,80,512]{2,1,0:T(8,128)(2,1)S(1)} %get-tuple-element.42), channel_id=1, source_target_pairs={{0,1},{1,2},{2,3},{3,4},{4,5},{5,6},{6,7},{7,0},{8,15},{9,8},{10,9... | collective-permute-start | bytes 491528 | tf_op jit(solution)/shard_map/ppermute | solution.py:346
  79.5 18.2 %all-to-all-start.2 = ((bf16[8,128,128]{2,1,0:T(8,128)(2,1)}), bf16[8,128,128]{2,1,0:T(8,128)(2,1)S(1)}, u32[]{:S(2)}, u32[]{:S(2)}) async-start(bf16[8,128,128]{2,1,0:T(8,128)(2,1)} %shard_map.142), calls=%async_computation.2 | async-start | bytes 524288 | tf_op jit(solution)/shard_map/all_to_all | solution.py:335
  86.0 10.5 %collective-permute-start.9 = (bf16[1,80,512]{2,1,0:T(8,128)(2,1)S(1)}, bf16[1,80,512]{2,1,0:T(8,128)(2,1)S(1)}, u32[]{:S(2)}, u32[]{:S(2)}) collective-permute-start(bf16[1,80,512]{2,1,0:T(8,128)(2,1)S(1)} %get-tuple-element.44), channel_id=1, source_target_pairs={{0,4},{1,5},{2,6},{3,7},{4,0},{5,1},{6,2},{7,3},{8,12},{9,13},{10,... | collective-permute-start | bytes 245768 | tf_op jit(solution)/shard_map/ppermute | solution.py:346
  90.9 4.9 %collective-permute-start.10 = (bf16[256,128]{1,0:T(8,128)(2,1)S(1)}, bf16[256,128]{1,0:T(8,128)(2,1)S(1)}, u32[]{:S(2)}, u32[]{:S(2)}) collective-permute-start(bf16[256,128]{1,0:T(8,128)(2,1)S(1)} %get-tuple-element.47), channel_id=1, source_target_pairs={{0,8},{8,0},{16,24},{24,16},{32,40},{40,32},{48,56},{56,48},{64,72... | collective-permute-start | bytes 196616 | tf_op jit(solution)/shard_map/ppermute | solution.py:338

commit v7 on v6

--- a/solution.py
+++ b/solution.py
@@ -87,9 +87,8 @@
         copy.wait()
 
 
-def column_block(place_ref, shift, parts, width):
-    way = 1 - 2 * lax.rem(place_ref[0], 2)
-    owner = lax.rem(place_ref[1] - shift * way + 2 * parts, parts)
+def column_block(place_ref, step, parts, width):
+    owner = lax.bitwise_xor(place_ref[1], jnp.int32(step))
     return pl.ds(pl.multiple_of(owner * width, width), width)
 
 
@@ -106,8 +105,8 @@
 def weight_copies(place_ref, weight_ref, held, sems):
     parts, _, width = held.shape
     copies = []
-    for at, shift in enumerate(tp_order(parts)):
-        columns = column_block(place_ref, shift, parts, width)
+    for at, step in enumerate(tp_order(parts)):
+        columns = column_block(place_ref, step, parts, width)
         copies.append(pltpu.make_async_copy(weight_ref.at[:, columns], held.at[at], sems.at[at]))
     for copy in copies:
         copy.start()
@@ -296,13 +295,12 @@
     dv_ref[...] = total[slots : 2 * slots, :].astype(BF16)
 
 
-def tp_shifts(parts):
-    half = parts // 2
-    return [shift if 2 * shift <= half else shift - half for shift in range(1, half)]
+def tp_steps(parts):
+    return list(range(parts // 2 - 1, 0, -1))
 
 
 def tp_order(parts):
-    return [shift + step for shift in [0] + tp_shifts(parts) for step in (0, parts // 2)]
+    return [step ^ far for step in [0] + tp_steps(parts) for far in (0, parts // 2)]
 
 
 def on_device(
@@ -337,13 +335,8 @@
     def to_sibling(array):
         return lax.ppermute(array, "ctx", [(i, i ^ 1) for i in range(ny * nx * nc)])
 
-    def tp_send(array, shift):
-        pairs = []
-        for shard in range(ny * nx * nc):
-            for part in range(tp_count):
-                to = (part + shift * (1 - 2 * (shard % nc))) % tp_count
-                pairs.append((shard * tp_count + part, shard * tp_count + to))
-        return lax.ppermute(array, ("ctx", "tp"), pairs)
+    def tp_swap(array, step):
+        return lax.ppermute(array, "tp", [(part, part ^ step) for part in range(tp_count)])
 
     def summed(first, second):
         return (first.astype(F32) + second.astype(F32)).astype(BF16)
@@ -373,7 +366,7 @@
         (my_shard * TOK_DEV + chosen_index).astype(F32)[None, :],
         frequency,
     )
-    first_arrival = tp_send(out_cotangent[None], tp_count // 2)
+    first_arrival = tp_swap(out_cotangent[None], tp_count // 2)
     pieces = exchange(payloads, all_groups)
 
     own_queries, gate = call(
@@ -388,7 +381,7 @@
         pltpu.SemaphoreType.DMA((tp_count,)),
     ]
     pair = jnp.concatenate([out_cotangent[None], first_arrival], axis=0)
-    cot = [pair] + [tp_send(pair, shift) for shift in tp_shifts(tp_count)]
+    cot = [pair] + [tp_swap(pair, step) for step in tp_steps(tp_count)]
     grad_attention = call(
         cotangent_kernel,
         jax.ShapeDtypeStruct((slots, width), BF16),
@@ -436,16 +429,17 @@
     grad_queries = call(
         query_grad_kernel, jax.ShapeDtypeStruct((slots, width), BF16), [VMEM] * 4
     )(cos_full, sin_signed, dq_own, dq_arrived)
-    arrived = [tp_send(share, -shift) for share, shift in zip(shares[1:], tp_shifts(tp_count))]
+    arrived = [tp_swap(share, step) for share, step in zip(shares[1:], tp_steps(tp_count))]
     shares = functools.reduce(jnp.add, [part.astype(F32) for part in [shares[0]] + arrived]).astype(BF16)
     near, far = shares[:1], shares[1:]
     far, _ = lax.optimization_barrier((far, stacked))
-    arrived = tp_send(far, -(tp_count // 2))
+    arrived = tp_swap(far, tp_count // 2)
 
     grad_keys, grad_values = call(
         finish_kernel, [jax.ShapeDtypeStruct((slots, HD), BF16)] * 2, [VMEM] * 3
     )(cos_full, sin_signed, landed)
 
+    arrived, grad_keys, grad_values = lax.optimization_barrier((arrived, grad_keys, grad_values))
     update, hidden_after, grad_row = call(
         update_kernel,
         [

time: 99.9 us -> 101 us (1.011); the launches traced: 98.4 us -> 101 us
  waiting for transfers between devices: 6.7 us -> 7.89 us
    ppermute x8, waiting for transfers between devices: 2.16 us -> 3.78 us  [tp_swap(): lax.ppermute(array, 'tp', [(part, part ^ step) for part in range(tp_count)])]
  transfers between devices with their start and end apart: 14 -> 14, of which waited for: 4 -> 5; matrix products, arithmetic and copies ran while one was open for 1% -> 1% of each run, Pallas kernels for 10% -> 9%
where the time goes in v7:
time: 101 us
  starting transfers between devices  70.4 us (70%)
  Pallas kernels  16.7 us (17%)
  waiting for transfers between devices  7.89 us (8%)
  other arithmetic  2.5 us (2%)
  local copies, waits for them, and re-layouts  1.52 us (2%)
  between operations  1.52 us (2%)
    ppermute x8, starting transfers between devices, tp_swap(): lax.ppermute(array, 'tp', [(part, part ^ step) for part in range(tp_count)])  37.7 us
    all_to_all x3, starting transfers between devices, exchange(): lax.all_to_all(array, 'ctx', 0, 0, axis_index_groups=groups, tiled=True)  21 us
    ppermute x3, starting transfers between devices, to_sibling(): return lax.ppermute(array, 'ctx', [(i, i ^ 1) for i in range(ny * nx * nc)])  11.7 us
    ppermute x8, waiting for transfers between devices, tp_swap(): lax.ppermute(array, 'tp', [(part, part ^ step) for part in range(tp_count)])  3.78 us
    pallas_call x1, Pallas kernels, on_device(): call(projection_kernel, [jax.ShapeDtypeStruct((2, slots + 16, width), BF1...  3.34 us
    pallas_call x1, Pallas kernels, on_device(): call(cotangent_kernel, jax.ShapeDtypeStruct((slots, width), BF16), [SMEM,...  3.29 us
    pallas_call x1, Pallas kernels, on_device(): call(backward_kernel, [jax.ShapeDtypeStruct((slots, width), BF16), jax.Sh...  2.87 us
    pallas_call x1, Pallas kernels, on_device(): call(forward_kernel, [jax.ShapeDtypeStruct((HD + 8 + slots, rows), F32),...  2.38 us
  transfers between devices with their start and end apart: 14, of which 5 were waited for; matrix products, arithmetic and copies ran while one was open for 1% of the time, Pallas kernels for 9%

profile of v7, /device:TPU:1, one launch (start us, length us, event | category | flops | bytes accessed | tf_op | source)
XLA Modules:
  0.0 100.5 jit_solution(11583836613388602935)
XLA Ops:
  2.8 1.2 %shard_map.136 = (bf16[128,128]{1,0:T(8,128)(2,1)S(1)}, bf16[32,128,128]{2,1,0:T(8,128)(2,1)}, f32[64,128]{1,0:T(8,128)S(1)}, f32[64,128]{1,0:T(8,128)S(1)}) custom-call(s32[1]{0:T(128)S(6)} %copy.15.count_ref, bf16[128,128]{1,0:T(8,128)(2,1)S(1)} %pad_maximum_fusion.1.pair_ref, f32[1,64]{1,0:T(1,128)S(1)} %convert_bitcast_fusion.position_ref, ...), custom_call_target="tpu_custom_call" | custom-call | tf_op jit(solution)/shard_map/pallas_call | solution.py:352
  4.0 10.5 %all-to-all-start = ((bf16[32,128,128]{2,1,0:T(8,128)(2,1)}), bf16[32,128,128]{2,1,0:T(8,128)(2,1)S(1)}, u32[]{:S(2)}, u32[]{:S(2)}) async-start(bf16[32,128,128]{2,1,0:T(8,128)(2,1)} %get-tuple-element.37), calls=%async_computation | async-start | bytes 2097152 | tf_op jit(solution)/shard_map/all_to_all | solution.py:333
  14.6 10.6 %collective-permute-start.1 = (bf16[1,64,512]{2,1,0:T(8,128)(2,1)}, bf16[1,64,512]{2,1,0:T(8,128)(2,1)S(1)}, u32[]{:S(2)}, u32[]{:S(2)}) collective-permute-start(bf16[1,64,512]{2,1,0:T(8,128)(2,1)} %bitcast.15), channel_id=1, source_target_pairs={{0,4},{1,5},{2,6},{3,7},{4,0},{5,1},{6,2},{7,3},{8,12},{9,13},{10,... | collective-permute-start | bytes 196616 | tf_op jit(solution)/shard_map/ppermute | solution.py:339
  25.2 2.1 %collective-permute-done.1 = bf16[1,64,512]{2,1,0:T(8,128)(2,1)S(1)} collective-permute-done((bf16[1,64,512]{2,1,0:T(8,128)(2,1)}, bf16[1,64,512]{2,1,0:T(8,128)(2,1)S(1)}, u32[]{:S(2)}, u32[]{:S(2)}) %collective-permute-start.1) | collective-permute-done | bytes 65568 | tf_op jit(solution)/shard_map/ppermute | solution.py:339
  28.2 3.1 %collective-permute-start.4 = (bf16[2,64,512]{2,1,0:T(8,128)(2,1)S(1)}, bf16[2,64,512]{2,1,0:T(8,128)(2,1)S(1)}, u32[]{:S(2)}, u32[]{:S(2)}) collective-permute-start(bf16[2,64,512]{2,1,0:T(8,128)(2,1)S(1)} %pad_maximum_fusion.pair_ref), channel_id=1, source_target_pairs={{0,1},{1,0},{2,3},{3,2},{4,5},{5,4},{6,7},{7,6},{8,9},{9,8},{10,11... | collective-permute-start | bytes 393224 | tf_op jit(solution)/shard_map/ppermute | solution.py:339
  31.3 4.5 %collective-permute-start.3 = (bf16[2,64,512]{2,1,0:T(8,128)(2,1)S(1)}, bf16[2,64,512]{2,1,0:T(8,128)(2,1)S(1)}, u32[]{:S(2)}, u32[]{:S(2)}) collective-permute-start(bf16[2,64,512]{2,1,0:T(8,128)(2,1)S(1)} %pad_maximum_fusion.pair_ref), channel_id=1, source_target_pairs={{0,2},{1,3},{2,0},{3,1},{4,6},{5,7},{6,4},{7,5},{8,10},{9,11},{10,... | collective-permute-start | bytes 393224 | tf_op jit(solution)/shard_map/ppermute | solution.py:339
  35.8 3.1 %collective-permute-start.2 = (bf16[2,64,512]{2,1,0:T(8,128)(2,1)S(1)}, bf16[2,64,512]{2,1,0:T(8,128)(2,1)S(1)}, u32[]{:S(2)}, u32[]{:S(2)}) collective-permute-start(bf16[2,64,512]{2,1,0:T(8,128)(2,1)S(1)} %pad_maximum_fusion.pair_ref), channel_id=1, source_target_pairs={{0,3},{1,2},{2,1},{3,0},{4,7},{5,6},{6,5},{7,4},{8,11},{9,10},{10,... | collective-permute-start | bytes 393224 | tf_op jit(solution)/shard_map/ppermute | solution.py:339
  40.5 3.5 %collective-permute-start = (bf16[64,512]{1,0:T(8,128)(2,1)S(1)}, bf16[64,512]{1,0:T(8,128)(2,1)S(1)}, u32[]{:S(2)}, u32[]{:S(2)}) collective-permute-start(bf16[64,512]{1,0:T(8,128)(2,1)S(1)} %get-tuple-element.34.own_ref), channel_id=1, source_target_pairs={{0,8},{8,0},{16,24},{24,16},{32,40},{40,32},{48,56},{56,48},{64,72... | collective-permute-start | bytes 196616 | tf_op jit(solution)/shard_map/ppermute | solution.py:336
  44.1 3.3 %shard_map.138.grad_ref = bf16[64,512]{1,0:T(8,128)(2,1)S(1)} custom-call(s32[2]{0:T(128)S(1)} %pad_add_fusion.place_ref, bf16[512,4096]{1,0:T(8,128)(2,1)} %weight_ref.3, f32[64,128]{1,0:T(8,128)S(1)} %get-tuple-element.35.gate_ref, bf16[2,64,512]{2,1,0:T(8,128)(2,1)S(1)} %pad_maximum_fusion.pair_ref, ...), custom_call_target="tpu_custom_call" | custom-call | tf_op jit(solution)/shard_map/pallas_call | solution.py:385
  47.5 2.4 %shard_map.139 = (f32[200,512]{1,0:T(8,128)S(1)}, bf16[4,512,512]{2,1,0:T(8,128)(2,1)S(1)}) custom-call(s32[2]{0:T(128)S(1)} %pad_add_fusion.place_ref, s32[1,64]{1,0:T(1,128)S(1)} %bitcast.11, bf16[64,512]{1,0:T(8,128)(2,1)S(1)} %get-tuple-element.34.own_ref, bf16[64,512]{1,0:T(8,128)(2,1)S(1)} %collective-permute-done.sibling_ref, ...), custom_call_target="tpu_custom_call" | custom-call | tf_op jit(solution)/shard_map/pallas_call | solution.py:394
  49.9 5.1 %collective-permute-start.5 = (f32[200,512]{1,0:T(8,128)S(1)}, f32[200,512]{1,0:T(8,128)S(1)}, u32[]{:S(2)}, u32[]{:S(2)}) collective-permute-start(f32[200,512]{1,0:T(8,128)S(1)} %get-tuple-element.38.own_part), channel_id=1, source_target_pairs={{0,8},{8,0},{16,24},{24,16},{32,40},{40,32},{48,56},{56,48},{64,72... | collective-permute-start | bytes 1228808 | tf_op jit(solution)/shard_map/ppermute | solution.py:336
  55.0 1.4 %collective-permute-done.5.sibling_part = f32[200,512]{1,0:T(8,128)S(1)} collective-permute-done((f32[200,512]{1,0:T(8,128)S(1)}, f32[200,512]{1,0:T(8,128)S(1)}, u32[]{:S(2)}, u32[]{:S(2)}) %collective-permute-start.5) | collective-permute-done | bytes 409632 | tf_op jit(solution)/shard_map/ppermute | solution.py:336
  56.3 2.9 %shard_map.140 = (bf16[64,512]{1,0:T(8,128)(2,1)S(1)}, f32[8,256]{1,0:T(8,128)S(1)}, f32[256,128]{1,0:T(8,128)S(1)}, bf16[256,128]{1,0:T(8,128)(2,1)S(1)}, bf16[32,128,128]{2,1,0:T(8,128)(2,1)}) custom-call(f32[200,512]{1,0:T(8,128)S(1)} %get-tuple-element.38.own_part, f32[200,512]{1,0:T(8,128)S(1)} %collective-permute-done.5.sibling_part, ...), custom_call_target="tpu_custom_call" | custom-call | tf_op jit(solution)/shard_map/pallas_call | solution.py:404
  59.2 4.2 %all-to-all-start.1 = ((bf16[4,8,128,128]{3,2,1,0:T(8,128)(2,1)}), bf16[4,8,128,128]{3,2,1,0:T(8,128)(2,1)S(1)}, u32[]{:S(2)}, u32[]{:S(2)}) async-start(bf16[4,8,128,128]{3,2,1,0:T(8,128)(2,1)} %bitcast.7), calls=%async_computation.1 | async-start | bytes 2097152 | tf_op jit(solution)/shard_map/all_to_all | solution.py:333
  63.3 3.3 %shard_map.141 = (bf16[2,80,512]{2,1,0:T(8,128)(2,1)S(1)}, bf16[2,80,512]{2,1,0:T(8,128)(2,1)S(1)}, bf16[2,80,512]{2,1,0:T(8,128)(2,1)S(1)}, bf16[2,80,512]{2,1,0:T(8,128)(2,1)S(1)}) custom-call(s32[2]{0:T(128)S(1)} %pad_add_fusion.place_ref, bf16[512,4096]{1,0:T(8,128)(2,1)} %weight_ref.3, bf16[64,512]{1,0:T(8,128)(2,1)S(1)} %get-tuple-element.40.att_ref, ...), custom_call_target="tpu_custom_call" | custom-call | tf_op jit(solution)/shard_map/pallas_call | solution.py:421
  66.7 4.1 %collective-permute-start.6 = (bf16[2,80,512]{2,1,0:T(8,128)(2,1)S(1)}, bf16[2,80,512]{2,1,0:T(8,128)(2,1)S(1)}, u32[]{:S(2)}, u32[]{:S(2)}) collective-permute-start(bf16[2,80,512]{2,1,0:T(8,128)(2,1)S(1)} %get-tuple-element.43), channel_id=1, source_target_pairs={{0,3},{1,2},{2,1},{3,0},{4,7},{5,6},{6,5},{7,4},{8,11},{9,10},{10,... | collective-permute-start | bytes 491528 | tf_op jit(solution)/shard_map/ppermute | solution.py:339
  70.8 2.8 %collective-permute-start.7 = (bf16[2,80,512]{2,1,0:T(8,128)(2,1)S(1)}, bf16[2,80,512]{2,1,0:T(8,128)(2,1)S(1)}, u32[]{:S(2)}, u32[]{:S(2)}) collective-permute-start(bf16[2,80,512]{2,1,0:T(8,128)(2,1)S(1)} %get-tuple-element.44), channel_id=1, source_target_pairs={{0,2},{1,3},{2,0},{3,1},{4,6},{5,7},{6,4},{7,5},{8,10},{9,11},{10,... | collective-permute-start | bytes 491528 | tf_op jit(solution)/shard_map/ppermute | solution.py:339
  73.6 2.4 %collective-permute-start.8 = (bf16[2,80,512]{2,1,0:T(8,128)(2,1)S(1)}, bf16[2,80,512]{2,1,0:T(8,128)(2,1)S(1)}, u32[]{:S(2)}, u32[]{:S(2)}) collective-permute-start(bf16[2,80,512]{2,1,0:T(8,128)(2,1)S(1)} %get-tuple-element.45), channel_id=1, source_target_pairs={{0,1},{1,0},{2,3},{3,2},{4,5},{5,4},{6,7},{7,6},{8,9},{9,8},{10,11... | collective-permute-start | bytes 491528 | tf_op jit(solution)/shard_map/ppermute | solution.py:339
  76.0 1.9 %all-to-all-done.1.stack_ref = bf16[4,8,128,128]{3,2,1,0:T(8,128)(2,1)S(1)} async-done(((bf16[4,8,128,128]{3,2,1,0:T(8,128)(2,1)}), bf16[4,8,128,128]{3,2,1,0:T(8,128)(2,1)S(1)}, u32[]{:S(2)}, u32[]{:S(2)}) %all-to-all-start.1) | async-done | bytes 1048608 | tf_op jit(solution)/shard_map/all_to_all | solution.py:333
  78.7 6.4 %all-to-all-start.2 = ((bf16[8,128,128]{2,1,0:T(8,128)(2,1)}), bf16[8,128,128]{2,1,0:T(8,128)(2,1)S(1)}, u32[]{:S(2)}, u32[]{:S(2)}) async-start(bf16[8,128,128]{2,1,0:T(8,128)(2,1)} %shard_map.142), calls=%async_computation.2 | async-start | bytes 524288 | tf_op jit(solution)/shard_map/all_to_all | solution.py:333
  85.1 1.6 %collective-permute-done.7 = bf16[2,80,512]{2,1,0:T(8,128)(2,1)S(1)} collective-permute-done((bf16[2,80,512]{2,1,0:T(8,128)(2,1)S(1)}, bf16[2,80,512]{2,1,0:T(8,128)(2,1)S(1)}, u32[]{:S(2)}, u32[]{:S(2)}) %collective-permute-start.7) | collective-permute-done | bytes 163872 | tf_op jit(solution)/shard_map/ppermute | solution.py:339
  86.8 7.1 %collective-permute-start.9 = (bf16[1,80,512]{2,1,0:T(8,128)(2,1)S(1)}, bf16[1,80,512]{2,1,0:T(8,128)(2,1)S(1)}, u32[]{:S(2)}, u32[]{:S(2)}) collective-permute-start(bf16[1,80,512]{2,1,0:T(8,128)(2,1)S(1)} %get-tuple-element.47), channel_id=1, source_target_pairs={{0,4},{1,5},{2,6},{3,7},{4,0},{5,1},{6,2},{7,3},{8,12},{9,13},{10,... | collective-permute-start | bytes 245768 | tf_op jit(solution)/shard_map/ppermute | solution.py:339
  93.9 3.1 %collective-permute-start.10 = (bf16[256,128]{1,0:T(8,128)(2,1)S(1)}, bf16[256,128]{1,0:T(8,128)(2,1)S(1)}, u32[]{:S(2)}, u32[]{:S(2)}) collective-permute-start(bf16[256,128]{1,0:T(8,128)(2,1)S(1)} %get-tuple-element.53), channel_id=1, source_target_pairs={{0,8},{8,0},{16,24},{24,16},{32,40},{40,32},{48,56},{56,48},{64,72... | collective-permute-start | bytes 196616 | tf_op jit(solution)/shard_map/ppermute | solution.py:336
  99.4 1.2 %shard_map.144 = (bf16[64,512]{1,0:T(8,128)(2,1)}, bf16[512,512]{1,0:T(8,128)(2,1)}, f32[1,64]{1,0:T(1,128)}) custom-call(s32[1]{0:T(128)S(6)} %copy.15.count_ref, bf16[1,80,512]{2,1,0:T(8,128)(2,1)S(1)} %get-tuple-element.59.own_ref, bf16[1,80,512]{2,1,0:T(8,128)(2,1)S(1)} %collective-permute-done.9.landed_ref, f32[1,64]{1,0:T(1,128)S(1)} %bitcast.14, ...), custom_call_target="tpu_custom_call" | custom-call | tf_op jit(solution)/shard_map/pallas_call | solution.py:443
  (32 shorter events, 7.3 us)
Async XLA Ops:
  0.6 46.8 %copy-start.2 = (s32[64]{0:T(128)S(1)}, s32[64]{0:T(128)}, u32[]{:S(2)}) copy-start(s32[64]{0:T(128)} %param.14) | copy-start | bytes 772
  4.0 43.4 %all-to-all-start = ((bf16[32,128,128]{2,1,0:T(8,128)(2,1)}), bf16[32,128,128]{2,1,0:T(8,128)(2,1)S(1)}, u32[]{:S(2)}, u32[]{:S(2)}) async-start(bf16[32,128,128]{2,1,0:T(8,128)(2,1)} %get-tuple-element.37), calls=%async_computation | async-start | bytes 2097152 | tf_op jit(solution)/shard_map/all_to_all | solution.py:333
  14.6 12.8 %collective-permute-start.1 = (bf16[1,64,512]{2,1,0:T(8,128)(2,1)}, bf16[1,64,512]{2,1,0:T(8,128)(2,1)S(1)}, u32[]{:S(2)}, u32[]{:S(2)}) collective-permute-start(bf16[1,64,512]{2,1,0:T(8,128)(2,1)} %bitcast.15), channel_id=1, source_target_pairs={{0,4},{1,5},{2,6},{3,7},{4,0},{5,1},{6,2},{7,3},{8,12},{9,13},{10,... | collective-permute-start | bytes 196616 | tf_op jit(solution)/shard_map/ppermute | solution.py:339
  28.2 15.9 %collective-permute-start.4 = (bf16[2,64,512]{2,1,0:T(8,128)(2,1)S(1)}, bf16[2,64,512]{2,1,0:T(8,128)(2,1)S(1)}, u32[]{:S(2)}, u32[]{:S(2)}) collective-permute-start(bf16[2,64,512]{2,1,0:T(8,128)(2,1)S(1)} %pad_maximum_fusion.pair_ref), channel_id=1, source_target_pairs={{0,1},{1,0},{2,3},{3,2},{4,5},{5,4},{6,7},{7,6},{8,9},{9,8},{10,11... | collective-permute-start | bytes 393224 | tf_op jit(solution)/shard_map/ppermute | solution.py:339
  31.3 12.8 %collective-permute-start.3 = (bf16[2,64,512]{2,1,0:T(8,128)(2,1)S(1)}, bf16[2,64,512]{2,1,0:T(8,128)(2,1)S(1)}, u32[]{:S(2)}, u32[]{:S(2)}) collective-permute-start(bf16[2,64,512]{2,1,0:T(8,128)(2,1)S(1)} %pad_maximum_fusion.pair_ref), channel_id=1, source_target_pairs={{0,2},{1,3},{2,0},{3,1},{4,6},{5,7},{6,4},{7,5},{8,10},{9,11},{10,... | collective-permute-start | bytes 393224 | tf_op jit(solution)/shard_map/ppermute | solution.py:339
  35.8 8.4 %collective-permute-start.2 = (bf16[2,64,512]{2,1,0:T(8,128)(2,1)S(1)}, bf16[2,64,512]{2,1,0:T(8,128)(2,1)S(1)}, u32[]{:S(2)}, u32[]{:S(2)}) collective-permute-start(bf16[2,64,512]{2,1,0:T(8,128)(2,1)S(1)} %pad_maximum_fusion.pair_ref), channel_id=1, source_target_pairs={{0,3},{1,2},{2,1},{3,0},{4,7},{5,6},{6,5},{7,4},{8,11},{9,10},{10,... | collective-permute-start | bytes 393224 | tf_op jit(solution)/shard_map/ppermute | solution.py:339
  38.9 0.8 copy-start.1
  39.7 0.7 copy-start.3
  40.5 6.9 %collective-permute-start = (bf16[64,512]{1,0:T(8,128)(2,1)S(1)}, bf16[64,512]{1,0:T(8,128)(2,1)S(1)}, u32[]{:S(2)}, u32[]{:S(2)}) collective-permute-start(bf16[64,512]{1,0:T(8,128)(2,1)S(1)} %get-tuple-element.34.own_ref), channel_id=1, source_target_pairs={{0,8},{8,0},{16,24},{24,16},{32,40},{40,32},{48,56},{56,48},{64,72... | collective-permute-start | bytes 196616 | tf_op jit(solution)/shard_map/ppermute | solution.py:336
  49.9 6.5 %collective-permute-start.5 = (f32[200,512]{1,0:T(8,128)S(1)}, f32[200,512]{1,0:T(8,128)S(1)}, u32[]{:S(2)}, u32[]{:S(2)}) collective-permute-start(f32[200,512]{1,0:T(8,128)S(1)} %get-tuple-element.38.own_part), channel_id=1, source_target_pairs={{0,8},{8,0},{16,24},{24,16},{32,40},{40,32},{48,56},{56,48},{64,72... | collective-permute-start | bytes 1228808 | tf_op jit(solution)/shard_map/ppermute | solution.py:336
  59.2 18.7 %all-to-all-start.1 = ((bf16[4,8,128,128]{3,2,1,0:T(8,128)(2,1)}), bf16[4,8,128,128]{3,2,1,0:T(8,128)(2,1)S(1)}, u32[]{:S(2)}, u32[]{:S(2)}) async-start(bf16[4,8,128,128]{3,2,1,0:T(8,128)(2,1)} %bitcast.7), calls=%async_computation.1 | async-start | bytes 2097152 | tf_op jit(solution)/shard_map/all_to_all | solution.py:333
  63.3 36.0 %copy-start = (bf16[512,512]{1,0:T(8,128)(2,1)S(1)}, bf16[512,512]{1,0:T(8,128)(2,1)}, u32[]{:S(2)}) copy-start(bf16[512,512]{1,0:T(8,128)(2,1)} %hidden_ref.1) | copy-start | bytes 1572868
  63.3 36.0 %copy-start.4 = (f32[64]{0:T(128)S(1)}, f32[64]{0:T(128)}, u32[]{:S(2)}) copy-start(f32[64]{0:T(128)} %param.13) | copy-start | bytes 772
  66.7 18.4 %collective-permute-start.6 = (bf16[2,80,512]{2,1,0:T(8,128)(2,1)S(1)}, bf16[2,80,512]{2,1,0:T(8,128)(2,1)S(1)}, u32[]{:S(2)}, u32[]{:S(2)}) collective-permute-start(bf16[2,80,512]{2,1,0:T(8,128)(2,1)S(1)} %get-tuple-element.43), channel_id=1, source_target_pairs={{0,3},{1,2},{2,1},{3,0},{4,7},{5,6},{6,5},{7,4},{8,11},{9,10},{10,... | collective-permute-start | bytes 491528 | tf_op jit(solution)/shard_map/ppermute | solution.py:339
  70.8 15.9 %collective-permute-start.7 = (bf16[2,80,512]{2,1,0:T(8,128)(2,1)S(1)}, bf16[2,80,512]{2,1,0:T(8,128)(2,1)S(1)}, u32[]{:S(2)}, u32[]{:S(2)}) collective-permute-start(bf16[2,80,512]{2,1,0:T(8,128)(2,1)S(1)} %get-tuple-element.44), channel_id=1, source_target_pairs={{0,2},{1,3},{2,0},{3,1},{4,6},{5,7},{6,4},{7,5},{8,10},{9,11},{10,... | collective-permute-start | bytes 491528 | tf_op jit(solution)/shard_map/ppermute | solution.py:339
  73.6 13.1 %collective-permute-start.8 = (bf16[2,80,512]{2,1,0:T(8,128)(2,1)S(1)}, bf16[2,80,512]{2,1,0:T(8,128)(2,1)S(1)}, u32[]{:S(2)}, u32[]{:S(2)}) collective-permute-start(bf16[2,80,512]{2,1,0:T(8,128)(2,1)S(1)} %get-tuple-element.45), channel_id=1, source_target_pairs={{0,1},{1,0},{2,3},{3,2},{4,5},{5,4},{6,7},{7,6},{8,9},{9,8},{10,11... | collective-permute-start | bytes 491528 | tf_op jit(solution)/shard_map/ppermute | solution.py:339
  78.7 20.0 %all-to-all-start.2 = ((bf16[8,128,128]{2,1,0:T(8,128)(2,1)}), bf16[8,128,128]{2,1,0:T(8,128)(2,1)S(1)}, u32[]{:S(2)}, u32[]{:S(2)}) async-start(bf16[8,128,128]{2,1,0:T(8,128)(2,1)} %shard_map.142), calls=%async_computation.2 | async-start | bytes 524288 | tf_op jit(solution)/shard_map/all_to_all | solution.py:333
  86.8 12.5 %collective-permute-start.9 = (bf16[1,80,512]{2,1,0:T(8,128)(2,1)S(1)}, bf16[1,80,512]{2,1,0:T(8,128)(2,1)S(1)}, u32[]{:S(2)}, u32[]{:S(2)}) collective-permute-start(bf16[1,80,512]{2,1,0:T(8,128)(2,1)S(1)} %get-tuple-element.47), channel_id=1, source_target_pairs={{0,4},{1,5},{2,6},{3,7},{4,0},{5,1},{6,2},{7,3},{8,12},{9,13},{10,... | collective-permute-start | bytes 245768 | tf_op jit(solution)/shard_map/ppermute | solution.py:339
  93.9 4.0 %collective-permute-start.10 = (bf16[256,128]{1,0:T(8,128)(2,1)S(1)}, bf16[256,128]{1,0:T(8,128)(2,1)S(1)}, u32[]{:S(2)}, u32[]{:S(2)}) collective-permute-start(bf16[256,128]{1,0:T(8,128)(2,1)S(1)} %get-tuple-element.53), channel_id=1, source_target_pairs={{0,8},{8,0},{16,24},{24,16},{32,40},{40,32},{48,56},{56,48},{64,72... | collective-permute-start | bytes 196616 | tf_op jit(solution)/shard_map/ppermute | solution.py:336

commit v8 on v6

--- a/solution.py
+++ b/solution.py
@@ -446,6 +446,7 @@
         finish_kernel, [jax.ShapeDtypeStruct((slots, HD), BF16)] * 2, [VMEM] * 3
     )(cos_full, sin_signed, landed)
 
+    arrived, grad_keys, grad_values = lax.optimization_barrier((arrived, grad_keys, grad_values))
     update, hidden_after, grad_row = call(
         update_kernel,
         [

time: 99.9 us -> 99.2 us (level)
  transfers between devices with their start and end apart: 14 -> 14, of which waited for: 4 -> 4; matrix products, arithmetic and copies ran while one was open for 1% -> 1% of each run, Pallas kernels for 10% -> 9%
where the time goes in v8:
time: 99.2 us; the launch traced here: 98.4 us
  starting transfers between devices  69.4 us (70%)
  Pallas kernels  16.7 us (17%)
  waiting for transfers between devices  6.7 us (7%)
  other arithmetic  2.5 us (3%)
  between operations  1.53 us (2%)
  local copies, waits for them, and re-layouts  1.52 us (2%)
    ppermute x8, starting transfers between devices, tp_send(): return lax.ppermute(array, ('ctx', 'tp'), pairs)  37.3 us
    all_to_all x3, starting transfers between devices, exchange(): lax.all_to_all(array, 'ctx', 0, 0, axis_index_groups=groups, tiled=True)  21.2 us
    ppermute x3, starting transfers between devices, to_sibling(): return lax.ppermute(array, 'ctx', [(i, i ^ 1) for i in range(ny * nx * nc)])  11 us
    pallas_call x1, Pallas kernels, on_device(): call(projection_kernel, [jax.ShapeDtypeStruct((2, slots + 16, width), BF1...  3.34 us
    pallas_call x1, Pallas kernels, on_device(): call(cotangent_kernel, jax.ShapeDtypeStruct((slots, width), BF16), [SMEM,...  3.3 us
    pallas_call x1, Pallas kernels, on_device(): call(backward_kernel, [jax.ShapeDtypeStruct((slots, width), BF16), jax.Sh...  2.87 us
    pallas_call x1, Pallas kernels, on_device(): call(forward_kernel, [jax.ShapeDtypeStruct((HD + 8 + slots, rows), F32),...  2.38 us
    all_to_all x3, waiting for transfers between devices, exchange(): lax.all_to_all(array, 'ctx', 0, 0, axis_index_groups=groups, tiled=True)  2.31 us
  transfers between devices with their start and end apart: 14, of which 4 were waited for; matrix products, arithmetic and copies ran while one was open for 1% of the time, Pallas kernels for 9%

profile of v8, /device:TPU:1, one launch (start us, length us, event | category | flops | bytes accessed | tf_op | source)
XLA Modules:
  0.0 98.4 jit_solution(724018982430120046)
XLA Ops:
  2.8 1.2 %shard_map.136 = (bf16[128,128]{1,0:T(8,128)(2,1)S(1)}, bf16[32,128,128]{2,1,0:T(8,128)(2,1)}, f32[64,128]{1,0:T(8,128)S(1)}, f32[64,128]{1,0:T(8,128)S(1)}) custom-call(s32[1]{0:T(128)S(6)} %copy.15.count_ref, bf16[128,128]{1,0:T(8,128)(2,1)S(1)} %pad_maximum_fusion.1.pair_ref, f32[1,64]{1,0:T(1,128)S(1)} %convert_bitcast_fusion.position_ref, ...), custom_call_target="tpu_custom_call" | custom-call | tf_op jit(solution)/shard_map/pallas_call | solution.py:359
  4.0 10.5 %all-to-all-start = ((bf16[32,128,128]{2,1,0:T(8,128)(2,1)}), bf16[32,128,128]{2,1,0:T(8,128)(2,1)S(1)}, u32[]{:S(2)}, u32[]{:S(2)}) async-start(bf16[32,128,128]{2,1,0:T(8,128)(2,1)} %get-tuple-element.37), calls=%async_computation | async-start | bytes 2097152 | tf_op jit(solution)/shard_map/all_to_all | solution.py:335
  14.6 10.6 %collective-permute-start.1 = (bf16[1,64,512]{2,1,0:T(8,128)(2,1)}, bf16[1,64,512]{2,1,0:T(8,128)(2,1)S(1)}, u32[]{:S(2)}, u32[]{:S(2)}) collective-permute-start(bf16[1,64,512]{2,1,0:T(8,128)(2,1)} %bitcast.15), channel_id=1, source_target_pairs={{0,4},{1,5},{2,6},{3,7},{4,0},{5,1},{6,2},{7,3},{8,12},{9,13},{10,... | collective-permute-start | bytes 196616 | tf_op jit(solution)/shard_map/ppermute | solution.py:346
  25.2 2.1 %collective-permute-done.1 = bf16[1,64,512]{2,1,0:T(8,128)(2,1)S(1)} collective-permute-done((bf16[1,64,512]{2,1,0:T(8,128)(2,1)}, bf16[1,64,512]{2,1,0:T(8,128)(2,1)S(1)}, u32[]{:S(2)}, u32[]{:S(2)}) %collective-permute-start.1) | collective-permute-done | bytes 65568 | tf_op jit(solution)/shard_map/ppermute | solution.py:346
  28.2 3.1 %collective-permute-start.4 = (bf16[2,64,512]{2,1,0:T(8,128)(2,1)S(1)}, bf16[2,64,512]{2,1,0:T(8,128)(2,1)S(1)}, u32[]{:S(2)}, u32[]{:S(2)}) collective-permute-start(bf16[2,64,512]{2,1,0:T(8,128)(2,1)S(1)} %pad_maximum_fusion.pair_ref), channel_id=1, source_target_pairs={{0,7},{1,0},{2,1},{3,2},{4,3},{5,4},{6,5},{7,6},{8,9},{9,10},{10,1... | collective-permute-start | bytes 393224 | tf_op jit(solution)/shard_map/ppermute | solution.py:346
  31.3 7.1 %collective-permute-start.3 = (bf16[2,64,512]{2,1,0:T(8,128)(2,1)S(1)}, bf16[2,64,512]{2,1,0:T(8,128)(2,1)S(1)}, u32[]{:S(2)}, u32[]{:S(2)}) collective-permute-start(bf16[2,64,512]{2,1,0:T(8,128)(2,1)S(1)} %pad_maximum_fusion.pair_ref), channel_id=1, source_target_pairs={{0,2},{1,3},{2,4},{3,5},{4,6},{5,7},{6,0},{7,1},{8,14},{9,15},{10,... | collective-permute-start | bytes 393224 | tf_op jit(solution)/shard_map/ppermute | solution.py:346
  38.4 2.8 %collective-permute-start.2 = (bf16[2,64,512]{2,1,0:T(8,128)(2,1)S(1)}, bf16[2,64,512]{2,1,0:T(8,128)(2,1)S(1)}, u32[]{:S(2)}, u32[]{:S(2)}) collective-permute-start(bf16[2,64,512]{2,1,0:T(8,128)(2,1)S(1)} %pad_maximum_fusion.pair_ref), channel_id=1, source_target_pairs={{0,1},{1,2},{2,3},{3,4},{4,5},{5,6},{6,7},{7,0},{8,15},{9,8},{10,9... | collective-permute-start | bytes 393224 | tf_op jit(solution)/shard_map/ppermute | solution.py:346
  42.8 2.2 %collective-permute-start = (bf16[64,512]{1,0:T(8,128)(2,1)S(1)}, bf16[64,512]{1,0:T(8,128)(2,1)S(1)}, u32[]{:S(2)}, u32[]{:S(2)}) collective-permute-start(bf16[64,512]{1,0:T(8,128)(2,1)S(1)} %get-tuple-element.34.own_ref), channel_id=1, source_target_pairs={{0,8},{8,0},{16,24},{24,16},{32,40},{40,32},{48,56},{56,48},{64,72... | collective-permute-start | bytes 196616 | tf_op jit(solution)/shard_map/ppermute | solution.py:338
  45.1 3.3 %shard_map.138.grad_ref = bf16[64,512]{1,0:T(8,128)(2,1)S(1)} custom-call(s32[2]{0:T(128)S(1)} %pad_add_fusion.place_ref, bf16[512,4096]{1,0:T(8,128)(2,1)} %weight_ref.3, f32[64,128]{1,0:T(8,128)S(1)} %get-tuple-element.35.gate_ref, bf16[2,64,512]{2,1,0:T(8,128)(2,1)S(1)} %pad_maximum_fusion.pair_ref, ...), custom_call_target="tpu_custom_call" | custom-call | tf_op jit(solution)/shard_map/pallas_call | solution.py:392
  48.4 2.4 %shard_map.139 = (f32[200,512]{1,0:T(8,128)S(1)}, bf16[4,512,512]{2,1,0:T(8,128)(2,1)S(1)}) custom-call(s32[2]{0:T(128)S(1)} %pad_add_fusion.place_ref, s32[1,64]{1,0:T(1,128)S(1)} %bitcast.11, bf16[64,512]{1,0:T(8,128)(2,1)S(1)} %get-tuple-element.34.own_ref, bf16[64,512]{1,0:T(8,128)(2,1)S(1)} %collective-permute-done.sibling_ref, ...), custom_call_target="tpu_custom_call" | custom-call | tf_op jit(solution)/shard_map/pallas_call | solution.py:401
  50.8 4.8 %collective-permute-start.5 = (f32[200,512]{1,0:T(8,128)S(1)}, f32[200,512]{1,0:T(8,128)S(1)}, u32[]{:S(2)}, u32[]{:S(2)}) collective-permute-start(f32[200,512]{1,0:T(8,128)S(1)} %get-tuple-element.38.own_part), channel_id=1, source_target_pairs={{0,8},{8,0},{16,24},{24,16},{32,40},{40,32},{48,56},{56,48},{64,72... | collective-permute-start | bytes 1228808 | tf_op jit(solution)/shard_map/ppermute | solution.py:338
  55.6 1.4 %collective-permute-done.5.sibling_part = f32[200,512]{1,0:T(8,128)S(1)} collective-permute-done((f32[200,512]{1,0:T(8,128)S(1)}, f32[200,512]{1,0:T(8,128)S(1)}, u32[]{:S(2)}, u32[]{:S(2)}) %collective-permute-start.5) | collective-permute-done | bytes 409632 | tf_op jit(solution)/shard_map/ppermute | solution.py:338
  57.0 2.9 %shard_map.140 = (bf16[64,512]{1,0:T(8,128)(2,1)S(1)}, f32[8,256]{1,0:T(8,128)S(1)}, f32[256,128]{1,0:T(8,128)S(1)}, bf16[256,128]{1,0:T(8,128)(2,1)S(1)}, bf16[32,128,128]{2,1,0:T(8,128)(2,1)}) custom-call(f32[200,512]{1,0:T(8,128)S(1)} %get-tuple-element.38.own_part, f32[200,512]{1,0:T(8,128)S(1)} %collective-permute-done.5.sibling_part, ...), custom_call_target="tpu_custom_call" | custom-call | tf_op jit(solution)/shard_map/pallas_call | solution.py:411
  59.8 4.3 %all-to-all-start.1 = ((bf16[4,8,128,128]{3,2,1,0:T(8,128)(2,1)}), bf16[4,8,128,128]{3,2,1,0:T(8,128)(2,1)S(1)}, u32[]{:S(2)}, u32[]{:S(2)}) async-start(bf16[4,8,128,128]{3,2,1,0:T(8,128)(2,1)} %bitcast.7), calls=%async_computation.1 | async-start | bytes 2097152 | tf_op jit(solution)/shard_map/all_to_all | solution.py:335
  64.2 3.3 %shard_map.141 = (bf16[2,80,512]{2,1,0:T(8,128)(2,1)S(1)}, bf16[2,80,512]{2,1,0:T(8,128)(2,1)S(1)}, bf16[2,80,512]{2,1,0:T(8,128)(2,1)S(1)}, bf16[2,80,512]{2,1,0:T(8,128)(2,1)S(1)}) custom-call(s32[2]{0:T(128)S(1)} %pad_add_fusion.place_ref, bf16[512,4096]{1,0:T(8,128)(2,1)} %weight_ref.3, bf16[64,512]{1,0:T(8,128)(2,1)S(1)} %get-tuple-element.40.att_ref, ...), custom_call_target="tpu_custom_call" | custom-call | tf_op jit(solution)/shard_map/pallas_call | solution.py:428
  67.5 1.9 %collective-permute-start.6 = (bf16[2,80,512]{2,1,0:T(8,128)(2,1)S(1)}, bf16[2,80,512]{2,1,0:T(8,128)(2,1)S(1)}, u32[]{:S(2)}, u32[]{:S(2)}) collective-permute-start(bf16[2,80,512]{2,1,0:T(8,128)(2,1)S(1)} %get-tuple-element.43), channel_id=1, source_target_pairs={{0,7},{1,0},{2,1},{3,2},{4,3},{5,4},{6,5},{7,6},{8,9},{9,10},{10,1... | collective-permute-start | bytes 491528 | tf_op jit(solution)/shard_map/ppermute | solution.py:346
  69.4 3.5 %collective-permute-start.7 = (bf16[2,80,512]{2,1,0:T(8,128)(2,1)S(1)}, bf16[2,80,512]{2,1,0:T(8,128)(2,1)S(1)}, u32[]{:S(2)}, u32[]{:S(2)}) collective-permute-start(bf16[2,80,512]{2,1,0:T(8,128)(2,1)S(1)} %get-tuple-element.44), channel_id=1, source_target_pairs={{0,6},{1,7},{2,0},{3,1},{4,2},{5,3},{6,4},{7,5},{8,10},{9,11},{10,... | collective-permute-start | bytes 491528 | tf_op jit(solution)/shard_map/ppermute | solution.py:346
  73.0 3.4 %collective-permute-start.8 = (bf16[2,80,512]{2,1,0:T(8,128)(2,1)S(1)}, bf16[2,80,512]{2,1,0:T(8,128)(2,1)S(1)}, u32[]{:S(2)}, u32[]{:S(2)}) collective-permute-start(bf16[2,80,512]{2,1,0:T(8,128)(2,1)S(1)} %get-tuple-element.45), channel_id=1, source_target_pairs={{0,1},{1,2},{2,3},{3,4},{4,5},{5,6},{6,7},{7,0},{8,15},{9,8},{10,9... | collective-permute-start | bytes 491528 | tf_op jit(solution)/shard_map/ppermute | solution.py:346
  76.4 2.3 %all-to-all-done.1.stack_ref = bf16[4,8,128,128]{3,2,1,0:T(8,128)(2,1)S(1)} async-done(((bf16[4,8,128,128]{3,2,1,0:T(8,128)(2,1)}), bf16[4,8,128,128]{3,2,1,0:T(8,128)(2,1)S(1)}, u32[]{:S(2)}, u32[]{:S(2)}) %all-to-all-start.1) | async-done | bytes 1048608 | tf_op jit(solution)/shard_map/all_to_all | solution.py:335
  79.5 6.4 %all-to-all-start.2 = ((bf16[8,128,128]{2,1,0:T(8,128)(2,1)}), bf16[8,128,128]{2,1,0:T(8,128)(2,1)S(1)}, u32[]{:S(2)}, u32[]{:S(2)}) async-start(bf16[8,128,128]{2,1,0:T(8,128)(2,1)} %shard_map.142), calls=%async_computation.2 | async-start | bytes 524288 | tf_op jit(solution)/shard_map/all_to_all | solution.py:335
  86.0 4.8 %collective-permute-start.9 = (bf16[1,80,512]{2,1,0:T(8,128)(2,1)S(1)}, bf16[1,80,512]{2,1,0:T(8,128)(2,1)S(1)}, u32[]{:S(2)}, u32[]{:S(2)}) collective-permute-start(bf16[1,80,512]{2,1,0:T(8,128)(2,1)S(1)} %get-tuple-element.47), channel_id=1, source_target_pairs={{0,4},{1,5},{2,6},{3,7},{4,0},{5,1},{6,2},{7,3},{8,12},{9,13},{10,... | collective-permute-start | bytes 245768 | tf_op jit(solution)/shard_map/ppermute | solution.py:346
  90.9 4.0 %collective-permute-start.10 = (bf16[256,128]{1,0:T(8,128)(2,1)S(1)}, bf16[256,128]{1,0:T(8,128)(2,1)S(1)}, u32[]{:S(2)}, u32[]{:S(2)}) collective-permute-start(bf16[256,128]{1,0:T(8,128)(2,1)S(1)} %get-tuple-element.53), channel_id=1, source_target_pairs={{0,8},{8,0},{16,24},{24,16},{32,40},{40,32},{48,56},{56,48},{64,72... | collective-permute-start | bytes 196616 | tf_op jit(solution)/shard_map/ppermute | solution.py:338
  94.9 0.9 collective-permute-done.10.arrived_ref
  97.2 1.2 %shard_map.144 = (bf16[64,512]{1,0:T(8,128)(2,1)}, bf16[512,512]{1,0:T(8,128)(2,1)}, f32[1,64]{1,0:T(1,128)}) custom-call(s32[1]{0:T(128)S(6)} %copy.15.count_ref, bf16[1,80,512]{2,1,0:T(8,128)(2,1)S(1)} %get-tuple-element.59.own_ref, bf16[1,80,512]{2,1,0:T(8,128)(2,1)S(1)} %collective-permute-done.9.landed_ref, f32[1,64]{1,0:T(1,128)S(1)} %bitcast.14, ...), custom_call_target="tpu_custom_call" | custom-call | tf_op jit(solution)/shard_map/pallas_call | solution.py:450
  (32 shorter events, 6.4 us)
Async XLA Ops:
  0.6 47.8 %copy-start.2 = (s32[64]{0:T(128)S(1)}, s32[64]{0:T(128)}, u32[]{:S(2)}) copy-start(s32[64]{0:T(128)} %param.14) | copy-start | bytes 772
  4.0 44.4 %all-to-all-start = ((bf16[32,128,128]{2,1,0:T(8,128)(2,1)}), bf16[32,128,128]{2,1,0:T(8,128)(2,1)S(1)}, u32[]{:S(2)}, u32[]{:S(2)}) async-start(bf16[32,128,128]{2,1,0:T(8,128)(2,1)} %get-tuple-element.37), calls=%async_computation | async-start | bytes 2097152 | tf_op jit(solution)/shard_map/all_to_all | solution.py:335
  14.6 12.8 %collective-permute-start.1 = (bf16[1,64,512]{2,1,0:T(8,128)(2,1)}, bf16[1,64,512]{2,1,0:T(8,128)(2,1)S(1)}, u32[]{:S(2)}, u32[]{:S(2)}) collective-permute-start(bf16[1,64,512]{2,1,0:T(8,128)(2,1)} %bitcast.15), channel_id=1, source_target_pairs={{0,4},{1,5},{2,6},{3,7},{4,0},{5,1},{6,2},{7,3},{8,12},{9,13},{10,... | collective-permute-start | bytes 196616 | tf_op jit(solution)/shard_map/ppermute | solution.py:346
  28.2 16.9 %collective-permute-start.4 = (bf16[2,64,512]{2,1,0:T(8,128)(2,1)S(1)}, bf16[2,64,512]{2,1,0:T(8,128)(2,1)S(1)}, u32[]{:S(2)}, u32[]{:S(2)}) collective-permute-start(bf16[2,64,512]{2,1,0:T(8,128)(2,1)S(1)} %pad_maximum_fusion.pair_ref), channel_id=1, source_target_pairs={{0,7},{1,0},{2,1},{3,2},{4,3},{5,4},{6,5},{7,6},{8,9},{9,10},{10,1... | collective-permute-start | bytes 393224 | tf_op jit(solution)/shard_map/ppermute | solution.py:346
  31.3 13.8 %collective-permute-start.3 = (bf16[2,64,512]{2,1,0:T(8,128)(2,1)S(1)}, bf16[2,64,512]{2,1,0:T(8,128)(2,1)S(1)}, u32[]{:S(2)}, u32[]{:S(2)}) collective-permute-start(bf16[2,64,512]{2,1,0:T(8,128)(2,1)S(1)} %pad_maximum_fusion.pair_ref), channel_id=1, source_target_pairs={{0,2},{1,3},{2,4},{3,5},{4,6},{5,7},{6,0},{7,1},{8,14},{9,15},{10,... | collective-permute-start | bytes 393224 | tf_op jit(solution)/shard_map/ppermute | solution.py:346
  38.4 6.7 %collective-permute-start.2 = (bf16[2,64,512]{2,1,0:T(8,128)(2,1)S(1)}, bf16[2,64,512]{2,1,0:T(8,128)(2,1)S(1)}, u32[]{:S(2)}, u32[]{:S(2)}) collective-permute-start(bf16[2,64,512]{2,1,0:T(8,128)(2,1)S(1)} %pad_maximum_fusion.pair_ref), channel_id=1, source_target_pairs={{0,1},{1,2},{2,3},{3,4},{4,5},{5,6},{6,7},{7,0},{8,15},{9,8},{10,9... | collective-permute-start | bytes 393224 | tf_op jit(solution)/shard_map/ppermute | solution.py:346
  41.2 0.8 copy-start.1
  42.0 0.7 copy-start.3
  42.8 5.6 %collective-permute-start = (bf16[64,512]{1,0:T(8,128)(2,1)S(1)}, bf16[64,512]{1,0:T(8,128)(2,1)S(1)}, u32[]{:S(2)}, u32[]{:S(2)}) collective-permute-start(bf16[64,512]{1,0:T(8,128)(2,1)S(1)} %get-tuple-element.34.own_ref), channel_id=1, source_target_pairs={{0,8},{8,0},{16,24},{24,16},{32,40},{40,32},{48,56},{56,48},{64,72... | collective-permute-start | bytes 196616 | tf_op jit(solution)/shard_map/ppermute | solution.py:338
  50.8 6.1 %collective-permute-start.5 = (f32[200,512]{1,0:T(8,128)S(1)}, f32[200,512]{1,0:T(8,128)S(1)}, u32[]{:S(2)}, u32[]{:S(2)}) collective-permute-start(f32[200,512]{1,0:T(8,128)S(1)} %get-tuple-element.38.own_part), channel_id=1, source_target_pairs={{0,8},{8,0},{16,24},{24,16},{32,40},{40,32},{48,56},{56,48},{64,72... | collective-permute-start | bytes 1228808 | tf_op jit(solution)/shard_map/ppermute | solution.py:338
  59.8 18.8 %all-to-all-start.1 = ((bf16[4,8,128,128]{3,2,1,0:T(8,128)(2,1)}), bf16[4,8,128,128]{3,2,1,0:T(8,128)(2,1)S(1)}, u32[]{:S(2)}, u32[]{:S(2)}) async-start(bf16[4,8,128,128]{3,2,1,0:T(8,128)(2,1)} %bitcast.7), calls=%async_computation.1 | async-start | bytes 2097152 | tf_op jit(solution)/shard_map/all_to_all | solution.py:335
  64.2 33.0 %copy-start = (bf16[512,512]{1,0:T(8,128)(2,1)S(1)}, bf16[512,512]{1,0:T(8,128)(2,1)}, u32[]{:S(2)}) copy-start(bf16[512,512]{1,0:T(8,128)(2,1)} %hidden_ref.1) | copy-start | bytes 1572868
  64.2 33.0 %copy-start.4 = (f32[64]{0:T(128)S(1)}, f32[64]{0:T(128)}, u32[]{:S(2)}) copy-start(f32[64]{0:T(128)} %param.13) | copy-start | bytes 772
  67.5 18.4 %collective-permute-start.6 = (bf16[2,80,512]{2,1,0:T(8,128)(2,1)S(1)}, bf16[2,80,512]{2,1,0:T(8,128)(2,1)S(1)}, u32[]{:S(2)}, u32[]{:S(2)}) collective-permute-start(bf16[2,80,512]{2,1,0:T(8,128)(2,1)S(1)} %get-tuple-element.43), channel_id=1, source_target_pairs={{0,7},{1,0},{2,1},{3,2},{4,3},{5,4},{6,5},{7,6},{8,9},{9,10},{10,1... | collective-permute-start | bytes 491528 | tf_op jit(solution)/shard_map/ppermute | solution.py:346
  69.4 16.4 %collective-permute-start.7 = (bf16[2,80,512]{2,1,0:T(8,128)(2,1)S(1)}, bf16[2,80,512]{2,1,0:T(8,128)(2,1)S(1)}, u32[]{:S(2)}, u32[]{:S(2)}) collective-permute-start(bf16[2,80,512]{2,1,0:T(8,128)(2,1)S(1)} %get-tuple-element.44), channel_id=1, source_target_pairs={{0,6},{1,7},{2,0},{3,1},{4,2},{5,3},{6,4},{7,5},{8,10},{9,11},{10,... | collective-permute-start | bytes 491528 | tf_op jit(solution)/shard_map/ppermute | solution.py:346
  73.0 12.9 %collective-permute-start.8 = (bf16[2,80,512]{2,1,0:T(8,128)(2,1)S(1)}, bf16[2,80,512]{2,1,0:T(8,128)(2,1)S(1)}, u32[]{:S(2)}, u32[]{:S(2)}) collective-permute-start(bf16[2,80,512]{2,1,0:T(8,128)(2,1)S(1)} %get-tuple-element.45), channel_id=1, source_target_pairs={{0,1},{1,2},{2,3},{3,4},{4,5},{5,6},{6,7},{7,0},{8,15},{9,8},{10,9... | collective-permute-start | bytes 491528 | tf_op jit(solution)/shard_map/ppermute | solution.py:346
  79.5 17.0 %all-to-all-start.2 = ((bf16[8,128,128]{2,1,0:T(8,128)(2,1)}), bf16[8,128,128]{2,1,0:T(8,128)(2,1)S(1)}, u32[]{:S(2)}, u32[]{:S(2)}) async-start(bf16[8,128,128]{2,1,0:T(8,128)(2,1)} %shard_map.142), calls=%async_computation.2 | async-start | bytes 524288 | tf_op jit(solution)/shard_map/all_to_all | solution.py:335
  86.0 11.2 %collective-permute-start.9 = (bf16[1,80,512]{2,1,0:T(8,128)(2,1)S(1)}, bf16[1,80,512]{2,1,0:T(8,128)(2,1)S(1)}, u32[]{:S(2)}, u32[]{:S(2)}) collective-permute-start(bf16[1,80,512]{2,1,0:T(8,128)(2,1)S(1)} %get-tuple-element.47), channel_id=1, source_target_pairs={{0,4},{1,5},{2,6},{3,7},{4,0},{5,1},{6,2},{7,3},{8,12},{9,13},{10,... | collective-permute-start | bytes 245768 | tf_op jit(solution)/shard_map/ppermute | solution.py:346
  90.9 4.9 %collective-permute-start.10 = (bf16[256,128]{1,0:T(8,128)(2,1)S(1)}, bf16[256,128]{1,0:T(8,128)(2,1)S(1)}, u32[]{:S(2)}, u32[]{:S(2)}) collective-permute-start(bf16[256,128]{1,0:T(8,128)(2,1)S(1)} %get-tuple-element.53), channel_id=1, source_target_pairs={{0,8},{8,0},{16,24},{24,16},{32,40},{40,32},{48,56},{56,48},{64,72... | collective-permute-start | bytes 196616 | tf_op jit(solution)/shard_map/ppermute | solution.py:338

commit v9 on v8

--- a/solution.py
+++ b/solution.py
@@ -298,7 +298,7 @@
 
 def tp_shifts(parts):
     half = parts // 2
-    return [shift if 2 * shift <= half else shift - half for shift in range(1, half)]
+    return sorted((shift if 2 * shift <= half else shift - half for shift in range(1, half)), key=abs)
 
 
 def tp_order(parts):

time: 99.2 us -> 100 us (level)
  starting transfers between devices: 69.4 us -> 70.8 us
    ppermute x8, starting transfers between devices: 37.3 us -> 40.2 us  [tp_send(): return lax.ppermute(array, ('ctx', 'tp'), pairs)]
    ppermute x3, starting transfers between devices: 11 us -> 9.39 us  [to_sibling(): return lax.ppermute(array, 'ctx', [(i, i ^ 1) for i in range(ny * nx * nc)])]
where the time goes in v9:
time: 100 us; the launch traced here: 99.6 us
  starting transfers between devices  70.8 us (71%)
  Pallas kernels  16.7 us (17%)
  waiting for transfers between devices  6.59 us (7%)
  other arithmetic  2.5 us (2%)
  between operations  1.53 us (2%)
  local copies, waits for them, and re-layouts  1.52 us (2%)
    ppermute x8, starting transfers between devices, tp_send(): return lax.ppermute(array, ('ctx', 'tp'), pairs)  40.2 us
    all_to_all x3, starting transfers between devices, exchange(): lax.all_to_all(array, 'ctx', 0, 0, axis_index_groups=groups, tiled=True)  21.2 us
    ppermute x3, starting transfers between devices, to_sibling(): return lax.ppermute(array, 'ctx', [(i, i ^ 1) for i in range(ny * nx * nc)])  9.39 us
    pallas_call x1, Pallas kernels, on_device(): call(projection_kernel, [jax.ShapeDtypeStruct((2, slots + 16, width), BF1...  3.34 us
    pallas_call x1, Pallas kernels, on_device(): call(cotangent_kernel, jax.ShapeDtypeStruct((slots, width), BF16), [SMEM,...  3.29 us
    pallas_call x1, Pallas kernels, on_device(): call(backward_kernel, [jax.ShapeDtypeStruct((slots, width), BF16), jax.Sh...  2.87 us
    pallas_call x1, Pallas kernels, on_device(): call(forward_kernel, [jax.ShapeDtypeStruct((HD + 8 + slots, rows), F32),...  2.38 us
    ppermute x3, waiting for transfers between devices, to_sibling(): return lax.ppermute(array, 'ctx', [(i, i ^ 1) for i in range(ny * nx * nc)])  2.23 us
  transfers between devices with their start and end apart: 14, of which 4 were waited for; matrix products, arithmetic and copies ran while one was open for 1% of the time, Pallas kernels for 9%

profile of v9, /device:TPU:1, one launch (start us, length us, event | category | flops | bytes accessed | tf_op | source)
XLA Modules:
  0.0 99.6 jit_solution(13558361379679049890)
XLA Ops:
  2.8 1.2 %shard_map.136 = (bf16[128,128]{1,0:T(8,128)(2,1)S(1)}, bf16[32,128,128]{2,1,0:T(8,128)(2,1)}, f32[64,128]{1,0:T(8,128)S(1)}, f32[64,128]{1,0:T(8,128)S(1)}) custom-call(s32[1]{0:T(128)S(6)} %copy.15.count_ref, bf16[128,128]{1,0:T(8,128)(2,1)S(1)} %pad_maximum_fusion.1.pair_ref, f32[1,64]{1,0:T(1,128)S(1)} %convert_bitcast_fusion.position_ref, ...), custom_call_target="tpu_custom_call" | custom-call | tf_op jit(solution)/shard_map/pallas_call | solution.py:359
  4.0 10.5 %all-to-all-start = ((bf16[32,128,128]{2,1,0:T(8,128)(2,1)}), bf16[32,128,128]{2,1,0:T(8,128)(2,1)S(1)}, u32[]{:S(2)}, u32[]{:S(2)}) async-start(bf16[32,128,128]{2,1,0:T(8,128)(2,1)} %get-tuple-element.37), calls=%async_computation | async-start | bytes 2097152 | tf_op jit(solution)/shard_map/all_to_all | solution.py:335
  14.6 10.6 %collective-permute-start.1 = (bf16[1,64,512]{2,1,0:T(8,128)(2,1)}, bf16[1,64,512]{2,1,0:T(8,128)(2,1)S(1)}, u32[]{:S(2)}, u32[]{:S(2)}) collective-permute-start(bf16[1,64,512]{2,1,0:T(8,128)(2,1)} %bitcast.15), channel_id=1, source_target_pairs={{0,4},{1,5},{2,6},{3,7},{4,0},{5,1},{6,2},{7,3},{8,12},{9,13},{10,... | collective-permute-start | bytes 196616 | tf_op jit(solution)/shard_map/ppermute | solution.py:346
  25.2 2.1 %collective-permute-done.1 = bf16[1,64,512]{2,1,0:T(8,128)(2,1)S(1)} collective-permute-done((bf16[1,64,512]{2,1,0:T(8,128)(2,1)}, bf16[1,64,512]{2,1,0:T(8,128)(2,1)S(1)}, u32[]{:S(2)}, u32[]{:S(2)}) %collective-permute-start.1) | collective-permute-done | bytes 65568 | tf_op jit(solution)/shard_map/ppermute | solution.py:346
  28.2 7.7 %collective-permute-start.4 = (bf16[2,64,512]{2,1,0:T(8,128)(2,1)S(1)}, bf16[2,64,512]{2,1,0:T(8,128)(2,1)S(1)}, u32[]{:S(2)}, u32[]{:S(2)}) collective-permute-start(bf16[2,64,512]{2,1,0:T(8,128)(2,1)S(1)} %pad_maximum_fusion.pair_ref), channel_id=1, source_target_pairs={{0,2},{1,3},{2,4},{3,5},{4,6},{5,7},{6,0},{7,1},{8,14},{9,15},{10,... | collective-permute-start | bytes 393224 | tf_op jit(solution)/shard_map/ppermute | solution.py:346
  35.9 2.5 %collective-permute-start.3 = (bf16[2,64,512]{2,1,0:T(8,128)(2,1)S(1)}, bf16[2,64,512]{2,1,0:T(8,128)(2,1)S(1)}, u32[]{:S(2)}, u32[]{:S(2)}) collective-permute-start(bf16[2,64,512]{2,1,0:T(8,128)(2,1)S(1)} %pad_maximum_fusion.pair_ref), channel_id=1, source_target_pairs={{0,7},{1,0},{2,1},{3,2},{4,3},{5,4},{6,5},{7,6},{8,9},{9,10},{10,1... | collective-permute-start | bytes 393224 | tf_op jit(solution)/shard_map/ppermute | solution.py:346
  38.4 4.0 %collective-permute-start.2 = (bf16[2,64,512]{2,1,0:T(8,128)(2,1)S(1)}, bf16[2,64,512]{2,1,0:T(8,128)(2,1)S(1)}, u32[]{:S(2)}, u32[]{:S(2)}) collective-permute-start(bf16[2,64,512]{2,1,0:T(8,128)(2,1)S(1)} %pad_maximum_fusion.pair_ref), channel_id=1, source_target_pairs={{0,1},{1,2},{2,3},{3,4},{4,5},{5,6},{6,7},{7,0},{8,15},{9,8},{10,9... | collective-permute-start | bytes 393224 | tf_op jit(solution)/shard_map/ppermute | solution.py:346
  44.0 1.9 %collective-permute-start = (bf16[64,512]{1,0:T(8,128)(2,1)S(1)}, bf16[64,512]{1,0:T(8,128)(2,1)S(1)}, u32[]{:S(2)}, u32[]{:S(2)}) collective-permute-start(bf16[64,512]{1,0:T(8,128)(2,1)S(1)} %get-tuple-element.34.own_ref), channel_id=1, source_target_pairs={{0,8},{8,0},{16,24},{24,16},{32,40},{40,32},{48,56},{56,48},{64,72... | collective-permute-start | bytes 196616 | tf_op jit(solution)/shard_map/ppermute | solution.py:338
  46.0 3.3 %shard_map.138.grad_ref = bf16[64,512]{1,0:T(8,128)(2,1)S(1)} custom-call(s32[2]{0:T(128)S(1)} %pad_add_fusion.place_ref, bf16[512,4096]{1,0:T(8,128)(2,1)} %weight_ref.3, f32[64,128]{1,0:T(8,128)S(1)} %get-tuple-element.35.gate_ref, bf16[2,64,512]{2,1,0:T(8,128)(2,1)S(1)} %pad_maximum_fusion.pair_ref, ...), custom_call_target="tpu_custom_call" | custom-call | tf_op jit(solution)/shard_map/pallas_call | solution.py:392
  49.4 2.4 %shard_map.139 = (f32[200,512]{1,0:T(8,128)S(1)}, bf16[4,512,512]{2,1,0:T(8,128)(2,1)S(1)}) custom-call(s32[2]{0:T(128)S(1)} %pad_add_fusion.place_ref, s32[1,64]{1,0:T(1,128)S(1)} %bitcast.11, bf16[64,512]{1,0:T(8,128)(2,1)S(1)} %get-tuple-element.34.own_ref, bf16[64,512]{1,0:T(8,128)(2,1)S(1)} %collective-permute-done.sibling_ref, ...), custom_call_target="tpu_custom_call" | custom-call | tf_op jit(solution)/shard_map/pallas_call | solution.py:401
  51.8 3.5 %collective-permute-start.5 = (f32[200,512]{1,0:T(8,128)S(1)}, f32[200,512]{1,0:T(8,128)S(1)}, u32[]{:S(2)}, u32[]{:S(2)}) collective-permute-start(f32[200,512]{1,0:T(8,128)S(1)} %get-tuple-element.38.own_part), channel_id=1, source_target_pairs={{0,8},{8,0},{16,24},{24,16},{32,40},{40,32},{48,56},{56,48},{64,72... | collective-permute-start | bytes 1228808 | tf_op jit(solution)/shard_map/ppermute | solution.py:338
  55.2 1.4 %collective-permute-done.5.sibling_part = f32[200,512]{1,0:T(8,128)S(1)} collective-permute-done((f32[200,512]{1,0:T(8,128)S(1)}, f32[200,512]{1,0:T(8,128)S(1)}, u32[]{:S(2)}, u32[]{:S(2)}) %collective-permute-start.5) | collective-permute-done | bytes 409632 | tf_op jit(solution)/shard_map/ppermute | solution.py:338
  56.6 2.9 %shard_map.140 = (bf16[64,512]{1,0:T(8,128)(2,1)S(1)}, f32[8,256]{1,0:T(8,128)S(1)}, f32[256,128]{1,0:T(8,128)S(1)}, bf16[256,128]{1,0:T(8,128)(2,1)S(1)}, bf16[32,128,128]{2,1,0:T(8,128)(2,1)}) custom-call(f32[200,512]{1,0:T(8,128)S(1)} %get-tuple-element.38.own_part, f32[200,512]{1,0:T(8,128)S(1)} %collective-permute-done.5.sibling_part, ...), custom_call_target="tpu_custom_call" | custom-call | tf_op jit(solution)/shard_map/pallas_call | solution.py:411
  59.5 4.3 %all-to-all-start.1 = ((bf16[4,8,128,128]{3,2,1,0:T(8,128)(2,1)}), bf16[4,8,128,128]{3,2,1,0:T(8,128)(2,1)S(1)}, u32[]{:S(2)}, u32[]{:S(2)}) async-start(bf16[4,8,128,128]{3,2,1,0:T(8,128)(2,1)} %bitcast.7), calls=%async_computation.1 | async-start | bytes 2097152 | tf_op jit(solution)/shard_map/all_to_all | solution.py:335
  63.8 3.3 %shard_map.141 = (bf16[2,80,512]{2,1,0:T(8,128)(2,1)S(1)}, bf16[2,80,512]{2,1,0:T(8,128)(2,1)S(1)}, bf16[2,80,512]{2,1,0:T(8,128)(2,1)S(1)}, bf16[2,80,512]{2,1,0:T(8,128)(2,1)S(1)}) custom-call(s32[2]{0:T(128)S(1)} %pad_add_fusion.place_ref, bf16[512,4096]{1,0:T(8,128)(2,1)} %weight_ref.3, bf16[64,512]{1,0:T(8,128)(2,1)S(1)} %get-tuple-element.40.att_ref, ...), custom_call_target="tpu_custom_call" | custom-call | tf_op jit(solution)/shard_map/pallas_call | solution.py:428
  67.1 1.9 %collective-permute-start.6 = (bf16[2,80,512]{2,1,0:T(8,128)(2,1)S(1)}, bf16[2,80,512]{2,1,0:T(8,128)(2,1)S(1)}, u32[]{:S(2)}, u32[]{:S(2)}) collective-permute-start(bf16[2,80,512]{2,1,0:T(8,128)(2,1)S(1)} %get-tuple-element.43), channel_id=1, source_target_pairs={{0,7},{1,0},{2,1},{3,2},{4,3},{5,4},{6,5},{7,6},{8,9},{9,10},{10,1... | collective-permute-start | bytes 491528 | tf_op jit(solution)/shard_map/ppermute | solution.py:346
  69.1 4.6 %collective-permute-start.7 = (bf16[2,80,512]{2,1,0:T(8,128)(2,1)S(1)}, bf16[2,80,512]{2,1,0:T(8,128)(2,1)S(1)}, u32[]{:S(2)}, u32[]{:S(2)}) collective-permute-start(bf16[2,80,512]{2,1,0:T(8,128)(2,1)S(1)} %get-tuple-element.44), channel_id=1, source_target_pairs={{0,1},{1,2},{2,3},{3,4},{4,5},{5,6},{6,7},{7,0},{8,15},{9,8},{10,9... | collective-permute-start | bytes 491528 | tf_op jit(solution)/shard_map/ppermute | solution.py:346
  73.6 2.5 %collective-permute-start.8 = (bf16[2,80,512]{2,1,0:T(8,128)(2,1)S(1)}, bf16[2,80,512]{2,1,0:T(8,128)(2,1)S(1)}, u32[]{:S(2)}, u32[]{:S(2)}) collective-permute-start(bf16[2,80,512]{2,1,0:T(8,128)(2,1)S(1)} %get-tuple-element.45), channel_id=1, source_target_pairs={{0,6},{1,7},{2,0},{3,1},{4,2},{5,3},{6,4},{7,5},{8,10},{9,11},{10,... | collective-permute-start | bytes 491528 | tf_op jit(solution)/shard_map/ppermute | solution.py:346
  76.1 2.2 %all-to-all-done.1.stack_ref = bf16[4,8,128,128]{3,2,1,0:T(8,128)(2,1)S(1)} async-done(((bf16[4,8,128,128]{3,2,1,0:T(8,128)(2,1)}), bf16[4,8,128,128]{3,2,1,0:T(8,128)(2,1)S(1)}, u32[]{:S(2)}, u32[]{:S(2)}) %all-to-all-start.1) | async-done | bytes 1048608 | tf_op jit(solution)/shard_map/all_to_all | solution.py:335
  79.1 6.4 %all-to-all-start.2 = ((bf16[8,128,128]{2,1,0:T(8,128)(2,1)}), bf16[8,128,128]{2,1,0:T(8,128)(2,1)S(1)}, u32[]{:S(2)}, u32[]{:S(2)}) async-start(bf16[8,128,128]{2,1,0:T(8,128)(2,1)} %shard_map.142), calls=%async_computation.2 | async-start | bytes 524288 | tf_op jit(solution)/shard_map/all_to_all | solution.py:335
  85.6 6.4 %collective-permute-start.9 = (bf16[1,80,512]{2,1,0:T(8,128)(2,1)S(1)}, bf16[1,80,512]{2,1,0:T(8,128)(2,1)S(1)}, u32[]{:S(2)}, u32[]{:S(2)}) collective-permute-start(bf16[1,80,512]{2,1,0:T(8,128)(2,1)S(1)} %get-tuple-element.47), channel_id=1, source_target_pairs={{0,4},{1,5},{2,6},{3,7},{4,0},{5,1},{6,2},{7,3},{8,12},{9,13},{10,... | collective-permute-start | bytes 245768 | tf_op jit(solution)/shard_map/ppermute | solution.py:346
  92.1 4.0 %collective-permute-start.10 = (bf16[256,128]{1,0:T(8,128)(2,1)S(1)}, bf16[256,128]{1,0:T(8,128)(2,1)S(1)}, u32[]{:S(2)}, u32[]{:S(2)}) collective-permute-start(bf16[256,128]{1,0:T(8,128)(2,1)S(1)} %get-tuple-element.53), channel_id=1, source_target_pairs={{0,8},{8,0},{16,24},{24,16},{32,40},{40,32},{48,56},{56,48},{64,72... | collective-permute-start | bytes 196616 | tf_op jit(solution)/shard_map/ppermute | solution.py:338
  96.1 0.9 collective-permute-done.10.arrived_ref
  98.4 1.2 %shard_map.144 = (bf16[64,512]{1,0:T(8,128)(2,1)}, bf16[512,512]{1,0:T(8,128)(2,1)}, f32[1,64]{1,0:T(1,128)}) custom-call(s32[1]{0:T(128)S(6)} %copy.15.count_ref, bf16[1,80,512]{2,1,0:T(8,128)(2,1)S(1)} %get-tuple-element.59.own_ref, bf16[1,80,512]{2,1,0:T(8,128)(2,1)S(1)} %collective-permute-done.9.landed_ref, f32[1,64]{1,0:T(1,128)S(1)} %bitcast.14, ...), custom_call_target="tpu_custom_call" | custom-call | tf_op jit(solution)/shard_map/pallas_call | solution.py:450
  (32 shorter events, 6.4 us)
Async XLA Ops:
  0.6 48.7 %copy-start.2 = (s32[64]{0:T(128)S(1)}, s32[64]{0:T(128)}, u32[]{:S(2)}) copy-start(s32[64]{0:T(128)} %param.14) | copy-start | bytes 772
  4.0 45.3 %all-to-all-start = ((bf16[32,128,128]{2,1,0:T(8,128)(2,1)}), bf16[32,128,128]{2,1,0:T(8,128)(2,1)S(1)}, u32[]{:S(2)}, u32[]{:S(2)}) async-start(bf16[32,128,128]{2,1,0:T(8,128)(2,1)} %get-tuple-element.37), calls=%async_computation | async-start | bytes 2097152 | tf_op jit(solution)/shard_map/all_to_all | solution.py:335
  14.6 12.8 %collective-permute-start.1 = (bf16[1,64,512]{2,1,0:T(8,128)(2,1)}, bf16[1,64,512]{2,1,0:T(8,128)(2,1)S(1)}, u32[]{:S(2)}, u32[]{:S(2)}) collective-permute-start(bf16[1,64,512]{2,1,0:T(8,128)(2,1)} %bitcast.15), channel_id=1, source_target_pairs={{0,4},{1,5},{2,6},{3,7},{4,0},{5,1},{6,2},{7,3},{8,12},{9,13},{10,... | collective-permute-start | bytes 196616 | tf_op jit(solution)/shard_map/ppermute | solution.py:346
  28.2 17.8 %collective-permute-start.4 = (bf16[2,64,512]{2,1,0:T(8,128)(2,1)S(1)}, bf16[2,64,512]{2,1,0:T(8,128)(2,1)S(1)}, u32[]{:S(2)}, u32[]{:S(2)}) collective-permute-start(bf16[2,64,512]{2,1,0:T(8,128)(2,1)S(1)} %pad_maximum_fusion.pair_ref), channel_id=1, source_target_pairs={{0,2},{1,3},{2,4},{3,5},{4,6},{5,7},{6,0},{7,1},{8,14},{9,15},{10,... | collective-permute-start | bytes 393224 | tf_op jit(solution)/shard_map/ppermute | solution.py:346
  35.9 10.1 %collective-permute-start.3 = (bf16[2,64,512]{2,1,0:T(8,128)(2,1)S(1)}, bf16[2,64,512]{2,1,0:T(8,128)(2,1)S(1)}, u32[]{:S(2)}, u32[]{:S(2)}) collective-permute-start(bf16[2,64,512]{2,1,0:T(8,128)(2,1)S(1)} %pad_maximum_fusion.pair_ref), channel_id=1, source_target_pairs={{0,7},{1,0},{2,1},{3,2},{4,3},{5,4},{6,5},{7,6},{8,9},{9,10},{10,1... | collective-permute-start | bytes 393224 | tf_op jit(solution)/shard_map/ppermute | solution.py:346
  38.4 7.6 %collective-permute-start.2 = (bf16[2,64,512]{2,1,0:T(8,128)(2,1)S(1)}, bf16[2,64,512]{2,1,0:T(8,128)(2,1)S(1)}, u32[]{:S(2)}, u32[]{:S(2)}) collective-permute-start(bf16[2,64,512]{2,1,0:T(8,128)(2,1)S(1)} %pad_maximum_fusion.pair_ref), channel_id=1, source_target_pairs={{0,1},{1,2},{2,3},{3,4},{4,5},{5,6},{6,7},{7,0},{8,15},{9,8},{10,9... | collective-permute-start | bytes 393224 | tf_op jit(solution)/shard_map/ppermute | solution.py:346
  42.4 0.8 copy-start.1
  43.2 0.7 copy-start.3
  44.0 5.3 %collective-permute-start = (bf16[64,512]{1,0:T(8,128)(2,1)S(1)}, bf16[64,512]{1,0:T(8,128)(2,1)S(1)}, u32[]{:S(2)}, u32[]{:S(2)}) collective-permute-start(bf16[64,512]{1,0:T(8,128)(2,1)S(1)} %get-tuple-element.34.own_ref), channel_id=1, source_target_pairs={{0,8},{8,0},{16,24},{24,16},{32,40},{40,32},{48,56},{56,48},{64,72... | collective-permute-start | bytes 196616 | tf_op jit(solution)/shard_map/ppermute | solution.py:338
  51.8 4.8 %collective-permute-start.5 = (f32[200,512]{1,0:T(8,128)S(1)}, f32[200,512]{1,0:T(8,128)S(1)}, u32[]{:S(2)}, u32[]{:S(2)}) collective-permute-start(f32[200,512]{1,0:T(8,128)S(1)} %get-tuple-element.38.own_part), channel_id=1, source_target_pairs={{0,8},{8,0},{16,24},{24,16},{32,40},{40,32},{48,56},{56,48},{64,72... | collective-permute-start | bytes 1228808 | tf_op jit(solution)/shard_map/ppermute | solution.py:338
  59.5 18.8 %all-to-all-start.1 = ((bf16[4,8,128,128]{3,2,1,0:T(8,128)(2,1)}), bf16[4,8,128,128]{3,2,1,0:T(8,128)(2,1)S(1)}, u32[]{:S(2)}, u32[]{:S(2)}) async-start(bf16[4,8,128,128]{3,2,1,0:T(8,128)(2,1)} %bitcast.7), calls=%async_computation.1 | async-start | bytes 2097152 | tf_op jit(solution)/shard_map/all_to_all | solution.py:335
  63.8 34.6 %copy-start = (bf16[512,512]{1,0:T(8,128)(2,1)S(1)}, bf16[512,512]{1,0:T(8,128)(2,1)}, u32[]{:S(2)}) copy-start(bf16[512,512]{1,0:T(8,128)(2,1)} %hidden_ref.1) | copy-start | bytes 1572868
  63.8 34.6 %copy-start.4 = (f32[64]{0:T(128)S(1)}, f32[64]{0:T(128)}, u32[]{:S(2)}) copy-start(f32[64]{0:T(128)} %param.13) | copy-start | bytes 772
  67.1 18.4 %collective-permute-start.6 = (bf16[2,80,512]{2,1,0:T(8,128)(2,1)S(1)}, bf16[2,80,512]{2,1,0:T(8,128)(2,1)S(1)}, u32[]{:S(2)}, u32[]{:S(2)}) collective-permute-start(bf16[2,80,512]{2,1,0:T(8,128)(2,1)S(1)} %get-tuple-element.43), channel_id=1, source_target_pairs={{0,7},{1,0},{2,1},{3,2},{4,3},{5,4},{6,5},{7,6},{8,9},{9,10},{10,1... | collective-permute-start | bytes 491528 | tf_op jit(solution)/shard_map/ppermute | solution.py:346
  69.1 16.4 %collective-permute-start.7 = (bf16[2,80,512]{2,1,0:T(8,128)(2,1)S(1)}, bf16[2,80,512]{2,1,0:T(8,128)(2,1)S(1)}, u32[]{:S(2)}, u32[]{:S(2)}) collective-permute-start(bf16[2,80,512]{2,1,0:T(8,128)(2,1)S(1)} %get-tuple-element.44), channel_id=1, source_target_pairs={{0,1},{1,2},{2,3},{3,4},{4,5},{5,6},{6,7},{7,0},{8,15},{9,8},{10,9... | collective-permute-start | bytes 491528 | tf_op jit(solution)/shard_map/ppermute | solution.py:346
  73.6 11.9 %collective-permute-start.8 = (bf16[2,80,512]{2,1,0:T(8,128)(2,1)S(1)}, bf16[2,80,512]{2,1,0:T(8,128)(2,1)S(1)}, u32[]{:S(2)}, u32[]{:S(2)}) collective-permute-start(bf16[2,80,512]{2,1,0:T(8,128)(2,1)S(1)} %get-tuple-element.45), channel_id=1, source_target_pairs={{0,6},{1,7},{2,0},{3,1},{4,2},{5,3},{6,4},{7,5},{8,10},{9,11},{10,... | collective-permute-start | bytes 491528 | tf_op jit(solution)/shard_map/ppermute | solution.py:346
  79.1 18.6 %all-to-all-start.2 = ((bf16[8,128,128]{2,1,0:T(8,128)(2,1)}), bf16[8,128,128]{2,1,0:T(8,128)(2,1)S(1)}, u32[]{:S(2)}, u32[]{:S(2)}) async-start(bf16[8,128,128]{2,1,0:T(8,128)(2,1)} %shard_map.142), calls=%async_computation.2 | async-start | bytes 524288 | tf_op jit(solution)/shard_map/all_to_all | solution.py:335
  85.6 12.8 %collective-permute-start.9 = (bf16[1,80,512]{2,1,0:T(8,128)(2,1)S(1)}, bf16[1,80,512]{2,1,0:T(8,128)(2,1)S(1)}, u32[]{:S(2)}, u32[]{:S(2)}) collective-permute-start(bf16[1,80,512]{2,1,0:T(8,128)(2,1)S(1)} %get-tuple-element.47), channel_id=1, source_target_pairs={{0,4},{1,5},{2,6},{3,7},{4,0},{5,1},{6,2},{7,3},{8,12},{9,13},{10,... | collective-permute-start | bytes 245768 | tf_op jit(solution)/shard_map/ppermute | solution.py:346
  92.1 4.9 %collective-permute-start.10 = (bf16[256,128]{1,0:T(8,128)(2,1)S(1)}, bf16[256,128]{1,0:T(8,128)(2,1)S(1)}, u32[]{:S(2)}, u32[]{:S(2)}) collective-permute-start(bf16[256,128]{1,0:T(8,128)(2,1)S(1)} %get-tuple-element.53), channel_id=1, source_target_pairs={{0,8},{8,0},{16,24},{24,16},{32,40},{40,32},{48,56},{56,48},{64,72... | collective-permute-start | bytes 196616 | tf_op jit(solution)/shard_map/ppermute | solution.py:338
